TPU v7x, 32 devices: a whole 2x2x4 slice. The times are simulated.
32 devices in a mesh: dp: 4 (over x, core), fsdp: 8 (over z, y).
Axes of the slice: x: 2, y: 2, z: 4, core: 2. Of those that a mesh axis runs over, the one named last changes fastest.
Arguments:
- tokens: bfloat16 [2, 16384, 768], P(None, ('dp', 'fsdp')), may hold values from -6 to 6
- lengths: int32 [2, 32], P(None, ('dp', 'fsdp')), may hold values from 256 to 512, as said below
- cotangent: bfloat16 [2, 16384, 768], P(None, ('dp', 'fsdp')), may hold values from -6 to 6
- mixer_in: bfloat16 [768, 3072], P(('dp', 'fsdp')), may hold values from -0.21875 to 0.21875
- w_eta: bfloat16 [768, 12], P(('dp', 'fsdp')), may hold values from -0.21875 to 0.21875
- eta_bias: bfloat16 [12], replicated, may hold values from -1 to 1
- w_out: bfloat16 [768, 768], P(('dp', 'fsdp')), may hold values from -0.4375 to 0.4375
- inner_w: bfloat16 [768, 64], P(('dp', 'fsdp')), may hold values from -0.75 to 0.75
- inner_b: bfloat16 [768], P(('dp', 'fsdp')), may hold values from -3 to 3
- ttt_gain: bfloat16 [768], P(('dp', 'fsdp')), may hold values from 0.5 to 1.5
- ttt_shift: bfloat16 [768], P(('dp', 'fsdp')), may hold values from -2 to 2
- norm_one: bfloat16 [768], P(('dp', 'fsdp')), may hold values from 0.5 to 1.5
- post_gain: bfloat16 [768], P(('dp', 'fsdp')), may hold values from 0.5 to 1.5
- post_shift: bfloat16 [768], P(('dp', 'fsdp')), may hold values from -2 to 2
- w_gate_up: bfloat16 [768, 4096], P(('dp', 'fsdp')), may hold values from -0.21875 to 0.21875
- w_down: bfloat16 [2048, 768], P(('dp', 'fsdp')), may hold values from -0.25 to 0.25
- norm_two: bfloat16 [768], P(('dp', 'fsdp')), may hold values from 0.5 to 1.5
Outputs:
- block_out: bfloat16 [2, 16384, 768], P(None, ('dp', 'fsdp'))
- grad_tokens: bfloat16 [2, 16384, 768], P(None, ('dp', 'fsdp'))
- grad_mixer_in: float32 [768, 3072], P(('dp', 'fsdp'))
- grad_w_eta: float32 [768, 12], P(('dp', 'fsdp'))
- grad_eta_bias: float32 [12], replicated
- grad_w_out: float32 [768, 768], P(('dp', 'fsdp'))
- grad_inner_w: float32 [768, 64], P(('dp', 'fsdp'))
- grad_inner_b: float32 [768], P(('dp', 'fsdp'))
- grad_ttt_gain: float32 [768], P(('dp', 'fsdp'))
- grad_ttt_shift: float32 [768], P(('dp', 'fsdp'))
- grad_norm_one: float32 [768], P(('dp', 'fsdp'))
- grad_post_gain: float32 [768], P(('dp', 'fsdp'))
- grad_post_shift: float32 [768], P(('dp', 'fsdp'))
- grad_w_gate_up: float32 [768, 4096], P(('dp', 'fsdp'))
- grad_w_down: float32 [2048, 768], P(('dp', 'fsdp'))
- grad_norm_two: float32 [768], P(('dp', 'fsdp'))
Inputs may be any that keep to these rules, and one draw needn't show every extreme that they name: `lengths`: every entry is a multiple of 16; some entry equals 512.
All inputs are finite; a program needn't handle non-finite values.
Results may differ from a plain program's by a relative error of at most 0.0085.
The roundings to bfloat16 on the way count: a program that leaves them out, or rounds other values in their place, can miss the bound.
Values may be sent and summed in bfloat16 or wider, within the bound.
No kernel may reach another device: no remote copies, remote signals or barrier semaphores. Data moves between devices by JAX's collectives and lax.ppermute only.
A program may use at most 256 MiB of HBM per device.

v0:
```python
import jax
import jax.numpy as jnp
from jax import lax
from jax.experimental import pallas as pl
from jax.experimental.pallas import tpu as pltpu
from jax.sharding import PartitionSpec as P
import numpy as np

MINI = 16
HEAD = 64
PAIR = 2 * HEAD
epsilon = 1e-06
low = jnp.bfloat16
full = jnp.float32


def dot_nn(former, latter):
    return lax.dot_general(former, latter, (((1,), (0,)), ((), ())), preferred_element_type=full)


def dot_nt(former, latter):
    return lax.dot_general(former, latter, (((1,), (1,)), ((), ())), preferred_element_type=full)


def tile_of(rows, at):
    return rows[:, PAIR * at : PAIR * (at + 1)]


def key_row(group, side, tile):
    return HEAD * group + 32 * side + MINI * tile


def query_row(group, side, tile):
    return key_row(1 - group, side, tile)


def expand(rows, sides):
    zero = jnp.zeros((MINI, PAIR), rows.dtype)
    blocks = []
    for side in range(2):
        for at in range(2):
            kept = tile_of(rows, at) * sides[side]
            blocks.append(jnp.concatenate([kept if other == at else zero for other in range(2)], axis=1))
    return jnp.concatenate(blocks, axis=0)


def expand_both(queries, keys, sides):
    width = 2 * PAIR
    blocks = [(expand(keys[:, width * group : width * (group + 1)], sides), expand(queries[:, width * group : width * (group + 1)], sides))
              for group in range(2)]
    return blocks, (jnp.concatenate(blocks[0], axis=0), jnp.concatenate(blocks[1][::-1], axis=0))


def to_feature(rows, first_side, groups):
    tiles = [tile_of(rows, 2 * group + at) for group in groups for _ in range(2) for at in range(2)]
    stacked = jnp.concatenate(tiles, axis=0).T
    return jnp.where(first_side, stacked[:HEAD], stacked[HEAD:])


def to_rows(columns, left, place):
    turned = jnp.concatenate([columns, columns], axis=0).T
    pick = lambda group, side, at: turned[place(group, side, at) : place(group, side, at) + MINI]
    return jnp.concatenate([jnp.where(left, pick(group, 0, at), pick(group, 1, at)) for group in range(2) for at in range(2)], axis=1)


def exchange(values):
    half = [values[:, HEAD * at : HEAD * (at + 1)] for at in range(values.shape[1] // HEAD)]
    return jnp.concatenate([half[at ^ 1] for at in range(len(half))], axis=1)


def mean_rows(values):
    return jnp.sum(values, axis=0, keepdims=True) * (1.0 / values.shape[0])


def both_sequences(ref, rows, base, width):
    return jnp.concatenate([ref[0, rows, base : base + width], ref[1, rows, base : base + width]], axis=1)


def store_sequences(ref, rows, base, width, pieces, kind):
    whole = jnp.concatenate(pieces, axis=1)
    ref[0, rows, base : base + width] = whole[:, :width].astype(kind)
    ref[1, rows, base : base + width] = whole[:, width:].astype(kind)


def read_constants(low_ref, full_ref):
    sides = [low_ref[0:MINI], low_ref[MINI : 2 * MINI]]
    same, crossed = low_ref[32:160], low_ref[160:288]
    return sides, same, crossed, full_ref[0:MINI], full_ref[16:144], full_ref[144:272]


def lane_masks(rows=HEAD, width=3 * PAIR):
    lane = lax.broadcasted_iota(jnp.int32, (rows, width), 1)
    return lane % PAIR < HEAD, lane % HEAD < 32


PARTS = range(3)


def thin(part):
    return slice(PAIR * part, PAIR * (part + 1))


def wide(part):
    return slice(4 * PAIR * part, 4 * PAIR * (part + 1))


def lanes(pieces):
    return jnp.concatenate(pieces, axis=1)


def ttt_forward_kernel(steps, q_ref, k_ref, v_ref, rate_ref, w0_ref, b0_ref, gain_ref, shift_ref, low_ref, full_ref,
                       out_ref, w_ref, xh_ref, h_ref, grs_ref, xb_ref, stat_ref, score_ref, w_run, b_run, gain_query, shift_query):
    width = 768

    @pl.when(pl.program_id(0) == 0)
    def _():
        w_run[...] = w0_ref[...]
        b_run[...] = b0_ref[...]
        gain_query[...] = exchange(gain_ref[...])
        shift_query[...] = exchange(shift_ref[...])

    sides, same, crossed, tri, _, _ = read_constants(low_ref, full_ref)
    left, first_side = lane_masks()
    left_one, first_one = left[:, :PAIR], first_side[:, :PAIR]
    tri = lanes([tri] * 3)

    def begin(at):
        rows = slice(at * MINI, (at + 1) * MINI)
        queries = both_sequences(q_ref, rows, 0, width)
        keys = both_sequences(k_ref, rows, 0, width)
        targets = both_sequences(v_ref, rows, 0, width) - keys
        query_low, key_low = queries.astype(low), keys.astype(low)
        expanded = [expand_both(query_low[:, wide(part)], key_low[:, wide(part)], sides) for part in PARTS]
        target = lanes([to_feature(targets[:, wide(part)], first_one, (0, 1)) for part in PARTS])
        return rows, queries, query_low, expanded, target

    def multiply(at, started, weights):
        _, _, query_low, expanded, _ = started
        products = []
        for part in PARTS:
            weight_low = weights[part].astype(low)
            w_ref[at, :, wide(part)] = weight_low
            for group in range(2):
                here = slice(2 * PAIR * group, 2 * PAIR * (group + 1))
                rows = jnp.concatenate([weight_low[:, here], query_low[:, wide(part)][:, here]], axis=0)
                products.append(dot_nt(rows, expanded[part][1][group]))
        return lanes(products[::2]), lanes(products[1::2])

    def finish(at, started, kept):
        rows, queries = started[:2]
        inner_grad, mixing, updated = kept
        inner_grad_low = inner_grad.astype(low)
        moved = []
        for part in PARTS:
            mixing_block = jnp.concatenate([mixing[:, thin(part)]] * 8, axis=0) * crossed
            moved.append(dot_nt(inner_grad_low[:, thin(part)], mixing_block))
        updated = updated - lanes(moved)
        updated = updated - mean_rows(updated)
        updated_inverse = lax.rsqrt(mean_rows(updated * updated) + epsilon)
        updated = updated * updated_inverse
        xb_ref[at] = updated
        stat_ref[at, 3:4] = updated_inverse
        updated = updated * gain_query[...] + shift_query[...]
        result = queries + lanes([to_rows(updated[:, thin(part)], left_one[:MINI], query_row) for part in PARTS])
        out_ref[0, rows, :] = result[:, :width]
        out_ref[1, rows, :] = result[:, width:]

    weights = [w_run[:, wide(part)] for part in PARTS]
    offset = b_run[...]
    started = begin(0)
    pending = None
    for at in range(steps):
        first, second = multiply(at, started, weights)
        if pending is not None:
            finish(*pending)
        gains, shifts = gain_ref[...], shift_ref[...]
        rate = rate_ref[at]
        _, _, _, expanded, target = started
        hidden = jnp.where(left, first[:HEAD], second[:HEAD]) + offset
        scores = jnp.where(left[:MINI], first[HEAD:], second[HEAD:]) + 1.0
        updated = jnp.where(left, second[:HEAD], first[:HEAD]) + exchange(offset)
        centred = hidden - mean_rows(hidden)
        inverse = lax.rsqrt(mean_rows(centred * centred) + epsilon)
        normed = centred * inverse
        held = gains * normed + (shifts - target)
        residual = held * gains
        residual_mean = mean_rows(residual)
        cross = mean_rows(residual * normed)
        inner_grad = (residual - residual_mean - normed * cross) * inverse
        scaled = inner_grad * (rate * (1.0 / MINI))
        scaled_low = scaled.astype(low)
        scaled_other = exchange(scaled).astype(low)
        xh_ref[at] = normed
        h_ref[at] = held
        grs_ref[at] = scaled
        stat_ref[at, 0:1] = inverse
        stat_ref[at, 1:2] = residual_mean
        stat_ref[at, 2:3] = cross
        score_ref[at] = scores
        changed = []
        for part in PARTS:
            blocks = expanded[part][0]
            change = [dot_nn(scaled_low[:, thin(part)][:, :HEAD], blocks[0][0]),
                      dot_nn(scaled_other[:, thin(part)][:, :HEAD], blocks[1][0])]
            changed.append(weights[part] - lanes(change))
        weights = changed
        offset = offset - lanes([dot_nn(scaled_low[:, thin(part)], same) for part in PARTS])
        pending = (at, started, (inner_grad, (tri * rate * scores).astype(low), updated))
        if at + 1 < steps:
            started = begin(at + 1)
    finish(*pending)
    for part in PARTS:
        w_run[:, wide(part)] = weights[part]
    b_run[...] = offset


def ttt_backward_kernel(steps, q_ref, k_ref, dout_ref, rate_ref, w_ref, xh_ref, h_ref, grs_ref, xb_ref, stat_ref, score_ref,
                        gain_ref, low_ref, full_ref, *refs):
    states, refs = refs[:6], refs[6:]
    grad_ref, rdr_ref, dw_ref, db_ref, dgain_ref, dshift_ref, dgain_query_ref, dshift_query_ref, gain_query = refs[-9:]
    width = 768

    @pl.when(pl.program_id(0) == 0)
    def _():
        for state, ref in zip(states, (dw_ref, db_ref, dgain_ref, dshift_ref, dgain_query_ref, dshift_query_ref)):
            ref[...] = state[...]
        gain_query[...] = exchange(gain_ref[...])

    sides, same, crossed, tri, scale, scale_turned = read_constants(low_ref, full_ref)
    left, first_side = lane_masks()
    left_one, first_one = left[:, :PAIR], first_side[:, :PAIR]
    left_rows = left_one[:MINI]
    left_square = lax.broadcasted_iota(jnp.int32, (PAIR, PAIR), 1) < HEAD
    zero = jnp.zeros((MINI, PAIR), full)
    tri = lanes([tri] * 3)

    def begin(at):
        rows = slice(at * MINI, (at + 1) * MINI)
        query_low = both_sequences(q_ref, rows, 0, width).astype(low)
        key_low = both_sequences(k_ref, rows, 0, width).astype(low)
        douts = both_sequences(dout_ref, rows, 0, width)
        expanded = [expand_both(query_low[:, wide(part)], key_low[:, wide(part)], sides) for part in PARTS]
        mixing = (tri * rate_ref[at] * score_ref[at]).astype(low)
        dout = lanes([to_feature(douts[:, wide(part)], first_one, (1, 0)) for part in PARTS])
        updated = xb_ref[at]
        dupdated = dout * gain_query[...]
        dupdated = stat_ref[at, 3:4] * (dupdated - mean_rows(dupdated) - updated * mean_rows(dupdated * updated))
        dgain_query_ref[...] += dout * updated
        dshift_query_ref[...] += dout
        dupdated_low = dupdated.astype(low)
        mixed = []
        for part in PARTS:
            mixing_block = jnp.concatenate([mixing[:, thin(part)]] * 8, axis=0) * crossed
            mixed.append(dot_nn(dupdated_low[:, thin(part)], mixing_block))
        return rows, douts, expanded, dupdated, dupdated_low, lanes(mixed)

    def finish(at, started, kept):
        rows, douts, expanded, dupdated, dupdated_low, _ = started
        dhidden, dtarget, dweights_low, rate_part = kept
        scaled = -grs_ref[at]
        scaled_low = scaled.astype(low)
        scores = score_ref[at]
        none = jnp.zeros((HEAD, PAIR), low)
        turned_low, turned_query, query_rows, dmixes, dmixes_turned = [], [], [], [], []
        for part in PARTS:
            turned_low.append(jnp.concatenate([dhidden[:, thin(part)], scaled[:, thin(part)]], axis=0).T.astype(low))
            turned_query.append(jnp.concatenate([dupdated[:, thin(part)], dtarget[:, thin(part)]], axis=0).T)
            query_rows.append(jnp.where(left_square, turned_query[part], 0.0).astype(low))
        for part in PARTS:
            dmix = dot_nn(query_rows[part][:, :HEAD], scaled_low[:, thin(part)]) * scale
            dmix_turned = dot_nn(turned_low[part], jnp.concatenate([none, dupdated_low[:, thin(part)]], axis=0)) * scale_turned
            dmixes.append(sum(dmix[MINI * row : MINI * (row + 1)] for row in range(8)))
            dmixes_turned.append(sum(dmix_turned[MINI * row : MINI * (row + 1)] for row in range(8)))
        rdr_ref[at] = rate_part + jnp.sum(lanes(dmixes) * scores, axis=0, keepdims=True)
        query_grads, key_grads, value_grads = [], [], []
        for part in PARTS:
            weight_low = w_ref[at, :, wide(part)]
            for group in range(2):
                keep_key, keep_query = (left_rows, ~left_rows) if group == 0 else (~left_rows, left_rows)
                key_side = jnp.where(keep_query, dmixes_turned[part], zero).astype(low)
                query_side = jnp.where(keep_key, dmixes[part], zero).astype(low)
                extra = jnp.concatenate([key_side, key_side, query_side, query_side], axis=0)
                for at_tile in range(2):
                    tile = 2 * group + at_tile
                    place = [key_row(group, side, at_tile) for side in range(2)]
                    place_query = [query_row(group, side, at_tile) for side in range(2)]
                    held_rows = jnp.concatenate(
                        [turned_low[part][row : row + MINI] for row in place]
                        + [query_rows[part][row : row + MINI] for row in place_query],
                        axis=0,
                    )
                    product = dot_nn(
                        jnp.concatenate([held_rows, extra], axis=1),
                        jnp.concatenate(
                            [tile_of(weight_low, tile), tile_of(dweights_low[part], tile), tile_of(expanded[part][1][group], at_tile)],
                            axis=0,
                        ),
                    )
                    dvalue = jnp.where(
                        left_rows,
                        exchange(turned_query[part][place[0] : place[0] + MINI]),
                        turned_query[part][place[1] : place[1] + MINI],
                    )
                    key_grads.append(dvalue + jnp.where(left_rows, product[:MINI], product[MINI : 2 * MINI]))
                    query_grads.append(
                        tile_of(douts[:, wide(part)], tile) + jnp.where(left_rows, product[2 * MINI : 3 * MINI], product[3 * MINI :])
                    )
                    value_grads.append(-dvalue)
        store_sequences(grad_ref, rows, 0, width, query_grads, low)
        store_sequences(grad_ref, rows, width, width, key_grads, low)
        store_sequences(grad_ref, rows, 2 * width, width, value_grads, low)

    dweights = [dw_ref[:, wide(part)] for part in PARTS]
    doffset = db_ref[...]
    started = begin(steps - 1)
    pending = None
    for at in reversed(range(steps)):
        _, _, expanded, dupdated, _, mixed = started
        dweights_low = [dweight.astype(low) for dweight in dweights]
        key_dw = []
        for part in PARTS:
            blocks = expanded[part][0]
            key_dw.append(dot_nt(dweights_low[part][:, : 2 * PAIR], blocks[0][0]))
            key_dw.append(dot_nt(dweights_low[part][:, 2 * PAIR :], blocks[1][0]))
        key_dw = lanes(key_dw) + doffset
        if pending is not None:
            finish(*pending)
        upcoming = begin(at - 1) if at > 0 else None
        gains = gain_ref[...]
        rate = rate_ref[at]
        normed, held, scaled = xh_ref[at], h_ref[at], grs_ref[at]
        inverse, residual_mean, cross = (stat_ref[at, row : row + 1] for row in range(3))
        grad_in = -mixed - (rate * (1.0 / MINI)) * key_dw
        rate_part = -jnp.sum(scaled * key_dw, axis=0, keepdims=True)
        residual = held * gains
        in_mean = mean_rows(grad_in)
        in_cross = mean_rows(grad_in * normed)
        in_held = inverse * (mean_rows(grad_in * residual) - residual_mean * in_mean - cross * in_cross)
        dresidual = inverse * (grad_in - in_mean - normed * in_cross)
        dtarget = dresidual * gains
        dnormed = dtarget * gains - inverse * (grad_in * cross + in_cross * residual)
        dhidden = inverse * (dnormed - mean_rows(dnormed) - normed * (mean_rows(dnormed * normed) + in_held))
        dgain_ref[...] += dresidual * (held + gains * normed)
        dshift_ref[...] += dtarget
        to_first = jnp.where(left, dhidden, dupdated).astype(low)
        to_second = jnp.where(left, dupdated, dhidden).astype(low)
        changed = []
        for part in PARTS:
            pairs = expanded[part][1]
            change = [dot_nn(to_first[:, thin(part)], pairs[0]), dot_nn(to_second[:, thin(part)], pairs[1])]
            changed.append(dweights[part] + lanes(change))
        total_low = (exchange(dupdated) + dhidden).astype(low)
        doffset = doffset + lanes([dot_nn(total_low[:, thin(part)], same) for part in PARTS])
        dweights = changed
        pending = (at, started, (dhidden, dtarget, dweights_low, rate_part))
        started = upcoming
    finish(*pending)
    for part in PARTS:
        dw_ref[:, wide(part)] = dweights[part]
    db_ref[...] = doffset


def ttt_constants():
    lane = np.arange(PAIR)
    row = np.arange(MINI)
    sides = np.concatenate([np.tile(lane < HEAD, (MINI, 1)), np.tile(lane >= HEAD, (MINI, 1))])
    token = lane % MINI
    tri = np.where(token[None] <= row[:, None], 1.0 / (row[:, None] + 1.0), 0.0)
    same = lane[:, None] // MINI == lane[None] // MINI
    crossed = (lane[:, None] + HEAD) % PAIR // MINI == lane[None] // MINI
    scale = np.where(crossed & (token[None] <= token[:, None]), MINI / (token[:, None] + 1.0), 0.0)
    return (
        jnp.asarray(np.concatenate([sides, same, crossed]).astype(np.float32), low),
        jnp.asarray(np.concatenate([tri, scale, scale.T]), full),
    )


def ttt_forward(projected, rates, state, gains, shifts, steps=4):
    count = projected.shape[1] // MINI
    first, begin, end = 0, 0, count
    queries, keys, values = projected, projected, projected
    constants = ttt_constants()
    whole = lambda *shape: pl.BlockSpec(shape, lambda at: (0,) * len(shape))
    column = lambda place: pl.BlockSpec((2, steps * MINI, 768), lambda at, place=place: (0, first + at, place))
    part = column(0)
    saved = lambda *tail: pl.BlockSpec((steps,) + tail, lambda at: (at, 0, 0))
    made = lambda kind, *tail: jax.ShapeDtypeStruct((end - begin,) + tail, kind)
    inputs = [queries, keys, values, rates, *state, gains, shifts, *constants]
    out, *rest = pl.pallas_call(
        lambda *refs: ttt_forward_kernel(steps, *refs),
        grid=((end - begin) // steps,),
        in_specs=[column(0), column(1), column(2), pl.BlockSpec((steps, 1, 384), lambda at: (first + at, 0, 0)), whole(64, 1536), whole(64, 384),
                  whole(64, 384), whole(64, 384), whole(288, 128), whole(272, 128)],
        out_specs=[part, saved(64, 1536), saved(64, 384), saved(64, 384), saved(64, 384), saved(64, 384), saved(8, 384),
                   saved(16, 384)],
        out_shape=[jax.ShapeDtypeStruct((2, count * MINI, 768), full), made(low, 64, 1536), made(full, 64, 384), made(full, 64, 384),
                   made(full, 64, 384), made(full, 64, 384), made(full, 8, 384), made(full, 16, 384)],
        scratch_shapes=[pltpu.VMEM((64, 1536), full)] + [pltpu.VMEM((64, 384), full)] * 3,
        compiler_params=pltpu.CompilerParams(vmem_limit_bytes=60 * 1024 * 1024),
        cost_estimate=pl.CostEstimate(flops=(end - begin) * 1_400_000_000, bytes_accessed=(end - begin) * 1_500_000, transcendentals=0),
        name="ttt_forward",
    )(*inputs)
    return out, rest


def ttt_backward(projected, dout, rates, saved_arrays, state, gains, begin, end, before, steps=4):
    count = projected.shape[1] // MINI
    first, blocks = begin // steps, (end - begin) // steps
    queries, keys = projected, projected
    constants = ttt_constants()
    whole = lambda *shape: pl.BlockSpec(shape, lambda at: (0,) * len(shape))
    part = lambda width, place=0: pl.BlockSpec((2, steps * MINI, width), lambda at: (0, first + blocks - 1 - at, place))
    saved = lambda *tail: pl.BlockSpec((steps,) + tail, lambda at: (first + blocks - 1 - at, 0, 0))
    made = lambda *tail: pl.BlockSpec((steps,) + tail, lambda at: (blocks - 1 - at, 0, 0))
    extra = [] if before is None else [before]
    inputs = [queries, keys, dout, rates, *saved_arrays, gains, *constants, *state]
    states = [whole(64, 1536)] + [whole(64, 384)] * 5
    grad, rate_back, *state = pl.pallas_call(
        lambda *refs: ttt_backward_kernel(steps, *refs),
        grid=(blocks,),
        in_specs=[part(768), part(768, 1), part(768), saved(1, 384),
                  saved(64, 1536), saved(64, 384), saved(64, 384), saved(64, 384), saved(64, 384), saved(8, 384), saved(16, 384),
                  whole(64, 384), whole(288, 128), whole(272, 128)]
        + states + [pl.BlockSpec(memory_space=pl.ANY)] * len(extra),
        out_specs=[part(2304), made(1, 384)] + states,
        out_shape=[jax.ShapeDtypeStruct((2, count * MINI, 2304), low), jax.ShapeDtypeStruct((end - begin, 1, 384), full)]
        + [jax.ShapeDtypeStruct((64, 1536), full)] + [jax.ShapeDtypeStruct((64, 384), full)] * 5,
        scratch_shapes=[pltpu.VMEM((64, 384), full)],
        input_output_aliases={len(inputs): 0} if extra else {},
        compiler_params=pltpu.CompilerParams(vmem_limit_bytes=60 * 1024 * 1024),
        cost_estimate=pl.CostEstimate(flops=(end - begin) * 2_000_000_000, bytes_accessed=(end - begin) * 1_500_000, transcendentals=0),
        name="ttt_backward",
    )(*inputs, *extra)
    return grad, rate_back, state


def silu_parts(gate):
    sigma = jax.nn.sigmoid(gate)
    return gate * sigma, sigma * (1.0 + gate * (1.0 - sigma))


def gelu_parts(values):
    slope = 0.7978845608028654
    turn = jnp.tanh(slope * (values + 0.044715 * values * values * values))
    half = 0.5 * (1.0 + turn)
    return values * half, half + 0.5 * values * (1.0 - turn * turn) * slope * (1.0 + 3 * 0.044715 * values * values)


def row_mean(values):
    return jnp.mean(values, axis=-1, keepdims=True)


def dot_tn(former, latter):
    return lax.dot_general(former, latter, (((0,), (0,)), ((), ())), preferred_element_type=full)


def exact_dot(former, latter):
    total = None
    for _ in range(3):
        part = former.astype(low)
        former = former - part.astype(full)
        term = dot_nn(part, latter)
        total = term if total is None else total + term
    return total


def constant_spec(*shape, at=0, buffers=None):
    index = lambda *steps: (0,) * (len(shape) - 1) + (at,)
    if buffers is None:
        return pl.BlockSpec(shape, index)
    return pl.BlockSpec(shape, index, pipeline_mode=pl.Buffered(buffers))


def call(kernel, name, grid, prefetch, in_specs, out_specs, out_shape, scratch, cost, arrays):
    return pl.pallas_call(
        kernel,
        grid_spec=pltpu.PrefetchScalarGridSpec(
            num_scalar_prefetch=prefetch, grid=grid, in_specs=in_specs, out_specs=out_specs, scratch_shapes=scratch
        ),
        out_shape=out_shape,
        compiler_params=pltpu.CompilerParams(vmem_limit_bytes=60 * 1024 * 1024),
        cost_estimate=pl.CostEstimate(flops=cost, bytes_accessed=cost // 500, transcendentals=0),
        name=name,
    )(*arrays)


ETA = 64
VECTORS = 80
BIAS = 96


def lane_table():
    lane = np.arange(384)
    part, group, side, tile, token = lane // 128, lane // 64 % 2, lane // 32 % 2, lane // 16 % 2, lane % 16
    pair = 4 * part + 2 * group + tile
    return token, pair // 6, 2 * (pair % 6) + side


def lane_constants():
    token, sequence, head = lane_table()
    table = np.zeros((32, 384), np.float32)
    table[:MINI] = token[None] == np.arange(MINI)[:, None]
    table[16], table[17] = sequence, token
    chosen = np.zeros((PAIR, 384), np.float32)
    chosen[ETA + head, np.arange(384)] = 1
    return jnp.asarray(table), jnp.asarray(chosen, low)


def block_copies(from_refs, table, to, columns, semaphores, first):
    started = []
    for place, ref in enumerate(from_refs):
        for item in range(ref.shape[0]):
            begin = pl.multiple_of(table[place * ref.shape[0] + item] * ref.shape[1], 16)
            target = to.at[pl.ds(begin, ref.shape[1]), columns]
            started.append(pltpu.make_async_copy(ref.at[item], target, semaphores.at[first + len(started)]))
    return started


def project_kernel(counts, length_ref, early_table_ref, late_table_ref, tokens_ref, bias_ref, table_ref, chosen_ref, *refs):
    early_refs, late_refs, refs = refs[: counts[0]], refs[counts[0] : sum(counts)], refs[sum(counts) :]
    whole_ref, proj_ref, normed_ref, rate_ref, rest_ref, wt_ref, b_ref, gain_ref, shift_ref, vec_ref, semaphores = refs
    at = pl.program_id(0)
    split = 512 // tokens_ref.shape[0]
    wide = proj_ref.shape[1]
    begin_small = whole_ref.shape[1] - PAIR
    cut = early_refs[0].shape[2]

    def copies():
        started = block_copies(early_refs, early_table_ref, whole_ref, slice(0, cut), semaphores, 0)
        return started + block_copies(late_refs, late_table_ref, whole_ref, slice(cut, whole_ref.shape[1]), semaphores, len(started))

    @pl.when(at == 0)
    def _():
        for copy in copies():
            copy.start()
        for copy in copies():
            copy.wait()
        small = whole_ref[:, begin_small:].astype(full)
        turned = small.T
        wt_ref[:, :768] = turned[:HEAD]
        wt_ref[:, 768:] = turned[:HEAD]
        vec_ref[...] = turned[VECTORS : VECTORS + 8]
        for place, ref in enumerate((b_ref, gain_ref, shift_ref)):
            total = jnp.zeros((HEAD, 384), full)
            for head in range(12):
                column = small[HEAD * head : HEAD * (head + 1), VECTORS + place : VECTORS + place + 1]
                total = total + column * chosen_ref[ETA + head : ETA + head + 1].astype(full)
            ref[...] = total
        rate_ref[...] = jnp.zeros_like(rate_ref)
        rest_ref[...] = jnp.zeros_like(rest_ref)

    values = tokens_ref[...].astype(full)
    normed = (values * lax.rsqrt(row_mean(values * values) + epsilon) * vec_ref[3:4]).astype(low)
    normed_ref[...] = normed
    proj_ref[...] = dot_nn(normed, whole_ref[:, :wide])
    last = dot_nn(normed, whole_ref[:, begin_small:])
    spread = exact_dot(last + bias_ref[...], chosen_ref[...])
    blocks = spread.shape[0] // MINI
    spread = jnp.sum(spread.reshape(blocks, MINI, 384) * table_ref[:MINI][None], axis=1)
    sequence, token = table_ref[16:17], table_ref[17:18]
    mine = sequence == (at // split).astype(full)
    sigma = jax.nn.sigmoid(spread)
    begin = (at % split) * blocks
    block = lax.broadcasted_iota(jnp.int32, spread.shape, 0) + begin
    live = (block * MINI).astype(full) + token < length_ref[at // split].astype(full)
    here = pl.ds(begin, blocks)
    rate_ref[here, 0, :] += jnp.where(live & mine, sigma * (1.0 / HEAD), 0.0)
    rest_ref[here, :] += jnp.where(mine, 1.0 - sigma, 0.0)


def project(lengths, tokens, early, late, bias_row):
    rows, width = tokens.shape
    table, chosen = lane_constants()
    tile = rows // 2
    columns = early[0][0].shape[2] + late[0][0].shape[2]
    counts = len(early[0]), len(late[0])
    row = lambda n: pl.BlockSpec((tile, n), lambda at, *_: (at, 0))
    shape = jax.ShapeDtypeStruct
    return call(
        lambda *refs: project_kernel(counts, *refs), "project", (2,), 3,
        [row(width), constant_spec(1, PAIR), constant_spec(32, 384), constant_spec(PAIR, 384)]
        + [pl.BlockSpec(memory_space=pl.ANY)] * sum(counts),
        [constant_spec(width, columns, buffers=1), row(3 * width), row(width), constant_spec(32, 1, 384), constant_spec(32, 384),
         constant_spec(64, 1536)] + [constant_spec(64, 384)] * 3 + [constant_spec(8, width)],
        [shape((width, columns), low), shape((rows, 3 * width), full), shape((rows, width), low), shape((32, 1, 384), full),
         shape((32, 384), full), shape((64, 1536), full)] + [shape((64, 384), full)] * 3 + [shape((8, width), full)],
        [pltpu.SemaphoreType.DMA((early[1].shape[0] + late[1].shape[0],))], 5_000_000_000,
        (lengths, early[1], late[1], tokens, bias_row, table, chosen, *early[0], *late[0]),
    )


def post_kernel(inner_ref, normed_ref, tokens_ref, w_gate_ref, w_out_ref, vec_ref, gate_ref, mixed_ref, first_ref, second_ref):
    gate = dot_nn(normed_ref[...], w_gate_ref[...])
    gate_ref[...] = gate
    inner = inner_ref[...]
    centred = inner - row_mean(inner)
    standard = centred * lax.rsqrt(row_mean(centred * centred) + epsilon)
    mixed = ((standard * vec_ref[4:5] + vec_ref[5:6]) * gelu_parts(gate)[0]).astype(low)
    mixed_ref[...] = mixed
    first = tokens_ref[...].astype(full) + dot_nn(mixed, w_out_ref[...])
    first_ref[...] = first
    second_ref[...] = (first * lax.rsqrt(row_mean(first * first) + epsilon) * vec_ref[6:7]).astype(low)


def post(inner, normed, tokens, whole, vectors):
    rows, width = tokens.shape
    tile = rows // 4
    row = pl.BlockSpec((tile, width), lambda at: (at, 0))
    shape = jax.ShapeDtypeStruct
    return call(
        post_kernel, "post", (4,), 0,
        [row, row, row, constant_spec(width, width, at=3, buffers=1), constant_spec(width, width, at=4, buffers=1), constant_spec(8, width)],
        [row] * 4, [shape((rows, width), kind) for kind in (full, low, full, low)], [], 4_000_000_000,
        (inner, normed, tokens, whole, whole, vectors),
    )


def store_blocks(table_ref, sent_ref, kept_ref, held_ref, block):
    half = kept_ref.shape[0]
    if block % 8:
        kept_ref[...] = held_ref[:half].astype(kept_ref.dtype)
        sent_ref[...] = held_ref[half:].astype(sent_ref.dtype)
        return
    for pair in range(held_ref.shape[0] // (2 * block)):
        rows = [held_ref[pl.ds(pl.multiple_of(table_ref[2 * pair + side] * block, 8), block), :] for side in range(2)]
        begin = 2 * block * pair
        ref, begin = (kept_ref, begin) if begin < half else (sent_ref, begin - half)
        ref[begin : begin + 2 * block, :] = jnp.concatenate(rows, axis=0).astype(ref.dtype)


def ffn_kernel(block, down_block, steps, counts, table_ref, shared_ref, both_table_ref, down_table_ref, second_ref, first_ref, up_ref, *refs):
    both_refs, refs = refs[: counts[0]], refs[counts[0] :]
    down_refs, refs = refs[: counts[1]], refs[counts[1] :]
    aligned = block % 8 == 0
    out_ref, dsecond_ref, sent_ref, kept_ref, *refs = refs
    natural_ref, refs = (None, refs) if aligned else (refs[0], refs[1:])
    turned, total, act, both_low, held, w_both, w_down_all, held_down, semaphores = refs
    at = pl.program_id(0)
    size = act.shape[1]
    hidden = w_down_all.shape[0]

    def copies():
        started = block_copies(both_refs, both_table_ref, w_both, slice(None), semaphores, 0)
        return started + block_copies(down_refs, down_table_ref, w_down_all, slice(None), semaphores, len(started))

    @pl.when(at == 0)
    def _():
        for copy in copies():
            copy.start()
        turned[...] = second_ref[...].T
        total[...] = first_ref[...]
        dsecond_ref[...] = jnp.zeros_like(dsecond_ref)
        for copy in copies():
            copy.wait()

    @pl.when(at < steps)
    def _():
        columns = pl.ds(pl.multiple_of(at * size, PAIR), size)
        w_gate, w_up = w_both[:, columns], w_both[:, pl.ds(pl.multiple_of(hidden + at * size, PAIR), size)]
        w_down = w_down_all[columns, :]
        second, upstream = second_ref[...], up_ref[...]
        cuts = [slice(begin, begin + size // 2) for begin in range(0, size, size // 2)]
        made = [(dot_nn(second, w_gate[:, cut]), dot_nn(second, w_up[:, cut]), dot_nt(upstream, w_down[cut])) for cut in cuts]
        for cut, (gate, up, dact) in zip(cuts, made):
            value, slope = silu_parts(gate)
            act[:, cut] = (value * up).astype(low)
            both_low[:, cut] = (dact * up * slope).astype(low)
            both_low[:, size + cut.start : size + cut.stop] = (dact * value).astype(low)
        total[...] += dot_nn(act[...], w_down)
        dsecond_ref[...] += dot_nt(both_low[:, :size], w_gate) + dot_nt(both_low[:, size:], w_up)
        ddown = dot_tn(act[...], upstream)
        held[...] = dot_nn(turned[...], both_low[...])
        if aligned:
            count = size // down_block
            third = ddown.shape[1] // 3
            for place in range(count):
                mine = ddown[down_block * place : down_block * (place + 1)]
                pieces = [jnp.concatenate([mine[8 * row : 8 * row + 8, third * part : third * (part + 1)] for row in range(down_block // 8)],
                                          axis=1) for part in range(3)]
                held_down[pl.ds(pl.multiple_of((at * count + place) * block, 8), block), :] = jnp.concatenate(pieces, axis=0)
        else:
            natural_ref[pl.ds(pl.multiple_of(at * size, 16), size), :] = ddown.astype(low)
        store_blocks(table_ref, sent_ref, kept_ref, held, block)

    @pl.when(at == steps - 1)
    def _():
        out_ref[...] = total[...].astype(low)

    if aligned:
        for extra in range(held_down.shape[1] // (2 * size)):

            @pl.when(at == steps + extra)
            def _():
                store_blocks(shared_ref, sent_ref, kept_ref, held_down.at[:, 2 * size * extra : 2 * size * (extra + 1)], block)


def ffn(table, shared, second, first, upstream, both, down, devices, steps):
    rows, width = second.shape
    hidden = down[0][0].shape[1] * down[1].shape[0]
    size = hidden // steps
    aligned = width // devices % 8 == 0
    columns = 3 * hidden if aligned else 2 * hidden
    shape = jax.ShapeDtypeStruct
    counts = len(both[0]), len(down[0])
    copies = both[1].shape[0] + down[1].shape[0]
    natural = [] if aligned else [(hidden, width)]
    return call(
        lambda *refs: ffn_kernel(width // devices, hidden // devices, steps, counts, *refs), "ffn", (columns // (2 * size),), 4,
        [constant_spec(rows, width, buffers=1)] * 3 + [pl.BlockSpec(memory_space=pl.ANY)] * sum(counts),
        [constant_spec(rows, width, buffers=1), constant_spec(rows, width, buffers=1),
         *[pl.BlockSpec((width // 2, 2 * size), lambda at, *_: (0, at))] * 2, *[constant_spec(*item, buffers=1) for item in natural]],
        [shape((rows, width), low), shape((rows, width), full), *[shape((width // 2, columns), low)] * 2,
         *[shape(item, low) for item in natural]],
        [pltpu.VMEM((width, rows), low), pltpu.VMEM((rows, width), full), pltpu.VMEM((rows, size), low),
         pltpu.VMEM((rows, 2 * size), low), pltpu.VMEM((width, 2 * size), full), pltpu.VMEM((width, 2 * hidden), low),
         pltpu.VMEM((hidden, width), low), pltpu.VMEM((width, hidden) if aligned else (8, PAIR), full),
         pltpu.SemaphoreType.DMA((copies,))],
        29_000_000_000, (table, shared, both[1], down[1], second, first, upstream, *both[0], *down[0]),
    )


def fold_kernel(counts, *refs):
    pairs, outs = refs[: 2 * sum(counts)], refs[2 * sum(counts) :]
    for group, count in enumerate(counts):
        sent_ref, kept_ref = outs[2 * group : 2 * group + 2]
        half = kept_ref.shape[0]
        begin = 0
        for _ in range(count):
            (kept, got), pairs = pairs[:2], pairs[2:]
            columns = slice(begin, begin + kept.shape[1])
            sent_ref[:, columns] = (kept[half:].astype(full) + got[half:].astype(full)).astype(low)
            kept_ref[:, columns] = kept[:half].astype(full) + got[:half].astype(full)
            begin = columns.stop


def fold(groups, steps):
    specs, arrays, outs, shapes = [], [], [], []
    for group in groups:
        rows = group[0][0].shape[0]
        width = 0
        for kept, got, first, columns in group:
            part = columns // steps
            specs += [pl.BlockSpec((rows, part), lambda at, begin=first // part: (0, begin + at))] * 2
            arrays += [kept, got]
            width += part
        outs += [pl.BlockSpec((rows // 2, width), lambda at: (0, at))] * 2
        shapes += [jax.ShapeDtypeStruct((rows // 2, width * steps), kind) for kind in (low, full)]
    results = call(
        lambda *refs: fold_kernel([len(group) for group in groups], *refs), "fold", (steps,), 0, specs, outs, shapes, [], 100_000_000, arrays
    )
    return [(results[place], results[place + 1]) for place in range(0, len(results), 2)]


def post_back_kernel(dsecond_ref, first_ref, up_ref, inner_ref, gate_ref, w_out_ref, vec_ref,
                     dfirst_ref, dgate_ref, dinner_ref, dfirst_low_ref, sums_ref):
    @pl.when(pl.program_id(0) == 0)
    def _():
        sums_ref[...] = jnp.zeros_like(sums_ref)

    first, dsecond = first_ref[...], dsecond_ref[...]
    scale = lax.rsqrt(row_mean(first * first) + epsilon)
    sums_ref[6:7] += jnp.sum(dsecond * first * scale, axis=0, keepdims=True)
    dsecond = dsecond * vec_ref[6:7]
    dfirst = up_ref[...].astype(full) + scale * dsecond - first * (scale * scale * scale * row_mean(first * dsecond))
    dfirst_ref[...] = dfirst
    dfirst_low = dfirst.astype(low)
    dfirst_low_ref[...] = dfirst_low
    dmixed = dot_nt(dfirst_low, w_out_ref[...])
    inner = inner_ref[...]
    centred = inner - row_mean(inner)
    inverse = lax.rsqrt(row_mean(centred * centred) + epsilon)
    standard = centred * inverse
    value, slope = gelu_parts(gate_ref[...])
    dgate_ref[...] = (dmixed * (standard * vec_ref[4:5] + vec_ref[5:6]) * slope).astype(low)
    dpost = dmixed * value
    sums_ref[4:5] += jnp.sum(dpost * standard, axis=0, keepdims=True)
    sums_ref[5:6] += jnp.sum(dpost, axis=0, keepdims=True)
    dpost = dpost * vec_ref[4:5]
    dinner_ref[...] = inverse * (dpost - row_mean(dpost) - standard * row_mean(dpost * standard))


def post_back(dsecond, first, upstream, inner, gate, whole, vectors):
    rows, width = first.shape
    tile = rows // 4
    row = pl.BlockSpec((tile, width), lambda at: (at, 0))
    shape = jax.ShapeDtypeStruct
    return call(
        post_back_kernel, "post_back", (4,), 0,
        [row] * 5 + [constant_spec(width, width, at=4, buffers=1), constant_spec(8, width)],
        [row, row, row, row, constant_spec(8, width)],
        [shape((rows, width), full), shape((rows, width), low), shape((rows, width), full), shape((rows, width), low),
         shape((8, width), full)],
        [], 4_000_000_000, (dsecond, first, upstream, inner, gate, whole, vectors),
    )


def middle_kernel(block, table_ref, mixed_ref, dfirst_ref, normed_ref, dgate_ref, sent_ref, kept_ref, held):
    @pl.when(pl.program_id(0) == 0)
    def _():
        held[...] = dot_tn(mixed_ref[...], dfirst_ref[...])

    @pl.when(pl.program_id(0) == 1)
    def _():
        held[...] = dot_tn(normed_ref[...], dgate_ref[...])

    store_blocks(table_ref, sent_ref, kept_ref, held, block)


def middle_grads(table, mixed, dfirst, normed, dgate, devices):
    rows, width = normed.shape
    whole = constant_spec(rows, width, buffers=1)
    return call(
        lambda *refs: middle_kernel(width // devices, *refs), "middle_grads", (2,), 1,
        [whole] * 4, [pl.BlockSpec((width // 2, width), lambda at, *_: (0, at))] * 2,
        [jax.ShapeDtypeStruct((width // 2, 2 * width), low)] * 2, [pltpu.VMEM((width, width), full)], 3_000_000_000,
        (table, mixed, dfirst, normed, dgate),
    )


def weight_kernel(block, table_ref, normed_ref, grad_ref, sent_ref, kept_ref, turned, held):
    @pl.when(pl.program_id(0) == 0)
    def _():
        turned[...] = normed_ref[...].T

    held[...] = dot_nn(turned[...], grad_ref[...])
    store_blocks(table_ref, sent_ref, kept_ref, held, block)


def weight_grads(table, normed, grads, devices):
    rows, width = normed.shape
    out = pl.BlockSpec((width // 2, width), lambda at, *_: (0, at))
    return call(
        lambda *refs: weight_kernel(width // devices, *refs), "weight_grads", (2,), 1,
        [constant_spec(rows, width, buffers=1), pl.BlockSpec((rows, width), lambda at, *_: (0, at))],
        [out, out], [jax.ShapeDtypeStruct((width // 2, 2 * width), low)] * 2,
        [pltpu.VMEM((width, rows), low), pltpu.VMEM((width, width), full)], 3_000_000_000, (table, normed, grads),
    )


def last_kernel(block, table_ref, normed_ref, grad_ref, sums_ref, dw_ref, db_ref, dgain_ref, dshift_ref, dgain_query_ref,
                dshift_query_ref, rate_ref, rest_ref, lane_ref, chosen_ref, sent_ref, kept_ref, dlog_ref, held):
    rows, width = normed_ref.shape
    turned = normed_ref[...].T
    held[:, :width] = dot_nn(turned, grad_ref[...])
    slots = rate_ref.shape[0] * MINI
    for sequence in range(rows // slots):
        mine = (lane_ref[16:17] == float(sequence)).astype(full)
        spread = rate_ref[:, 0, :] * rest_ref[...] * mine
        spread = (spread[:, None, :] * lane_ref[:MINI][None]).reshape(slots, 384).astype(low)
        dlog_ref[slots * sequence : slots * (sequence + 1)] = dot_nt(spread, chosen_ref[...]).astype(low)
    eta = dot_nn(turned, dlog_ref[...])
    inner = dw_ref[:, :width] + dw_ref[:, width:]
    fixed = jnp.concatenate(
        [inner, jnp.zeros((VECTORS - HEAD, width), full), sums_ref[...], jnp.zeros((PAIR - VECTORS - 8, width), full)], axis=0
    )
    lane = lax.broadcasted_iota(jnp.int32, (HEAD, PAIR), 1)
    chosen = chosen_ref[...].astype(full)
    bias = jnp.sum(rate_ref[:, 0, :] * rest_ref[...], axis=0, keepdims=True)
    held[:, width:] = eta + fixed.T
    bias = jnp.sum(chosen * bias, axis=1, keepdims=True)
    square = jnp.broadcast_to(bias, (PAIR, PAIR)).T[:1]
    bias_row = pltpu.roll(square, BIAS - ETA, axis=1)
    bias_row = jnp.where((lane[:1] >= BIAS) & (lane[:1] < BIAS + 12), bias_row, 0.0)
    lanes_of = [db_ref[...] * (1.0 / MINI), dgain_ref[...] + exchange(dgain_query_ref[...]), dshift_ref[...] + exchange(dshift_query_ref[...])]
    for head in range(12):
        here = pl.ds(HEAD * head, HEAD)
        mask = chosen[ETA + head : ETA + head + 1]
        total = held[here, width:] + bias_row
        for place, values in enumerate(lanes_of):
            column = jnp.sum(values * mask, axis=1, keepdims=True)
            total = total + jnp.where(lane == VECTORS + place, column, 0.0)
        held[here, width:] = total
    store_blocks(table_ref, sent_ref, kept_ref, held, block)


def last_grads(table, normed, grads, sums, state, rate_back, rest, devices):
    rows, width = normed.shape
    lane, chosen = lane_constants()
    spec = lambda array: constant_spec(*array.shape, buffers=1)
    others = (sums, *state, rate_back, rest, lane, chosen)
    shape = jax.ShapeDtypeStruct
    out = constant_spec(width // 2, width + PAIR, buffers=1)
    return call(
        lambda *refs: last_kernel(width // devices, *refs), "last_grads", (1,), 1,
        [spec(normed), constant_spec(rows, width, at=2, buffers=1)] + [spec(array) for array in others],
        [out, out, constant_spec(rows, PAIR, buffers=1)],
        [shape((width // 2, width + PAIR), low)] * 2 + [shape((rows, PAIR), low)],
        [pltpu.VMEM((width, width + PAIR), full)], 3_000_000_000, (table, normed, grads, *others),
    )


def finish_kernel(tokens_ref, dfirst_ref, dqkv_ref, dgate_ref, dlog_ref, w_ref, small_ref, w_gate_ref, vec_ref, out_ref):
    dnormed = dot_nt(dqkv_ref[...], w_ref[...]) + dot_nt(dgate_ref[...], w_gate_ref[...]) + dot_nt(dlog_ref[...], small_ref[...])
    values = tokens_ref[...].astype(full)
    scale = lax.rsqrt(row_mean(values * values) + epsilon)
    dnormed = dnormed * vec_ref[3:4]
    back = scale * dnormed - values * (scale * scale * scale * row_mean(values * dnormed))
    out_ref[...] = (dfirst_ref[...] + back).astype(low)


def finish(tokens, dfirst, dqkv, dgate, dlog, whole, vectors, at, before):
    rows, width = tokens.shape
    tile = rows // 2
    row = lambda n: pl.BlockSpec((tile, n), lambda step: (at, 0))
    arrays = [tokens, dfirst, dqkv, dgate, dlog, whole, whole, whole, vectors]
    extra = [] if before is None else [before]
    return pl.pallas_call(
        lambda *refs: finish_kernel(*refs[:9], refs[-1]),
        grid=(1,),
        in_specs=[row(width), row(width), row(3 * width), row(width), row(PAIR), constant_spec(width, 3 * width, buffers=1),
                  constant_spec(width, PAIR, at=5 * width // PAIR, buffers=1), constant_spec(width, width, at=3, buffers=1),
                  constant_spec(8, width)] + [pl.BlockSpec(memory_space=pl.ANY)] * len(extra),
        out_specs=row(width),
        out_shape=jax.ShapeDtypeStruct((rows, width), low),
        input_output_aliases={len(arrays): 0} if extra else {},
        compiler_params=pltpu.CompilerParams(vmem_limit_bytes=60 * 1024 * 1024),
        cost_estimate=pl.CostEstimate(flops=3_000_000_000, bytes_accessed=10_000_000, transcendentals=0),
        name="finish",
    )(*arrays, *extra)


class Links:
    def __init__(self, dp, fsdp):
        self.axes = ("dp", "fsdp")
        self.count = dp * fsdp
        self.core = fsdp
        self.far = fsdp // 2
        bits = [1 << place for place in reversed(range(self.count.bit_length() - 1))]
        self.others = [bit for bit in bits if bit != self.core]
        near = [bit for bit in reversed(self.others) if bit != self.far]
        near = near[:1] + near[:0:-1]
        turned = [near[turn:] + near[:turn] for turn in range(3)]
        self.orders = {"split": [turned[0], turned[2]], "shared": [turned[1]] * 2}
        self.phases = self.near = len(near)
        self.me = lax.axis_index("dp") * fsdp + lax.axis_index("fsdp")
        self.side = (self.me // self.core) % 2

    def swap(self, values, bits):
        pairs = [(place, place ^ bits[(place // self.core) % 2]) for place in range(self.count)]
        return lax.ppermute(values, self.axes, pairs)

    def one(self, bit):
        return (self.me // bit) % 2

    def join(self, held, bits):
        got = self.swap(held, bits)
        mine = jnp.where(self.side == 0, self.one(bits[0]), self.one(bits[1])) == 0
        return jnp.stack([jnp.where(mine, held, got), jnp.where(mine, got, held)])

    def gather(self, pieces, kinds):
        orders = [[[self.far] + order for order in self.orders[kind]] for kind in kinds]
        held = list(pieces)
        for phase in range(len(orders[0][0])):
            held = [self.join(array, [order[phase] for order in pair]) for array, pair in zip(held, orders)]
            changed = yield held
            held = held if changed is None else changed
        above = [bit for bit in self.others if bit > self.core]
        whole = []
        for array, pair in zip(held, orders):
            got = self.swap(array, [self.core] * 2)
            mine = self.side == 0
            cores = [jnp.where(mine, array, got), jnp.where(mine, got, array)]
            placed = []
            for half, order in zip(cores, pair):
                have = order[::-1]
                placed.append(half.transpose([have.index(bit) for bit in self.others] + [len(have), len(have) + 1]))
            whole.append(jnp.stack(placed, axis=len(above)).reshape(-1, array.shape[-1]))
        yield whole

    def gather_blocks(self, pieces, kinds, pairs, whole_last):
        held = list(pieces)
        orders = [self.orders[kind] for kind in kinds]
        count = self.phases

        def ready(array, place):
            rows = pieces[place].shape[0]
            if not pairs[place]:
                return array.reshape((-1, rows) + array.shape[-1:])
            turned = []
            stacked = array.ndim - 2
            for order in orders[place]:
                have = ([self.far] + order)[:stacked][::-1]
                at = have.index(1)
                turned.append(array.transpose([axis for axis in range(stacked) if axis != at] + [at, stacked, stacked + 1]))
            array = jnp.where(self.side == 0, turned[0], turned[1])
            return array.reshape((-1, 2 * rows) + array.shape[-1:])

        for phase in range(count):
            for place, pair in enumerate(orders):
                held[place] = self.join(held[place], [self.far] * 2 if phase == 0 else [order[phase - 1] for order in pair])
                if phase == count - 1 and not whole_last[place]:
                    held[place] = ready(held[place], place)
            changed = yield held
            held = held if changed is None else changed
        buffers = []
        for place, pair in enumerate(orders):
            last = [order[-1] for order in pair]
            if whole_last[place]:
                buffers.append([ready(self.join(held[place], last), place)])
            else:
                buffers.append([held[place], self.swap(held[place], last), self.swap(held[place], [self.core] * 2)])
        changed = yield buffers
        buffers = buffers if changed is None else changed
        buffers = [list(group) + [self.swap(group[0 if whole else 1], [self.core] * 2)] for group, whole in zip(buffers, whole_last)]

        def places(bits, device, unit):
            found = []
            clear = device & ~(sum(bits) + unit - 1)
            for place in range(1 << len(bits)):
                found.append((clear + sum(bit for at, bit in enumerate(bits) if place >> (len(bits) - 1 - at) & 1)) // unit)
            return jnp.stack(found)

        done = []
        for place, pair in enumerate(orders):
            unit = 2 if pairs[place] else 1
            table = []
            for core, last in ((0, 0), (self.core, 0)) if whole_last[place] else ((0, 0), (0, 1), (self.core, 0), (self.core, 1)):
                by_side = []
                for order in pair:
                    have = ([self.far] + order)[::-1] if whole_last[place] else ([self.far] + order[:-1])[::-1]
                    by_side.append(places([bit for bit in have if bit >= unit], self.me ^ core ^ (order[-1] if last else 0), unit))
                own = self.side if core == 0 else 1 - self.side
                table.append(jnp.where(own == 0, by_side[0], by_side[1]))
            done.append((buffers[place], jnp.concatenate(table).astype(jnp.int32)))
        yield done

    def table(self, kind):
        half = []
        for side in range(2):
            masks = self.orders[kind][side] + [self.far]
            half.append(np.array([sum(bit for at, bit in enumerate(masks) if place >> (len(masks) - 1 - at) & 1)
                                  for place in range(self.count // 2)], np.int32))
        keep = jnp.where(self.side == 0, half[0], half[1])
        send = jnp.where(self.side == 0, half[1], half[0])
        return jnp.concatenate([self.me ^ keep, self.me ^ self.core ^ send]).astype(jnp.int32)

    def exchange_cores(self, pair):
        return pair[1], self.swap(pair[0], [self.core] * 2)

    def step(self, groups, phase):
        done = []
        for (sent, kept), kind in zip(groups, ("split", "shared")):
            bits = [order[phase] for order in self.orders[kind]] if phase < self.near else [self.far] * 2
            done.append((kept, self.swap(sent, bits)))
        return done


def refold(groups, steps):
    return fold([[(kept, got, 0, kept.shape[1])] for kept, got in groups], steps)


def tie(*groups):
    flat, tree = jax.tree.flatten(groups)
    return jax.tree.unflatten(tree, lax.optimization_barrier(flat))


def halves(array):
    half = array.shape[0] // 2
    return array[half:], array[:half]


def tie(*groups):
    flat, tree = jax.tree.flatten(groups)
    return jax.tree.unflatten(tree, lax.optimization_barrier(flat))


def halves(array):
    half = array.shape[0] // 2
    return array[half:], array[:half]


def in_order(table, pair, rows):
    if rows % 8 == 0:
        return pair
    whole = jnp.concatenate([pair[1], pair[0]], axis=0)
    return halves(whole.reshape((-1, rows) + whole.shape[1:])[table].reshape(whole.shape))


def body(dp, fsdp, tokens, lengths, cotangent, mixer_in, w_eta, eta_bias, w_out, inner_w, inner_b, ttt_gain, ttt_shift,
         norm_one, post_gain, post_shift, w_gate_up, w_down, norm_two):
    links = Links(dp, fsdp)
    devices = dp * fsdp
    micro, slots, width = tokens.shape
    rows = micro * slots
    heads = eta_bias.shape[0]
    head = width // heads
    hidden = w_gate_up.shape[1] // 2
    device_rows = width // devices
    table, shared = links.table("split"), links.table("shared")
    zeros = lambda columns: jnp.zeros((device_rows, columns), low)

    vectors = jnp.stack([inner_b, ttt_gain, ttt_shift, norm_one, post_gain, post_shift, norm_two])
    vectors = dot_tn(vectors, jnp.eye(7, PAIR, VECTORS, dtype=low)).astype(low)
    small = jnp.concatenate([inner_w, w_eta, zeros(PAIR - ETA - heads)], axis=1) + vectors
    cut = 21 * PAIR
    pieces = [mixer_in[:, :cut], jnp.concatenate([mixer_in[:, cut:], w_out, small], axis=1)]
    rest = [w_gate_up, w_down]
    kinds = ["split", "shared"]
    aligned = device_rows % 8 == 0
    if aligned:
        mixer_phases = links.gather_blocks(pieces, kinds, [True, True], [False, True])
    else:
        mixer_phases = links.gather(pieces, kinds)
    places = lax.broadcasted_iota(jnp.int32, (micro, slots), 1)
    live = places < lengths
    upstream = jnp.where(live[..., None], cotangent, jnp.zeros_like(cotangent)).reshape(rows, width)
    held = next(mixer_phases)
    for _ in range(links.phases - 2):
        held = mixer_phases.send(held)
    held, rest, upstream = tie(held, rest, upstream)
    rest_phases = links.gather_blocks(rest, kinds, [True, False], [False, False]) if aligned else links.gather(rest, kinds)
    held, rest = mixer_phases.send(held), next(rest_phases)
    held, rest = tie(held, rest)
    held, rest = mixer_phases.send(held), rest_phases.send(rest)
    held, rest = tie(held, rest)
    held = mixer_phases.send(held)
    as_blocks = lambda arrays: [([array[None]], jnp.zeros((1,), jnp.int32)) for array in arrays]
    early, late = held if aligned else as_blocks(held)

    inputs = tokens.reshape(rows, width)
    bias_row = jnp.pad(eta_bias.astype(full), (ETA, PAIR - ETA - heads)).reshape(1, PAIR)
    early, late, rest = tie(early, late, rest)
    rest = rest_phases.send(rest)
    whole, projected, normed, rate_lanes, rest_lanes, start_w, start_b, gain_lanes, shift_lanes, vec_rows = project(
        lengths.reshape(micro), inputs, early, late, bias_row
    )
    projected = projected.reshape(micro, slots, -1)
    rate_lanes, rest = tie(rate_lanes, rest)
    rest = rest_phases.send(rest)
    inner, saved = ttt_forward(projected, rate_lanes, [start_w, start_b], gain_lanes, shift_lanes)
    inner = inner.reshape(rows, width)
    inner, rest = tie(inner, rest)
    rest = drain(rest_phases, rest)
    if not aligned:
        rest = as_blocks(rest)
    gate, mixed, first, second = post(inner, normed, inputs, whole, vec_rows)
    block_out, dsecond, large_sent, large_kept, *natural = ffn(table, shared, second, first, upstream, *rest, devices, dp)
    down_rows = hidden // devices
    unit = min(8, device_rows // 3)
    if not aligned:
        natural = natural[0].reshape(devices, -1, unit, 3, width // 3).transpose(0, 3, 2, 1, 4).reshape(width, hidden)
        pairs = in_order(table, (large_sent, large_kept), device_rows), in_order(shared, halves(natural), device_rows)
        large_sent, large_kept = (jnp.concatenate(pair, axis=1) for pair in zip(*pairs))
    large = links.exchange_cores((large_sent, large_kept))
    dfirst, dgate, dinner, dfirst_low, sums = post_back(dsecond, first, upstream, inner, gate, whole, vec_rows)
    middle = middle_grads(table, mixed, dfirst_low, normed, dgate, devices)
    middle = links.exchange_cores(in_order(table, tuple(middle), device_rows))
    dinner, large, middle = tie(dinner, large, middle)
    groups = fold([[(*large, 0, 2 * hidden), (*middle, 0, 2 * width)], [(*large, 2 * hidden, hidden)]], dp)
    dinner, groups = tie(dinner, groups)
    groups = links.step(groups, 0)
    dinner = dinner.reshape(micro, slots, width)
    state = [jnp.zeros((HEAD, 1536), full)] + [jnp.zeros((HEAD, 384), full)] * 5
    dqkv, rate_late, state = ttt_backward(projected, dinner, rate_lanes, saved, state, gain_lanes, 8, slots // MINI, None)
    dqkv, state, groups = tie(dqkv, state, groups)
    groups = refold(groups, dp)
    dqkv, state, groups = tie(dqkv, state, groups)
    groups = links.step(groups, 1)
    dqkv, rate_early, state = ttt_backward(projected, dinner, rate_lanes, saved, state, gain_lanes, 0, 8, dqkv)
    dqkv = dqkv.reshape(rows, 3 * width)
    rate_back = jnp.concatenate([rate_early, rate_late], axis=0)
    early = weight_grads(table, normed, dqkv, devices)
    dqkv, early, groups = tie(dqkv, list(early), groups)
    groups = refold(groups, dp)
    dqkv, early, groups = tie(dqkv, early, groups)
    for phase in range(2, links.near):
        groups = refold(groups, dp) if phase > 2 else groups
        groups = links.step(groups, phase)
    early = links.exchange_cores(in_order(table, tuple(early), device_rows))
    *late, dlog = last_grads(shared, normed, dqkv, sums, state, rate_back, rest_lanes, devices)
    late, dlog, early, groups = tie(list(late), dlog, early, groups)
    late = links.exchange_cores(in_order(shared, tuple(late), device_rows))
    groups = refold(groups, dp)
    late, groups = tie(late, groups)
    groups = links.step(groups, links.near)
    last = fold([[(*early, 0, 2 * width)], [(*late, 0, width + PAIR)]], 1)
    dlog, last = tie(dlog, last)
    last = links.step(last, 0)
    grad_tokens = None
    for half in range(2):
        grad_tokens = finish(inputs, dfirst, dqkv, dgate, dlog, whole, vec_rows, half, grad_tokens)
        grad_tokens, last = tie(grad_tokens, last)
        last = links.step(refold(last, 1), 1 + half)
    for phase in range(3, links.near + 1):
        last = links.step(refold(last, 1), phase)
    large, down = (kept + got.astype(full) for kept, got in groups)
    early, late = (kept + got.astype(full) for kept, got in last)
    part = hidden // dp
    large = large.reshape(device_rows, dp, -1)
    both = large[:, :, : 2 * part].reshape(device_rows, dp, 2, part).transpose(0, 2, 1, 3).reshape(device_rows, 2 * hidden)
    middle = large[:, :, 2 * part :].reshape(device_rows, 2 * width)
    out_small = late[:, width:]
    out_out, out_gate_in = middle[:, :width], middle[:, width:]
    out_mixer = jnp.concatenate([early, late[:, :width], out_gate_in], axis=1)
    out_eta = out_small[:, ETA : ETA + heads]
    out_norm_one = jnp.sum(mixer_in.astype(full) * out_mixer, axis=1) + jnp.sum(w_eta.astype(full) * out_eta, axis=1)
    out_norm_one = out_norm_one / norm_one.astype(full)
    out_inner_b, out_gain, out_shift, _, out_post_gain, out_post_shift, out_norm_two = (
        out_small[:, VECTORS + place] for place in range(7)
    )
    return (
        block_out.reshape(tokens.shape),
        grad_tokens.reshape(tokens.shape),
        out_mixer,
        out_eta,
        out_small[0, BIAS : BIAS + heads],
        out_out,
        out_small[:, :head],
        out_inner_b,
        out_gain,
        out_shift,
        out_norm_one,
        out_post_gain,
        out_post_shift,
        both,
        down.reshape(3, unit, -1, width // 3).transpose(2, 1, 0, 3).reshape(down_rows, width),
        out_norm_two,
    )


def drain(phases, arrays):
    try:
        while True:
            arrays = phases.send(arrays)
    except StopIteration:
        return arrays


def solution(mesh):
    split = ("dp", "fsdp")
    row, vector, token = P(split, None), P(split), P(None, split, None)
    dp, fsdp = mesh.shape["dp"], mesh.shape["fsdp"]
    return jax.shard_map(
        lambda *arrays: body(dp, fsdp, *arrays),
        mesh=mesh,
        in_specs=(token, P(None, split), token, row, row, P(), row, row) + (vector,) * 6 + (row, row, vector),
        out_specs=(token, token, row, row, P(), row, row) + (vector,) * 6 + (row, row, vector),
        check_vma=False,
    )
```

profile of v0, /device:TPU:0, one launch (start us, length us, event | category | flops | bytes accessed | tf_op | source)
XLA Modules:
  0.0 325.6 jit_solution(13161482933638455426)
XLA Ops:
  4.7 4.0 %collective-permute-start.2 = (bf16[24,1280]{1,0:T(8,128)(2,1)S(1)}, bf16[24,1280]{1,0:T(8,128)(2,1)S(1)}, u32[]{:S(2)}, u32[]{:S(2)}) collective-permute-start(bf16[24,1280]{1,0:T(8,128)(2,1)S(1)} %pad_maximum_fusion.13), channel_id=1, source_target_pairs={{0,4},{1,5},{2,6},{3,7},{4,0},{5,1},{6,2},{7,3},{8,12},{9,13},{10,... | collective-permute-start | bytes 184328 | tf_op jit(solution)/shard_map/ppermute | solution.py:940
  20.0 4.7 %collective-permute-done.1 = bf16[2,24,2688]{2,1,0:T(8,128)(2,1)S(1)} collective-permute-done((bf16[2,24,2688]{2,1,0:T(8,128)(2,1)S(1)}, bf16[2,24,2688]{2,1,0:T(8,128)(2,1)S(1)}, u32[]{:S(2)}, u32[]{:S(2)}) %collective-permute-start.1) | collective-permute-done | bytes 258080 | tf_op jit(solution)/shard_map/ppermute | solution.py:940
  30.0 6.8 %collective-permute-done.7 = bf16[64,768]{1,0:T(8,128)(2,1)S(1)} collective-permute-done((bf16[64,768]{1,0:T(8,128)(2,1)S(1)}, bf16[64,768]{1,0:T(8,128)(2,1)S(1)}, u32[]{:S(2)}, u32[]{:S(2)}) %collective-permute-start.7) | collective-permute-done | bytes 98336 | tf_op jit(solution)/shard_map/ppermute | solution.py:940
  43.7 3.8 %collective-permute-done.12 = bf16[2,64,768]{2,1,0:T(8,128)(2,1)S(1)} collective-permute-done((bf16[2,64,768]{2,1,0:T(8,128)(2,1)S(1)}, bf16[2,64,768]{2,1,0:T(8,128)(2,1)S(1)}, u32[]{:S(2)}, u32[]{:S(2)}) %collective-permute-start.12) | collective-permute-done | bytes 196640 | tf_op jit(solution)/shard_map/ppermute | solution.py:940
  47.6 4.6 %collective-permute-done.11 = bf16[2,24,4096]{2,1,0:T(8,128)(2,1)S(1)} collective-permute-done((bf16[2,24,4096]{2,1,0:T(8,128)(2,1)S(1)}, bf16[2,24,4096]{2,1,0:T(8,128)(2,1)S(1)}, u32[]{:S(2)}, u32[]{:S(2)}) %collective-permute-start.11) | collective-permute-done | bytes 393248 | tf_op jit(solution)/shard_map/ppermute | solution.py:940
  52.3 7.4 %collective-permute-done.10 = bf16[2,2,2,24,1280]{4,3,2,1,0:T(8,128)(2,1)S(1)} collective-permute-done((bf16[2,2,2,24,1280]{4,3,2,1,0:T(8,128)(2,1)S(1)}, bf16[2,2,2,24,1280]{4,3,2,1,0:T(8,128)(2,1)S(1)}, u32[]{:S(2)}, u32[]{:S(2)}) %collective-permute-start.10) | collective-permute-done | bytes 491552 | tf_op jit(solution)/shard_map/ppermute | solution.py:940
  68.2 14.5 %project.1 = (bf16[768,3968]{1,0:T(8,128)(2,1)}, f32[1024,2304]{1,0:T(8,128)}, bf16[1024,768]{1,0:T(8,128)(2,1)}, f32[32,1,384]{2,1,0:T(1,128)}, f32[32,384]{1,0...) custom-call(s32[2]{0:T(128)} %bitcast.206, ...), custom_call_target="tpu_custom_call" | custom-call | flops 5000000000 | bytes 10000000 | tf_op jit(solution)/shard_map/project/pallas_call | solution.py:475
  86.9 21.2 %ttt_forward.1 = (f32[2,512,768]{2,1,0:T(8,128)}, bf16[32,64,1536]{2,1,0:T(8,128)(2,1)}, f32[32,64,384]{2,1,0:T(8,128)}, f32[32,64,384]{2,1,0:T(8,128)}, f32[32,...) custom-call(f32[2,512,2304]{2,1,0:T(8,128)} %bitcast.215, ...), custom_call_target="tpu_custom_call" | custom-call | flops 44800000000 | bytes 48000000 | tf_op jit(solution)/shard_map/ttt_forward/pallas_call | solution.py:389
  110.6 8.5 %post.1 = (f32[1024,768]{1,0:T(8,128)}, bf16[1024,768]{1,0:T(8,128)(2,1)}, f32[1024,768]{1,0:T(8,128)}, bf16[1024,768]{1,0:T(8,128)(2,1)}) custom-call(f32[1024,768]{1,0:T(8,128)} %bitcast.185, bf16[1024,768]{1,0:T(8,128)(2,1)} %get-tuple-element.248.normed_ref.refs_3_.refs_1_, bf16[1024,768]{1,0:T(8,128)(2,1)} %bitcast.182, ...), custom_call_target="tpu_custom_call" | custom-call | flops 4000000000 | bytes 8000000 | tf_op jit(solution)/shard_map/post/pallas_call | solution.py:475
  120.6 43.3 %ffn.1 = (bf16[1024,768]{1,0:T(8,128)(2,1)}, f32[1024,768]{1,0:T(8,128)}, bf16[384,6144]{1,0:T(8,128)(2,1)}, bf16[384,6144]{1,0:T(8,128)(2,1)}) custom-call(s32[32]{0:T(128)} %pad_add_fusion.refs_0_, s32[32]{0:T(128)} %pad_add_fusion.1.refs_1_.refs_0_, s32[16]{0:T(128)} %pad_add_fusion.2.refs_1_.refs_2_, s32[32]{0:T(128)} %concatenate.33.refs_3_, ...), custom_call_target="tpu_custom_call" | custom-call | flops 28999999488 | bytes 58000000 | tf_op jit(solution)/shard_map/ffn/pallas_call | solution.py:475
  164.2 11.9 %post_back.1 = (f32[1024,768]{1,0:T(8,128)}, bf16[1024,768]{1,0:T(8,128)(2,1)}, f32[1024,768]{1,0:T(8,128)}, bf16[1024,768]{1,0:T(8,128)(2,1)}, f32[8,768]{1,0:T(8,128)}) custom-call(f32[1024,768]{1,0:T(8,128)} %get-tuple-element.261.dsecond_ref, f32[1024,768]{1,0:T(8,128)} %get-tuple-element.252.refs_5_.first_ref, bf16[1024,768]{1,0:T(8,128)(2,1)} %bitcast.189, ...), custom_call_target="tpu_custom_call" | custom-call | flops 4000000000 | bytes 8000000 | tf_op jit(solution)/shard_map/post_back/pallas_call | solution.py:475
  176.1 7.8 %middle_grads.1 = (bf16[384,1536]{1,0:T(8,128)(2,1)}, bf16[384,1536]{1,0:T(8,128)(2,1)}) custom-call(s32[32]{0:T(128)} %pad_add_fusion.refs_0_, bf16[1024,768]{1,0:T(8,128)(2,1)} %get-tuple-element.267.refs_1_, bf16[1024,768]{1,0:T(8,128)(2,1)} %get-tuple-element.268.refs_2_, bf16[1024,768]{1,0:T(8,128)(2,1)} %get-tuple-element.248.normed_ref.refs_3_.refs_1_, ...), custom_call_target="tpu_custom_call" | custom-call | flops 3000000000 | bytes 6000000 | tf_op jit(solution)/shard_map/middle_grads/pallas_call | solution.py:475
  188.0 8.2 %fold.8 = (bf16[192,5632]{1,0:T(8,128)(2,1)}, f32[192,5632]{1,0:T(8,128)}, bf16[192,2048]{1,0:T(8,128)(2,1)}, f32[192,2048]{1,0:T(8,128)}) custom-call(bf16[384,6144]{1,0:T(8,128)(2,1)} %get-tuple-element.273.refs_0_.refs_4_, bf16[384,6144]{1,0:T(8,128)(2,1)} %collective-permute-done.23.refs_1_.refs_5_, bf16[384,1536]{1,0:T(8,128)(2,1)} %get-tuple-element.275.refs_2_, ...), custom_call_target="tpu_custom_call" | custom-call | flops 100000000 | bytes 200000 | tf_op jit(solution)/shard_map/fold/pallas_call | solution.py:475
  199.7 22.7 %ttt_backward.2 = (bf16[2,512,2304]{2,1,0:T(8,128)(2,1)}, f32[24,1,384]{2,1,0:T(1,128)}, f32[64,1536]{1,0:T(8,128)}, f32[64,384]{1,0:T(8,128)}, f32[64,384]{1,0:...) custom-call(f32[2,512,2304]{2,1,0:T(8,128)} %bitcast.218, f32[2,512,2304]{2,1,0:T(8,128)} %bitcast.219, ...), custom_call_target="tpu_custom_call" | custom-call | flops 48000000000 | bytes 36000000 | tf_op jit(solution)/shard_map/ttt_backward/pallas_call | solution.py:418
  224.5 5.9 %fold.9 = (bf16[96,5632]{1,0:T(8,128)(2,1)}, f32[96,5632]{1,0:T(8,128)}, bf16[96,2048]{1,0:T(8,128)(2,1)}, f32[96,2048]{1,0:T(8,128)}) custom-call(f32[192,5632]{1,0:T(8,128)} %get-tuple-element.307.refs_0_, bf16[192,5632]{1,0:T(8,128)(2,1)} %copy-done, f32[192,2048]{1,0:T(8,128)} %get-tuple-element.309.refs_2_, bf16[192,2048]{1,0:T(8,128)(2,1)} %copy-done.8), custom_call_target="tpu_custom_call" | custom-call | flops 100000000 | bytes 200000 | tf_op jit(solution)/shard_map/fold/pallas_call | solution.py:475
  232.1 9.5 %ttt_backward.3 = (bf16[2,512,2304]{2,1,0:T(8,128)(2,1)}, f32[8,1,384]{2,1,0:T(1,128)}, f32[64,1536]{1,0:T(8,128)}, f32[64,384]{1,0:T(8,128)}, f32[64,384]{1,0:T...) custom-call(f32[2,512,2304]{2,1,0:T(8,128)} %bitcast.220, ...), custom_call_target="tpu_custom_call", output_to_operand_aliasing={{0}: (20, {})} | custom-call | flops 16000000000 | bytes 12000000 | tf_op jit(solution)/shard_map/ttt_backward/pallas_call | solution.py:418
  241.6 7.1 %weight_grads.1 = (bf16[384,1536]{1,0:T(8,128)(2,1)}, bf16[384,1536]{1,0:T(8,128)(2,1)}) custom-call(s32[32]{0:T(128)} %pad_add_fusion.refs_0_, bf16[1024,768]{1,0:T(8,128)(2,1)} %get-tuple-element.248.normed_ref.refs_3_.refs_1_, bf16[1024,2304]{1,0:T(8,128)(2,1)} %bitcast.177), custom_call_target="tpu_custom_call" | custom-call | flops 3000000000 | bytes 6000000 | tf_op jit(solution)/shard_map/weight_grads/pallas_call | solution.py:475
  249.8 4.3 %fold.10 = (bf16[48,5632]{1,0:T(8,128)(2,1)}, f32[48,5632]{1,0:T(8,128)}, bf16[48,2048]{1,0:T(8,128)(2,1)}, f32[48,2048]{1,0:T(8,128)}) custom-call(f32[96,5632]{1,0:T(8,128)} %get-tuple-element.332.refs_0_, bf16[96,5632]{1,0:T(8,128)(2,1)} %copy-done.6, f32[96,2048]{1,0:T(8,128)} %get-tuple-element.334.refs_2_, bf16[96,2048]{1,0:T(8,128)(2,1)} %copy-done.14), custom_call_target="tpu_custom_call" | custom-call | flops 100000000 | bytes 200000 | tf_op jit(solution)/shard_map/fold/pallas_call | solution.py:475
  257.2 6.2 %last_grads.1 = (bf16[384,896]{1,0:T(8,128)(2,1)}, bf16[384,896]{1,0:T(8,128)(2,1)}, bf16[1024,128]{1,0:T(8,128)(2,1)}) custom-call(s32[32]{0:T(128)} %pad_add_fusion.1.refs_1_.refs_0_, bf16[1024,768]{1,0:T(8,128)(2,1)} %get-tuple-element.248.normed_ref.refs_3_.refs_1_, bf16[1024,2304]{1,0:T(8,128)(2,1)} %bitcast.178, f32[8,768]{1,0:T(8,128)} %get-tuple-element.341.refs_3_, ...), custom_call_target="tpu_custom_call" | custom-call | flops 3000000000 | bytes 6000000 | tf_op jit(solution)/shard_map/last_grads/pallas_call | solution.py:475
  264.6 3.8 %fold.11 = (bf16[24,5632]{1,0:T(8,128)(2,1)}, f32[24,5632]{1,0:T(8,128)}, bf16[24,2048]{1,0:T(8,128)(2,1)}, f32[24,2048]{1,0:T(8,128)}) custom-call(f32[48,5632]{1,0:T(8,128)} %get-tuple-element.365.refs_0_, bf16[48,5632]{1,0:T(8,128)(2,1)} %copy-done.13, f32[48,2048]{1,0:T(8,128)} %get-tuple-element.367.refs_2_, bf16[48,2048]{1,0:T(8,128)(2,1)} %copy-done.17), custom_call_target="tpu_custom_call" | custom-call | flops 100000000 | bytes 200000 | tf_op jit(solution)/shard_map/fold/pallas_call | solution.py:475
  269.3 3.8 %fold.12 = (bf16[192,1536]{1,0:T(8,128)(2,1)}, f32[192,1536]{1,0:T(8,128)}, bf16[192,896]{1,0:T(8,128)(2,1)}, f32[192,896]{1,0:T(8,128)}) custom-call(bf16[384,1536]{1,0:T(8,128)(2,1)} %get-tuple-element.361.refs_0_, bf16[384,1536]{1,0:T(8,128)(2,1)} %copy-done.4, bf16[384,896]{1,0:T(8,128)(2,1)} %get-tuple-element.373.refs_2_, bf16[384,896]{1,0:T(8,128)(2,1)} %copy-done.10), custom_call_target="tpu_custom_call" | custom-call | flops 100000000 | bytes 200000 | tf_op jit(solution)/shard_map/fold/pallas_call | solution.py:475
  274.7 4.0 %collective-permute-start.42 = (bf16[24,2048]{1,0:T(8,128)(2,1)S(1)}, bf16[24,2048]{1,0:T(8,128)(2,1)S(1)}, u32[]{:S(2)}, u32[]{:S(2)}) collective-permute-start(bf16[24,2048]{1,0:T(8,128)(2,1)S(1)} %copy-done.43), channel_id=1, source_target_pairs={{0,4},{1,5},{2,6},{3,7},{4,0},{5,1},{6,2},{7,3},{8,12},{9,13},{10,... | collective-permute-start | bytes 294920 | tf_op jit(solution)/shard_map/ppermute | solution.py:940
  278.8 8.0 %finish.2.refs_9_ = bf16[1024,768]{1,0:T(8,128)(2,1)} custom-call(bf16[1024,768]{1,0:T(8,128)(2,1)} %bitcast.183, f32[1024,768]{1,0:T(8,128)} %get-tuple-element.263.refs_1_, bf16[1024,2304]{1,0:T(8,128)(2,1)} %bitcast.179, bf16[1024,768]{1,0:T(8,128)(2,1)} %get-tuple-element.269.refs_4_.refs_3_, bf16[1024,128]{1,0:T(8,128)(2,1)} %get-tuple-element.379.refs_4_, ...), custom_call_target="tpu_custom_call" | custom-call | flops 3000000000 | bytes 10000000 | tf_op jit(solution)/shard_map/finish/pallas_call | solution.py:907
  293.8 8.0 %finish.3 = bf16[1024,768]{1,0:T(8,128)(2,1)} custom-call(bf16[1024,768]{1,0:T(8,128)(2,1)} %bitcast.184, f32[1024,768]{1,0:T(8,128)} %get-tuple-element.263.refs_1_, bf16[1024,2304]{1,0:T(8,128)(2,1)} %bitcast.180, bf16[1024,768]{1,0:T(8,128)(2,1)} %get-tuple-element.269.refs_4_.refs_3_, ...), custom_call_target="tpu_custom_call", output_to_operand_aliasing={{}: (9, {})} | custom-call | flops 3000000000 | bytes 10000000 | tf_op jit(solution)/shard_map/finish/pallas_call | solution.py:907
  (247 shorter events, 93.5 us)
Async XLA Ops:
  24.9 11.9 %collective-permute-start.7 = (bf16[64,768]{1,0:T(8,128)(2,1)S(1)}, bf16[64,768]{1,0:T(8,128)(2,1)S(1)}, u32[]{:S(2)}, u32[]{:S(2)}) collective-permute-start(bf16[64,768]{1,0:T(8,128)(2,1)S(1)} %copy-done.24), channel_id=1, source_target_pairs={{0,4},{1,5},{2,6},{3,7},{4,0},{5,1},{6,2},{7,3},{8,12},{9,13},{10,... | collective-permute-start | bytes 294920 | tf_op jit(solution)/shard_map/ppermute | solution.py:940
  25.0 14.2 %collective-permute-start.6 = (bf16[24,4096]{1,0:T(8,128)(2,1)S(1)}, bf16[24,4096]{1,0:T(8,128)(2,1)S(1)}, u32[]{:S(2)}, u32[]{:S(2)}) collective-permute-start(bf16[24,4096]{1,0:T(8,128)(2,1)S(1)} %copy-done.18), channel_id=1, source_target_pairs={{0,4},{1,5},{2,6},{3,7},{4,0},{5,1},{6,2},{7,3},{8,12},{9,13},{10,... | collective-permute-start | bytes 589832 | tf_op jit(solution)/shard_map/ppermute | solution.py:940
  27.9 11.4 %collective-permute-start.5 = (bf16[2,2,24,1280]{3,2,1,0:T(8,128)(2,1)S(1)}, bf16[2,2,24,1280]{3,2,1,0:T(8,128)(2,1)S(1)}, u32[]{:S(2)}, u32[]{:S(2)}) collective-permute-start(bf16[2,2,24,1280]{3,2,1,0:T(8,128)(2,1)S(1)} %pad_maximum_fusion.10), channel_id=1, source_target_pairs={{0,2},{1,3},{2,0},{3,1},{4,6},{5,7},{6,4},{7,5},{8,10},{9,11},{10,... | collective-permute-start | bytes 737288 | tf_op jit(solution)/shard_map/ppermute | solution.py:940
  28.5 11.0 %collective-permute-start.4 = (bf16[2,2,24,2688]{3,2,1,0:T(8,128)(2,1)S(1)}, bf16[2,2,24,2688]{3,2,1,0:T(8,128)(2,1)S(1)}, u32[]{:S(2)}, u32[]{:S(2)}) collective-permute-start(bf16[2,2,24,2688]{3,2,1,0:T(8,128)(2,1)S(1)} %pad_maximum_fusion.4), channel_id=1, source_target_pairs={{0,16},{1,17},{2,18},{3,19},{4,20},{5,21},{6,22},{7,23},{8,9},{9,8... | collective-permute-start | bytes 1548296 | tf_op jit(solution)/shard_map/ppermute | solution.py:940
  41.4 10.7 %collective-permute-start.11 = (bf16[2,24,4096]{2,1,0:T(8,128)(2,1)S(1)}, bf16[2,24,4096]{2,1,0:T(8,128)(2,1)S(1)}, u32[]{:S(2)}, u32[]{:S(2)}) collective-permute-start(bf16[2,24,4096]{2,1,0:T(8,128)(2,1)S(1)} %pad_maximum_fusion.6), channel_id=1, source_target_pairs={{0,1},{1,0},{2,3},{3,2},{4,5},{5,4},{6,7},{7,6},{8,10},{9,11},{10,... | collective-permute-start | bytes 1179656 | tf_op jit(solution)/shard_map/ppermute | solution.py:940
  42.9 18.0 %collective-permute-start.8 = (bf16[4,48,2688]{2,1,0:T(8,128)(2,1)S(1)}, bf16[4,48,2688]{2,1,0:T(8,128)(2,1)}, u32[]{:S(2)}, u32[]{:S(2)}) collective-permute-start(bf16[4,48,2688]{2,1,0:T(8,128)(2,1)S(1)} %bitcast.194), channel_id=1, source_target_pairs={{0,2},{1,3},{2,0},{3,1},{4,6},{5,7},{6,4},{7,5},{8,24},{9,25},{10,... | collective-permute-start | bytes 3096584 | tf_op jit(solution)/shard_map/ppermute | solution.py:940
  43.2 17.8 %collective-permute-start.9 = (bf16[4,48,2688]{2,1,0:T(8,128)(2,1)S(1)}, bf16[4,48,2688]{2,1,0:T(8,128)(2,1)S(1)}, u32[]{:S(2)}, u32[]{:S(2)}) collective-permute-start(bf16[4,48,2688]{2,1,0:T(8,128)(2,1)S(1)} %bitcast.195), channel_id=1, source_target_pairs={{0,8},{1,9},{2,10},{3,11},{4,12},{5,13},{6,14},{7,15},{8,0},{9,1},... | collective-permute-start | bytes 3096584 | tf_op jit(solution)/shard_map/ppermute | solution.py:940
  43.2 16.5 %collective-permute-start.10 = (bf16[2,2,2,24,1280]{4,3,2,1,0:T(8,128)(2,1)S(1)}, bf16[2,2,2,24,1280]{4,3,2,1,0:T(8,128)(2,1)S(1)}, u32[]{:S(2)}, u32[]{:S(2)}) collective-permute-start(bf16[2,2,2,24,1280]{4,3,2,1,0:T(8,128)(2,1)S(1)} %pad_maximum_fusion.5), channel_id=1, source_target_pairs={{0,1},{1,0},{2,3},{3,2},{4,5},{5,4},{6,7},{7,6},{8,9},{9,8},{10,11... | collective-permute-start | bytes 1474568 | tf_op jit(solution)/shard_map/ppermute | solution.py:940
  67.2 15.5 %collective-permute-start.16 = (bf16[2,2,64,768]{3,2,1,0:T(8,128)(2,1)S(1)}, bf16[2,2,64,768]{3,2,1,0:T(8,128)(2,1)S(1)}, u32[]{:S(2)}, u32[]{:S(2)}) collective-permute-start(bf16[2,2,64,768]{3,2,1,0:T(8,128)(2,1)S(1)} %pad_maximum_fusion.7), channel_id=1, source_target_pairs={{0,2},{1,3},{2,0},{3,1},{4,6},{5,7},{6,4},{7,5},{8,10},{9,11},{10,... | collective-permute-start | bytes 1179656 | tf_op jit(solution)/shard_map/ppermute | solution.py:940
  67.5 15.4 %collective-permute-start.15 = (bf16[2,2,24,4096]{3,2,1,0:T(8,128)(2,1)S(1)}, bf16[2,2,24,4096]{3,2,1,0:T(8,128)(2,1)S(1)}, u32[]{:S(2)}, u32[]{:S(2)}) collective-permute-start(bf16[2,2,24,4096]{3,2,1,0:T(8,128)(2,1)S(1)} %pad_maximum_fusion.2), channel_id=1, source_target_pairs={{0,16},{1,17},{2,18},{3,19},{4,20},{5,21},{6,22},{7,23},{8,9},{9,8... | collective-permute-start | bytes 2359304 | tf_op jit(solution)/shard_map/ppermute | solution.py:940
  83.4 24.7 %collective-permute-start.17 = (bf16[4,48,4096]{2,1,0:T(8,128)(2,1)S(1)}, bf16[4,48,4096]{2,1,0:T(8,128)(2,1)}, u32[]{:S(2)}, u32[]{:S(2)}) collective-permute-start(bf16[4,48,4096]{2,1,0:T(8,128)(2,1)S(1)} %bitcast.190), channel_id=1, source_target_pairs={{0,2},{1,3},{2,0},{3,1},{4,6},{5,7},{6,4},{7,5},{8,24},{9,25},{10,... | collective-permute-start | bytes 4718600 | tf_op jit(solution)/shard_map/ppermute | solution.py:940
  85.1 23.0 %collective-permute-start.18 = (bf16[4,48,4096]{2,1,0:T(8,128)(2,1)S(1)}, bf16[4,48,4096]{2,1,0:T(8,128)(2,1)}, u32[]{:S(2)}, u32[]{:S(2)}) collective-permute-start(bf16[4,48,4096]{2,1,0:T(8,128)(2,1)S(1)} %bitcast.191), channel_id=1, source_target_pairs={{0,8},{1,9},{2,10},{3,11},{4,12},{5,13},{6,14},{7,15},{8,0},{9,1},... | collective-permute-start | bytes 4718600 | tf_op jit(solution)/shard_map/ppermute | solution.py:940
  85.1 23.0 %collective-permute-start.19 = (bf16[8,64,768]{2,1,0:T(8,128)(2,1)S(1)}, bf16[8,64,768]{2,1,0:T(8,128)(2,1)S(1)}, u32[]{:S(2)}, u32[]{:S(2)}) collective-permute-start(bf16[8,64,768]{2,1,0:T(8,128)(2,1)S(1)} %bitcast.197), channel_id=1, source_target_pairs={{0,1},{1,0},{2,3},{3,2},{4,5},{5,4},{6,7},{7,6},{8,9},{9,8},{10,11... | collective-permute-start | bytes 2359304 | tf_op jit(solution)/shard_map/ppermute | solution.py:940
  86.6 21.5 %collective-permute-start.20 = (bf16[8,64,768]{2,1,0:T(8,128)(2,1)S(1)}, bf16[8,64,768]{2,1,0:T(8,128)(2,1)}, u32[]{:S(2)}, u32[]{:S(2)}) collective-permute-start(bf16[8,64,768]{2,1,0:T(8,128)(2,1)S(1)} %bitcast.198), channel_id=1, source_target_pairs={{0,8},{1,9},{2,10},{3,11},{4,12},{5,13},{6,14},{7,15},{8,0},{9,1},... | collective-permute-start | bytes 2359304 | tf_op jit(solution)/shard_map/ppermute | solution.py:940
  108.1 11.0 %collective-permute-start.21 = (bf16[4,48,4096]{2,1,0:T(8,128)(2,1)}, bf16[4,48,4096]{2,1,0:T(8,128)(2,1)S(1)}, u32[]{:S(2)}, u32[]{:S(2)}) collective-permute-start(bf16[4,48,4096]{2,1,0:T(8,128)(2,1)} %collective-permute-done.17.refs_8_), channel_id=1, source_target_pairs={{0,8},{1,9},{2,10},{3,11},{4,12},{5,13},{6,14},{7,15},{8,0},{9,1},... | collective-permute-start | bytes 4718600 | tf_op jit(solution)/shard_map/ppermute | solution.py:940
  163.9 23.1 %collective-permute-start.23 = (bf16[384,6144]{1,0:T(8,128)(2,1)}, bf16[384,6144]{1,0:T(8,128)(2,1)}, u32[]{:S(2)}, u32[]{:S(2)}) collective-permute-start(bf16[384,6144]{1,0:T(8,128)(2,1)} %get-tuple-element.266), channel_id=1, source_target_pairs={{0,8},{1,9},{2,10},{3,11},{4,12},{5,13},{6,14},{7,15},{8,0},{9,1},... | collective-permute-start | bytes 14155784 | tf_op jit(solution)/shard_map/ppermute | solution.py:940
  196.2 26.9 %collective-permute-start.25 = (bf16[192,5632]{1,0:T(8,128)(2,1)}, bf16[192,5632]{1,0:T(8,128)(2,1)S(1)}, u32[]{:S(2)}, u32[]{:S(2)}) collective-permute-start(bf16[192,5632]{1,0:T(8,128)(2,1)} %get-tuple-element.297), channel_id=1, source_target_pairs={{0,1},{1,0},{2,3},{3,2},{4,5},{5,4},{6,7},{7,6},{8,10},{9,11},{10,... | collective-permute-start | bytes 6488072 | tf_op jit(solution)/shard_map/ppermute | solution.py:940
  196.7 25.7 %collective-permute-start.26 = (bf16[192,2048]{1,0:T(8,128)(2,1)}, bf16[192,2048]{1,0:T(8,128)(2,1)S(1)}, u32[]{:S(2)}, u32[]{:S(2)}) collective-permute-start(bf16[192,2048]{1,0:T(8,128)(2,1)} %get-tuple-element.299), channel_id=1, source_target_pairs={{0,16},{1,17},{2,18},{3,19},{4,20},{5,21},{6,22},{7,23},{8,24},{9,... | collective-permute-start | bytes 2359304 | tf_op jit(solution)/shard_map/ppermute | solution.py:940
  230.4 18.3 %collective-permute-start.27 = (bf16[96,5632]{1,0:T(8,128)(2,1)}, bf16[96,5632]{1,0:T(8,128)(2,1)S(1)}, u32[]{:S(2)}, u32[]{:S(2)}) collective-permute-start(bf16[96,5632]{1,0:T(8,128)(2,1)} %get-tuple-element.326), channel_id=1, source_target_pairs={{0,16},{1,17},{2,18},{3,19},{4,20},{5,21},{6,22},{7,23},{8,9},{9,8... | collective-permute-start | bytes 3244040 | tf_op jit(solution)/shard_map/ppermute | solution.py:940
  231.9 16.8 %collective-permute-start.28 = (bf16[96,2048]{1,0:T(8,128)(2,1)}, bf16[96,2048]{1,0:T(8,128)(2,1)S(1)}, u32[]{:S(2)}, u32[]{:S(2)}) collective-permute-start(bf16[96,2048]{1,0:T(8,128)(2,1)} %get-tuple-element.328), channel_id=1, source_target_pairs={{0,2},{1,3},{2,0},{3,1},{4,6},{5,7},{6,4},{7,5},{8,10},{9,11},{10,... | collective-permute-start | bytes 1179656 | tf_op jit(solution)/shard_map/ppermute | solution.py:940
  273.0 13.8 %collective-permute-start.33 = (bf16[192,1536]{1,0:T(8,128)(2,1)}, bf16[192,1536]{1,0:T(8,128)(2,1)S(1)}, u32[]{:S(2)}, u32[]{:S(2)}) collective-permute-start(bf16[192,1536]{1,0:T(8,128)(2,1)} %get-tuple-element.381), channel_id=1, source_target_pairs={{0,1},{1,0},{2,3},{3,2},{4,5},{5,4},{6,7},{7,6},{8,10},{9,11},{10,... | collective-permute-start | bytes 1769480 | tf_op jit(solution)/shard_map/ppermute | solution.py:940
  274.2 12.6 %collective-permute-start.34 = (bf16[192,896]{1,0:T(8,128)(2,1)}, bf16[192,896]{1,0:T(8,128)(2,1)S(1)}, u32[]{:S(2)}, u32[]{:S(2)}) collective-permute-start(bf16[192,896]{1,0:T(8,128)(2,1)} %get-tuple-element.383), channel_id=1, source_target_pairs={{0,16},{1,17},{2,18},{3,19},{4,20},{5,21},{6,22},{7,23},{8,24},{9,... | collective-permute-start | bytes 1032200 | tf_op jit(solution)/shard_map/ppermute | solution.py:940
  274.7 17.5 %collective-permute-start.42 = (bf16[24,2048]{1,0:T(8,128)(2,1)S(1)}, bf16[24,2048]{1,0:T(8,128)(2,1)S(1)}, u32[]{:S(2)}, u32[]{:S(2)}) collective-permute-start(bf16[24,2048]{1,0:T(8,128)(2,1)S(1)} %copy-done.43), channel_id=1, source_target_pairs={{0,4},{1,5},{2,6},{3,7},{4,0},{5,1},{6,2},{7,3},{8,12},{9,13},{10,... | collective-permute-start | bytes 294920 | tf_op jit(solution)/shard_map/ppermute | solution.py:940
  278.7 28.7 %collective-permute-start.41 = (bf16[24,5632]{1,0:T(8,128)(2,1)S(1)}, bf16[24,5632]{1,0:T(8,128)(2,1)S(1)}, u32[]{:S(2)}, u32[]{:S(2)}) collective-permute-start(bf16[24,5632]{1,0:T(8,128)(2,1)S(1)} %copy-done.42), channel_id=1, source_target_pairs={{0,4},{1,5},{2,6},{3,7},{4,0},{5,1},{6,2},{7,3},{8,12},{9,13},{10,... | collective-permute-start | bytes 811016 | tf_op jit(solution)/shard_map/ppermute | solution.py:940
  (65 other events, 408.0 us)
where the time goes:
time: 330 us; the launch traced here: 326 us
  Pallas kernels  201 us (61%)
  waiting for transfers between devices  44.2 us (13%)
  starting transfers between devices  41.9 us (13%)
  local copies, waits for them, and re-layouts  24.3 us (7%)
  other arithmetic  10.9 us (3%)
    pallas_call x15, Pallas kernels, call(): pl.pallas_call(kernel, grid_spec=pltpu.PrefetchScalarGridSpec(num_scalar_...  132 us
    ppermute x43, waiting for transfers between devices, swap(): return lax.ppermute(values, self.axes, pairs)  44.2 us
    ppermute x43, starting transfers between devices, swap(): return lax.ppermute(values, self.axes, pairs)  41.9 us
    pallas_call x2, Pallas kernels, ttt_backward(): pl.pallas_call(lambda *refs: ttt_backward_kernel(steps, *refs), grid=(blo...  32.2 us
    pallas_call x1, Pallas kernels, ttt_forward(): pl.pallas_call(lambda *refs: ttt_forward_kernel(steps, *refs), grid=((end...  21.2 us
    pallas_call x2, Pallas kernels, finish(): pl.pallas_call(lambda *refs: finish_kernel(*refs[:9], refs[-1]), grid=(1,...  16 us
    unnamed x95, local copies, waits for them, and re-layouts  13.2 us
  transfers between devices with their start and end apart: 43, of which 14 were waited for; matrix products, arithmetic and copies ran while one was open for 6% of the time, Pallas kernels for 41%

commit v1 on v0

--- a/solution.py
+++ b/solution.py
@@ -719,7 +719,7 @@
     )
 
 
-def fold_kernel(counts, *refs):
+def fold_kernel(counts, paired, *refs):
     pairs, outs = refs[: 2 * sum(counts)], refs[2 * sum(counts) :]
     for group, count in enumerate(counts):
         sent_ref, kept_ref = outs[2 * group : 2 * group + 2]
@@ -727,13 +727,22 @@
         begin = 0
         for _ in range(count):
             (kept, got), pairs = pairs[:2], pairs[2:]
-            columns = slice(begin, begin + kept.shape[1])
-            sent_ref[:, columns] = (kept[half:].astype(full) + got[half:].astype(full)).astype(low)
-            kept_ref[:, columns] = kept[:half].astype(full) + got[:half].astype(full)
-            begin = columns.stop
-
-
-def fold(groups, steps):
+            plain = kept.shape[1] - (2 * paired if group + 1 == len(counts) else 0)
+            columns = slice(begin, begin + plain)
+            sent_ref[:, columns] = (kept[half:, :plain].astype(full) + got[half:, :plain].astype(full)).astype(low)
+            kept_ref[:, columns] = (kept[:half, :plain].astype(full) + got[:half, :plain].astype(full)).astype(kept_ref.dtype)
+            if plain < kept.shape[1]:
+                total = kept[:, plain:].astype(full) + got[:, plain:].astype(full)
+                total = total[:, :paired] + total[:, paired:]
+                high = total[half:].astype(low)
+                sent_ref[:, plain : plain + paired] = high
+                sent_ref[:, plain + paired :] = (total[half:] - high.astype(full)).astype(low)
+                kept_ref[:, plain : plain + paired] = total[:half]
+                kept_ref[:, plain + paired :] = jnp.zeros_like(total[:half])
+            begin += kept.shape[1]
+
+
+def fold(groups, steps, paired=0, kind=full):
     specs, arrays, outs, shapes = [], [], [], []
     for group in groups:
         rows = group[0][0].shape[0]
@@ -744,9 +753,10 @@
             arrays += [kept, got]
             width += part
         outs += [pl.BlockSpec((rows // 2, width), lambda at: (0, at))] * 2
-        shapes += [jax.ShapeDtypeStruct((rows // 2, width * steps), kind) for kind in (low, full)]
+        shapes += [jax.ShapeDtypeStruct((rows // 2, width * steps), out) for out in (low, kind)]
     results = call(
-        lambda *refs: fold_kernel([len(group) for group in groups], *refs), "fold", (steps,), 0, specs, outs, shapes, [], 100_000_000, arrays
+        lambda *refs: fold_kernel([len(group) for group in groups], paired, *refs), "fold", (steps,), 0, specs, outs, shapes, [],
+        100_000_000, arrays,
     )
     return [(results[place], results[place + 1]) for place in range(0, len(results), 2)]
 
@@ -856,7 +866,7 @@
     lane = lax.broadcasted_iota(jnp.int32, (HEAD, PAIR), 1)
     chosen = chosen_ref[...].astype(full)
     bias = jnp.sum(rate_ref[:, 0, :] * rest_ref[...], axis=0, keepdims=True)
-    held[:, width:] = eta + fixed.T
+    held[:, width : width + PAIR] = eta + fixed.T
     bias = jnp.sum(chosen * bias, axis=1, keepdims=True)
     square = jnp.broadcast_to(bias, (PAIR, PAIR)).T[:1]
     bias_row = pltpu.roll(square, BIAS - ETA, axis=1)
@@ -865,11 +875,13 @@
     for head in range(12):
         here = pl.ds(HEAD * head, HEAD)
         mask = chosen[ETA + head : ETA + head + 1]
-        total = held[here, width:] + bias_row
+        total = held[here, width : width + PAIR] + bias_row
         for place, values in enumerate(lanes_of):
             column = jnp.sum(values * mask, axis=1, keepdims=True)
             total = total + jnp.where(lane == VECTORS + place, column, 0.0)
-        held[here, width:] = total
+        high = total.astype(low).astype(full)
+        held[here, width : width + PAIR] = high
+        held[here, width + PAIR :] = total - high
     store_blocks(table_ref, sent_ref, kept_ref, held, block)
 
 
@@ -879,13 +891,13 @@
     spec = lambda array: constant_spec(*array.shape, buffers=1)
     others = (sums, *state, rate_back, rest, lane, chosen)
     shape = jax.ShapeDtypeStruct
-    out = constant_spec(width // 2, width + PAIR, buffers=1)
+    out = constant_spec(width // 2, width + 2 * PAIR, buffers=1)
     return call(
         lambda *refs: last_kernel(width // devices, *refs), "last_grads", (1,), 1,
         [spec(normed), constant_spec(rows, width, at=2, buffers=1)] + [spec(array) for array in others],
         [out, out, constant_spec(rows, PAIR, buffers=1)],
-        [shape((width // 2, width + PAIR), low)] * 2 + [shape((rows, PAIR), low)],
-        [pltpu.VMEM((width, width + PAIR), full)], 3_000_000_000, (table, normed, grads, *others),
+        [shape((width // 2, width + 2 * PAIR), low)] * 2 + [shape((rows, PAIR), low)],
+        [pltpu.VMEM((width, width + 2 * PAIR), full)], 3_000_000_000, (table, normed, grads, *others),
     )
 
 
@@ -1045,8 +1057,8 @@
         return done
 
 
-def refold(groups, steps):
-    return fold([[(kept, got, 0, kept.shape[1])] for kept, got in groups], steps)
+def refold(groups, steps, paired=0):
+    return fold([[(kept, got, 0, kept.shape[1])] for kept, got in groups], steps, paired)
 
 
 def tie(*groups):
@@ -1107,7 +1119,9 @@
     held = next(mixer_phases)
     for _ in range(links.phases - 2):
         held = mixer_phases.send(held)
-    held, rest, upstream = tie(held, rest, upstream)
+    state = [jnp.zeros((HEAD, 1536), full), jnp.zeros((HEAD, 384), full)]
+    held, rest, upstream, state = tie(held, rest, upstream, state)
+    zero_state = [state[0]] + [state[1]] * 5
     rest_phases = links.gather_blocks(rest, kinds, [True, False], [False, False]) if aligned else links.gather(rest, kinds)
     held, rest = mixer_phases.send(held), next(rest_phases)
     held, rest = tie(held, rest)
@@ -1146,50 +1160,49 @@
     middle = middle_grads(table, mixed, dfirst_low, normed, dgate, devices)
     middle = links.exchange_cores(in_order(table, tuple(middle), device_rows))
     dinner, large, middle = tie(dinner, large, middle)
-    groups = fold([[(*large, 0, 2 * hidden), (*middle, 0, 2 * width)], [(*large, 2 * hidden, hidden)]], dp)
+    groups = fold([[(*large, 0, 2 * hidden), (*middle, 0, 2 * width)], [(*large, 2 * hidden, hidden)]], dp, 0, low)
     dinner, groups = tie(dinner, groups)
     groups = links.step(groups, 0)
     dinner = dinner.reshape(micro, slots, width)
-    state = [jnp.zeros((HEAD, 1536), full)] + [jnp.zeros((HEAD, 384), full)] * 5
-    dqkv, rate_late, state = ttt_backward(projected, dinner, rate_lanes, saved, state, gain_lanes, 8, slots // MINI, None)
+    dqkv, rate_late, state = ttt_backward(projected, dinner, rate_lanes, saved, zero_state, gain_lanes, 4, slots // MINI, None)
     dqkv, state, groups = tie(dqkv, state, groups)
-    groups = refold(groups, dp)
+    groups = refold(groups, 2)
     dqkv, state, groups = tie(dqkv, state, groups)
     groups = links.step(groups, 1)
-    dqkv, rate_early, state = ttt_backward(projected, dinner, rate_lanes, saved, state, gain_lanes, 0, 8, dqkv)
+    dqkv, rate_early, state = ttt_backward(projected, dinner, rate_lanes, saved, state, gain_lanes, 0, 4, dqkv)
     dqkv = dqkv.reshape(rows, 3 * width)
     rate_back = jnp.concatenate([rate_early, rate_late], axis=0)
     early = weight_grads(table, normed, dqkv, devices)
     dqkv, early, groups = tie(dqkv, list(early), groups)
-    groups = refold(groups, dp)
+    groups = refold(groups, 2)
     dqkv, early, groups = tie(dqkv, early, groups)
     for phase in range(2, links.near):
-        groups = refold(groups, dp) if phase > 2 else groups
+        groups = refold(groups, 2) if phase > 2 else groups
         groups = links.step(groups, phase)
     early = links.exchange_cores(in_order(table, tuple(early), device_rows))
     *late, dlog = last_grads(shared, normed, dqkv, sums, state, rate_back, rest_lanes, devices)
     late, dlog, early, groups = tie(list(late), dlog, early, groups)
     late = links.exchange_cores(in_order(shared, tuple(late), device_rows))
-    groups = refold(groups, dp)
+    groups = refold(groups, 2)
     late, groups = tie(late, groups)
     groups = links.step(groups, links.near)
-    last = fold([[(*early, 0, 2 * width)], [(*late, 0, width + PAIR)]], 1)
+    last = fold([[(*early, 0, 2 * width)], [(*late, 0, width + 2 * PAIR)]], 1, PAIR)
     dlog, last = tie(dlog, last)
     last = links.step(last, 0)
     grad_tokens = None
     for half in range(2):
         grad_tokens = finish(inputs, dfirst, dqkv, dgate, dlog, whole, vec_rows, half, grad_tokens)
         grad_tokens, last = tie(grad_tokens, last)
-        last = links.step(refold(last, 1), 1 + half)
+        last = links.step(refold(last, 1, PAIR), 1 + half)
     for phase in range(3, links.near + 1):
-        last = links.step(refold(last, 1), phase)
+        last = links.step(refold(last, 1, PAIR), phase)
     large, down = (kept + got.astype(full) for kept, got in groups)
     early, late = (kept + got.astype(full) for kept, got in last)
     part = hidden // dp
     large = large.reshape(device_rows, dp, -1)
     both = large[:, :, : 2 * part].reshape(device_rows, dp, 2, part).transpose(0, 2, 1, 3).reshape(device_rows, 2 * hidden)
     middle = large[:, :, 2 * part :].reshape(device_rows, 2 * width)
-    out_small = late[:, width:]
+    out_small = late[:, width : width + PAIR] + late[:, width + PAIR :]
     out_out, out_gate_in = middle[:, :width], middle[:, width:]
     out_mixer = jnp.concatenate([early, late[:, :width], out_gate_in], axis=1)
     out_eta = out_small[:, ETA : ETA + heads]

time: 330 us -> 326 us (0.988)
  Pallas kernels: 201 us -> 197 us
    pallas_call x15, Pallas kernels: 132 us -> 128 us  [call(): pl.pallas_call(kernel, grid_spec=pltpu.PrefetchScalarGridSpec(num_scalar_...]
    unnamed x95 -> x97, local copies, waits for them, and re-layouts: 13.2 us -> 13.4 us
  transfers between devices with their start and end apart: 43 -> 43, of which waited for: 14 -> 14; matrix products, arithmetic and copies ran while one was open for 6% -> 5% of each run, Pallas kernels for 41% -> 41%
where the time goes in v1:
time: 326 us; the launch traced here: 322 us
  Pallas kernels  197 us (60%)
  waiting for transfers between devices  45.3 us (14%)
  starting transfers between devices  41.2 us (13%)
  local copies, waits for them, and re-layouts  23.7 us (7%)
  other arithmetic  10.9 us (3%)
    pallas_call x15, Pallas kernels, call(): pl.pallas_call(kernel, grid_spec=pltpu.PrefetchScalarGridSpec(num_scalar_...  128 us
    ppermute x43, waiting for transfers between devices, swap(): return lax.ppermute(values, self.axes, pairs)  45.3 us
    ppermute x43, starting transfers between devices, swap(): return lax.ppermute(values, self.axes, pairs)  41.2 us
    pallas_call x2, Pallas kernels, ttt_backward(): pl.pallas_call(lambda *refs: ttt_backward_kernel(steps, *refs), grid=(blo...  32.3 us
    pallas_call x1, Pallas kernels, ttt_forward(): pl.pallas_call(lambda *refs: ttt_forward_kernel(steps, *refs), grid=((end...  21.2 us
    pallas_call x2, Pallas kernels, finish(): pl.pallas_call(lambda *refs: finish_kernel(*refs[:9], refs[-1]), grid=(1,...  16 us
    unnamed x97, local copies, waits for them, and re-layouts  13.4 us
  transfers between devices with their start and end apart: 43, of which 14 were waited for; matrix products, arithmetic and copies ran while one was open for 5% of the time, Pallas kernels for 41%

profile of v1, /device:TPU:0, one launch (start us, length us, event | category | flops | bytes accessed | tf_op | source)
XLA Modules:
  0.0 321.5 jit_solution(12237615321459856370)
XLA Ops:
  4.7 4.0 %collective-permute-start.2 = (bf16[24,1280]{1,0:T(8,128)(2,1)S(1)}, bf16[24,1280]{1,0:T(8,128)(2,1)S(1)}, u32[]{:S(2)}, u32[]{:S(2)}) collective-permute-start(bf16[24,1280]{1,0:T(8,128)(2,1)S(1)} %pad_maximum_fusion.13), channel_id=1, source_target_pairs={{0,4},{1,5},{2,6},{3,7},{4,0},{5,1},{6,2},{7,3},{8,12},{9,13},{10,... | collective-permute-start | bytes 184328 | tf_op jit(solution)/shard_map/ppermute | solution.py:952
  15.2 3.1 collective-permute-done
  20.0 4.7 %collective-permute-done.1 = bf16[2,24,2688]{2,1,0:T(8,128)(2,1)S(1)} collective-permute-done((bf16[2,24,2688]{2,1,0:T(8,128)(2,1)S(1)}, bf16[2,24,2688]{2,1,0:T(8,128)(2,1)S(1)}, u32[]{:S(2)}, u32[]{:S(2)}) %collective-permute-start.1) | collective-permute-done | bytes 258080 | tf_op jit(solution)/shard_map/ppermute | solution.py:952
  30.0 6.8 %collective-permute-done.7 = bf16[64,768]{1,0:T(8,128)(2,1)S(1)} collective-permute-done((bf16[64,768]{1,0:T(8,128)(2,1)S(1)}, bf16[64,768]{1,0:T(8,128)(2,1)S(1)}, u32[]{:S(2)}, u32[]{:S(2)}) %collective-permute-start.7) | collective-permute-done | bytes 98336 | tf_op jit(solution)/shard_map/ppermute | solution.py:952
  45.7 6.5 %collective-permute-done.11 = bf16[2,24,4096]{2,1,0:T(8,128)(2,1)S(1)} collective-permute-done((bf16[2,24,4096]{2,1,0:T(8,128)(2,1)S(1)}, bf16[2,24,4096]{2,1,0:T(8,128)(2,1)S(1)}, u32[]{:S(2)}, u32[]{:S(2)}) %collective-permute-start.11) | collective-permute-done | bytes 393248 | tf_op jit(solution)/shard_map/ppermute | solution.py:952
  52.3 7.4 %collective-permute-done.10 = bf16[2,2,2,24,1280]{4,3,2,1,0:T(8,128)(2,1)S(1)} collective-permute-done((bf16[2,2,2,24,1280]{4,3,2,1,0:T(8,128)(2,1)S(1)}, bf16[2,2,2,24,1280]{4,3,2,1,0:T(8,128)(2,1)S(1)}, u32[]{:S(2)}, u32[]{:S(2)}) %collective-permute-start.10) | collective-permute-done | bytes 491552 | tf_op jit(solution)/shard_map/ppermute | solution.py:952
  68.2 14.5 %project.1 = (bf16[768,3968]{1,0:T(8,128)(2,1)}, f32[1024,2304]{1,0:T(8,128)}, bf16[1024,768]{1,0:T(8,128)(2,1)}, f32[32,1,384]{2,1,0:T(1,128)}, f32[32,384]{1,0...) custom-call(s32[2]{0:T(128)} %bitcast.217, ...), custom_call_target="tpu_custom_call" | custom-call | flops 5000000000 | bytes 10000000 | tf_op jit(solution)/shard_map/project/pallas_call | solution.py:475
  86.9 21.2 %ttt_forward.1 = (f32[2,512,768]{2,1,0:T(8,128)}, bf16[32,64,1536]{2,1,0:T(8,128)(2,1)}, f32[32,64,384]{2,1,0:T(8,128)}, f32[32,64,384]{2,1,0:T(8,128)}, f32[32,...) custom-call(f32[2,512,2304]{2,1,0:T(8,128)} %bitcast.182, ...), custom_call_target="tpu_custom_call" | custom-call | flops 44800000000 | bytes 48000000 | tf_op jit(solution)/shard_map/ttt_forward/pallas_call | solution.py:389
  110.5 8.6 %post.1 = (f32[1024,768]{1,0:T(8,128)}, bf16[1024,768]{1,0:T(8,128)(2,1)}, f32[1024,768]{1,0:T(8,128)}, bf16[1024,768]{1,0:T(8,128)(2,1)}) custom-call(f32[1024,768]{1,0:T(8,128)} %bitcast.193, bf16[1024,768]{1,0:T(8,128)(2,1)} %get-tuple-element.250.normed_ref.refs_3_.refs_1_, bf16[1024,768]{1,0:T(8,128)(2,1)} %bitcast.190, ...), custom_call_target="tpu_custom_call" | custom-call | flops 4000000000 | bytes 8000000 | tf_op jit(solution)/shard_map/post/pallas_call | solution.py:475
  120.5 43.2 %ffn.1 = (bf16[1024,768]{1,0:T(8,128)(2,1)}, f32[1024,768]{1,0:T(8,128)}, bf16[384,6144]{1,0:T(8,128)(2,1)}, bf16[384,6144]{1,0:T(8,128)(2,1)}) custom-call(s32[32]{0:T(128)} %pad_add_fusion.refs_0_, s32[32]{0:T(128)} %pad_add_fusion.1.refs_1_.refs_0_, s32[16]{0:T(128)} %pad_add_fusion.2.refs_1_.refs_2_, s32[32]{0:T(128)} %concatenate.33.refs_3_, ...), custom_call_target="tpu_custom_call" | custom-call | flops 28999999488 | bytes 58000000 | tf_op jit(solution)/shard_map/ffn/pallas_call | solution.py:475
  163.9 11.9 %post_back.1 = (f32[1024,768]{1,0:T(8,128)}, bf16[1024,768]{1,0:T(8,128)(2,1)}, f32[1024,768]{1,0:T(8,128)}, bf16[1024,768]{1,0:T(8,128)(2,1)}, f32[8,768]{1,0:T(8,128)}) custom-call(f32[1024,768]{1,0:T(8,128)} %get-tuple-element.263.dsecond_ref, f32[1024,768]{1,0:T(8,128)} %get-tuple-element.254.refs_5_.first_ref, bf16[1024,768]{1,0:T(8,128)(2,1)} %bitcast.197, ...), custom_call_target="tpu_custom_call" | custom-call | flops 4000000000 | bytes 8000000 | tf_op jit(solution)/shard_map/post_back/pallas_call | solution.py:475
  175.8 7.7 %middle_grads.1 = (bf16[384,1536]{1,0:T(8,128)(2,1)}, bf16[384,1536]{1,0:T(8,128)(2,1)}) custom-call(s32[32]{0:T(128)} %pad_add_fusion.refs_0_, bf16[1024,768]{1,0:T(8,128)(2,1)} %get-tuple-element.269.refs_1_, bf16[1024,768]{1,0:T(8,128)(2,1)} %get-tuple-element.270.refs_2_, bf16[1024,768]{1,0:T(8,128)(2,1)} %get-tuple-element.250.normed_ref.refs_3_.refs_1_, ...), custom_call_target="tpu_custom_call" | custom-call | flops 3000000000 | bytes 6000000 | tf_op jit(solution)/shard_map/middle_grads/pallas_call | solution.py:475
  187.7 7.5 %fold.8 = (bf16[192,5632]{1,0:T(8,128)(2,1)}, bf16[192,5632]{1,0:T(8,128)(2,1)}, bf16[192,2048]{1,0:T(8,128)(2,1)}, bf16[192,2048]{1,0:T(8,128)(2,1)}) custom-call(bf16[384,6144]{1,0:T(8,128)(2,1)} %get-tuple-element.275.refs_0_.refs_4_, bf16[384,6144]{1,0:T(8,128)(2,1)} %collective-permute-done.23.refs_1_.refs_5_, ...), custom_call_target="tpu_custom_call" | custom-call | flops 100000000 | bytes 200000 | tf_op jit(solution)/shard_map/fold/pallas_call | solution.py:475
  198.6 25.9 %ttt_backward.2 = (bf16[2,512,2304]{2,1,0:T(8,128)(2,1)}, f32[28,1,384]{2,1,0:T(1,128)}, f32[64,1536]{1,0:T(8,128)}, f32[64,384]{1,0:T(8,128)}, f32[64,384]{1,0:...) custom-call(f32[2,512,2304]{2,1,0:T(8,128)} %bitcast.185, f32[2,512,2304]{2,1,0:T(8,128)} %bitcast.186, ...), custom_call_target="tpu_custom_call" | custom-call | flops 56000000000 | bytes 42000000 | tf_op jit(solution)/shard_map/ttt_backward/pallas_call | solution.py:418
  226.1 4.3 %fold.9 = (bf16[96,5632]{1,0:T(8,128)(2,1)}, f32[96,5632]{1,0:T(8,128)}, bf16[96,2048]{1,0:T(8,128)(2,1)}, f32[96,2048]{1,0:T(8,128)}) custom-call(bf16[192,5632]{1,0:T(8,128)(2,1)} %get-tuple-element.311.refs_0_, bf16[192,5632]{1,0:T(8,128)(2,1)} %copy-done, bf16[192,2048]{1,0:T(8,128)(2,1)} %get-tuple-element.313.refs_2_, bf16[192,2048]{1,0:T(8,128)(2,1)} %copy-done.10), custom_call_target="tpu_custom_call" | custom-call | flops 100000000 | bytes 200000 | tf_op jit(solution)/shard_map/fold/pallas_call | solution.py:475
  232.5 6.4 %ttt_backward.3 = (bf16[2,512,2304]{2,1,0:T(8,128)(2,1)}, f32[4,1,384]{2,1,0:T(1,128)}, f32[64,1536]{1,0:T(8,128)}, f32[64,384]{1,0:T(8,128)}, f32[64,384]{1,0:T...) custom-call(f32[2,512,2304]{2,1,0:T(8,128)} %bitcast.187, ...), custom_call_target="tpu_custom_call", output_to_operand_aliasing={{0}: (20, {})} | custom-call | flops 8000000000 | bytes 6000000 | tf_op jit(solution)/shard_map/ttt_backward/pallas_call | solution.py:418
  238.9 7.1 %weight_grads.1 = (bf16[384,1536]{1,0:T(8,128)(2,1)}, bf16[384,1536]{1,0:T(8,128)(2,1)}) custom-call(s32[32]{0:T(128)} %pad_add_fusion.refs_0_, bf16[1024,768]{1,0:T(8,128)(2,1)} %get-tuple-element.250.normed_ref.refs_3_.refs_1_, bf16[1024,2304]{1,0:T(8,128)(2,1)} %bitcast.178), custom_call_target="tpu_custom_call" | custom-call | flops 3000000000 | bytes 6000000 | tf_op jit(solution)/shard_map/weight_grads/pallas_call | solution.py:475
  247.1 3.4 %fold.10 = (bf16[48,5632]{1,0:T(8,128)(2,1)}, f32[48,5632]{1,0:T(8,128)}, bf16[48,2048]{1,0:T(8,128)(2,1)}, f32[48,2048]{1,0:T(8,128)}) custom-call(f32[96,5632]{1,0:T(8,128)} %get-tuple-element.336.refs_0_, bf16[96,5632]{1,0:T(8,128)(2,1)} %copy-done.6, f32[96,2048]{1,0:T(8,128)} %get-tuple-element.338.refs_2_, bf16[96,2048]{1,0:T(8,128)(2,1)} %copy-done.15), custom_call_target="tpu_custom_call" | custom-call | flops 100000000 | bytes 200000 | tf_op jit(solution)/shard_map/fold/pallas_call | solution.py:475
  253.3 6.3 %last_grads.1 = (bf16[384,1024]{1,0:T(8,128)(2,1)}, bf16[384,1024]{1,0:T(8,128)(2,1)}, bf16[1024,128]{1,0:T(8,128)(2,1)}) custom-call(s32[32]{0:T(128)} %pad_add_fusion.1.refs_1_.refs_0_, bf16[1024,768]{1,0:T(8,128)(2,1)} %get-tuple-element.250.normed_ref.refs_3_.refs_1_, bf16[1024,2304]{1,0:T(8,128)(2,1)} %bitcast.179, ...), custom_call_target="tpu_custom_call" | custom-call | flops 3000000000 | bytes 6000000 | tf_op jit(solution)/shard_map/last_grads/pallas_call | solution.py:475
  264.6 3.9 %fold.12 = (bf16[192,1536]{1,0:T(8,128)(2,1)}, f32[192,1536]{1,0:T(8,128)}, bf16[192,1024]{1,0:T(8,128)(2,1)}, f32[192,1024]{1,0:T(8,128)}) custom-call(bf16[384,1536]{1,0:T(8,128)(2,1)} %get-tuple-element.365.refs_0_, bf16[384,1536]{1,0:T(8,128)(2,1)} %copy-done.4, bf16[384,1024]{1,0:T(8,128)(2,1)} %get-tuple-element.377.refs_2_, bf16[384,1024]{1,0:T(8,128)(2,1)} %copy-done.11), custom_call_target="tpu_custom_call" | custom-call | flops 100000000 | bytes 200000 | tf_op jit(solution)/shard_map/fold/pallas_call | solution.py:475
  270.5 3.8 %collective-permute-start.42 = (bf16[24,2048]{1,0:T(8,128)(2,1)S(1)}, bf16[24,2048]{1,0:T(8,128)(2,1)S(1)}, u32[]{:S(2)}, u32[]{:S(2)}) collective-permute-start(bf16[24,2048]{1,0:T(8,128)(2,1)S(1)} %copy-done.44), channel_id=1, source_target_pairs={{0,4},{1,5},{2,6},{3,7},{4,0},{5,1},{6,2},{7,3},{8,12},{9,13},{10,... | collective-permute-start | bytes 294920 | tf_op jit(solution)/shard_map/ppermute | solution.py:952
  274.4 8.0 %finish.2.refs_9_ = bf16[1024,768]{1,0:T(8,128)(2,1)} custom-call(bf16[1024,768]{1,0:T(8,128)(2,1)} %bitcast.191, f32[1024,768]{1,0:T(8,128)} %get-tuple-element.265.refs_1_, bf16[1024,2304]{1,0:T(8,128)(2,1)} %bitcast.180, bf16[1024,768]{1,0:T(8,128)(2,1)} %get-tuple-element.271.refs_4_.refs_3_, bf16[1024,128]{1,0:T(8,128)(2,1)} %get-tuple-element.383.refs_4_, ...), custom_call_target="tpu_custom_call" | custom-call | flops 3000000000 | bytes 10000000 | tf_op jit(solution)/shard_map/finish/pallas_call | solution.py:919
  289.7 8.0 %finish.3 = bf16[1024,768]{1,0:T(8,128)(2,1)} custom-call(bf16[1024,768]{1,0:T(8,128)(2,1)} %bitcast.192, f32[1024,768]{1,0:T(8,128)} %get-tuple-element.265.refs_1_, bf16[1024,2304]{1,0:T(8,128)(2,1)} %bitcast.181, bf16[1024,768]{1,0:T(8,128)(2,1)} %get-tuple-element.271.refs_4_.refs_3_, ...), custom_call_target="tpu_custom_call", output_to_operand_aliasing={{}: (9, {})} | custom-call | flops 3000000000 | bytes 10000000 | tf_op jit(solution)/shard_map/finish/pallas_call | solution.py:919
  302.5 3.0 collective-permute-done.38.refs_3_
  (249 shorter events, 92.2 us)
Async XLA Ops:
  24.9 11.9 %collective-permute-start.7 = (bf16[64,768]{1,0:T(8,128)(2,1)S(1)}, bf16[64,768]{1,0:T(8,128)(2,1)S(1)}, u32[]{:S(2)}, u32[]{:S(2)}) collective-permute-start(bf16[64,768]{1,0:T(8,128)(2,1)S(1)} %copy-done.25), channel_id=1, source_target_pairs={{0,4},{1,5},{2,6},{3,7},{4,0},{5,1},{6,2},{7,3},{8,12},{9,13},{10,... | collective-permute-start | bytes 294920 | tf_op jit(solution)/shard_map/ppermute | solution.py:952
  25.0 14.2 %collective-permute-start.6 = (bf16[24,4096]{1,0:T(8,128)(2,1)S(1)}, bf16[24,4096]{1,0:T(8,128)(2,1)S(1)}, u32[]{:S(2)}, u32[]{:S(2)}) collective-permute-start(bf16[24,4096]{1,0:T(8,128)(2,1)S(1)} %copy-done.19), channel_id=1, source_target_pairs={{0,4},{1,5},{2,6},{3,7},{4,0},{5,1},{6,2},{7,3},{8,12},{9,13},{10,... | collective-permute-start | bytes 589832 | tf_op jit(solution)/shard_map/ppermute | solution.py:952
  27.9 11.4 %collective-permute-start.5 = (bf16[2,2,24,1280]{3,2,1,0:T(8,128)(2,1)S(1)}, bf16[2,2,24,1280]{3,2,1,0:T(8,128)(2,1)S(1)}, u32[]{:S(2)}, u32[]{:S(2)}) collective-permute-start(bf16[2,2,24,1280]{3,2,1,0:T(8,128)(2,1)S(1)} %pad_maximum_fusion.10), channel_id=1, source_target_pairs={{0,2},{1,3},{2,0},{3,1},{4,6},{5,7},{6,4},{7,5},{8,10},{9,11},{10,... | collective-permute-start | bytes 737288 | tf_op jit(solution)/shard_map/ppermute | solution.py:952
  28.5 11.0 %collective-permute-start.4 = (bf16[2,2,24,2688]{3,2,1,0:T(8,128)(2,1)S(1)}, bf16[2,2,24,2688]{3,2,1,0:T(8,128)(2,1)S(1)}, u32[]{:S(2)}, u32[]{:S(2)}) collective-permute-start(bf16[2,2,24,2688]{3,2,1,0:T(8,128)(2,1)S(1)} %pad_maximum_fusion.4), channel_id=1, source_target_pairs={{0,16},{1,17},{2,18},{3,19},{4,20},{5,21},{6,22},{7,23},{8,9},{9,8... | collective-permute-start | bytes 1548296 | tf_op jit(solution)/shard_map/ppermute | solution.py:952
  42.9 18.0 %collective-permute-start.9 = (bf16[4,48,2688]{2,1,0:T(8,128)(2,1)S(1)}, bf16[4,48,2688]{2,1,0:T(8,128)(2,1)S(1)}, u32[]{:S(2)}, u32[]{:S(2)}) collective-permute-start(bf16[4,48,2688]{2,1,0:T(8,128)(2,1)S(1)} %bitcast.204), channel_id=1, source_target_pairs={{0,8},{1,9},{2,10},{3,11},{4,12},{5,13},{6,14},{7,15},{8,0},{9,1},... | collective-permute-start | bytes 3096584 | tf_op jit(solution)/shard_map/ppermute | solution.py:952
  43.0 18.0 %collective-permute-start.8 = (bf16[4,48,2688]{2,1,0:T(8,128)(2,1)S(1)}, bf16[4,48,2688]{2,1,0:T(8,128)(2,1)}, u32[]{:S(2)}, u32[]{:S(2)}) collective-permute-start(bf16[4,48,2688]{2,1,0:T(8,128)(2,1)S(1)} %bitcast.205), channel_id=1, source_target_pairs={{0,2},{1,3},{2,0},{3,1},{4,6},{5,7},{6,4},{7,5},{8,24},{9,25},{10,... | collective-permute-start | bytes 3096584 | tf_op jit(solution)/shard_map/ppermute | solution.py:952
  43.2 16.5 %collective-permute-start.10 = (bf16[2,2,2,24,1280]{4,3,2,1,0:T(8,128)(2,1)S(1)}, bf16[2,2,2,24,1280]{4,3,2,1,0:T(8,128)(2,1)S(1)}, u32[]{:S(2)}, u32[]{:S(2)}) collective-permute-start(bf16[2,2,2,24,1280]{4,3,2,1,0:T(8,128)(2,1)S(1)} %pad_maximum_fusion.5), channel_id=1, source_target_pairs={{0,1},{1,0},{2,3},{3,2},{4,5},{5,4},{6,7},{7,6},{8,9},{9,8},{10,11... | collective-permute-start | bytes 1474568 | tf_op jit(solution)/shard_map/ppermute | solution.py:952
  67.2 15.5 %collective-permute-start.16 = (bf16[2,2,64,768]{3,2,1,0:T(8,128)(2,1)S(1)}, bf16[2,2,64,768]{3,2,1,0:T(8,128)(2,1)S(1)}, u32[]{:S(2)}, u32[]{:S(2)}) collective-permute-start(bf16[2,2,64,768]{3,2,1,0:T(8,128)(2,1)S(1)} %pad_maximum_fusion.7), channel_id=1, source_target_pairs={{0,2},{1,3},{2,0},{3,1},{4,6},{5,7},{6,4},{7,5},{8,10},{9,11},{10,... | collective-permute-start | bytes 1179656 | tf_op jit(solution)/shard_map/ppermute | solution.py:952
  67.5 15.4 %collective-permute-start.15 = (bf16[2,2,24,4096]{3,2,1,0:T(8,128)(2,1)S(1)}, bf16[2,2,24,4096]{3,2,1,0:T(8,128)(2,1)S(1)}, u32[]{:S(2)}, u32[]{:S(2)}) collective-permute-start(bf16[2,2,24,4096]{3,2,1,0:T(8,128)(2,1)S(1)} %pad_maximum_fusion.2), channel_id=1, source_target_pairs={{0,16},{1,17},{2,18},{3,19},{4,20},{5,21},{6,22},{7,23},{8,9},{9,8... | collective-permute-start | bytes 2359304 | tf_op jit(solution)/shard_map/ppermute | solution.py:952
  83.4 24.7 %collective-permute-start.20 = (bf16[8,64,768]{2,1,0:T(8,128)(2,1)S(1)}, bf16[8,64,768]{2,1,0:T(8,128)(2,1)S(1)}, u32[]{:S(2)}, u32[]{:S(2)}) collective-permute-start(bf16[8,64,768]{2,1,0:T(8,128)(2,1)S(1)} %bitcast.207), channel_id=1, source_target_pairs={{0,8},{1,9},{2,10},{3,11},{4,12},{5,13},{6,14},{7,15},{8,0},{9,1},... | collective-permute-start | bytes 2359304 | tf_op jit(solution)/shard_map/ppermute | solution.py:952
  83.9 24.2 %collective-permute-start.19 = (bf16[8,64,768]{2,1,0:T(8,128)(2,1)S(1)}, bf16[8,64,768]{2,1,0:T(8,128)(2,1)}, u32[]{:S(2)}, u32[]{:S(2)}) collective-permute-start(bf16[8,64,768]{2,1,0:T(8,128)(2,1)S(1)} %bitcast.208), channel_id=1, source_target_pairs={{0,1},{1,0},{2,3},{3,2},{4,5},{5,4},{6,7},{7,6},{8,9},{9,8},{10,11... | collective-permute-start | bytes 2359304 | tf_op jit(solution)/shard_map/ppermute | solution.py:952
  85.3 22.9 %collective-permute-start.18 = (bf16[4,48,4096]{2,1,0:T(8,128)(2,1)S(1)}, bf16[4,48,4096]{2,1,0:T(8,128)(2,1)}, u32[]{:S(2)}, u32[]{:S(2)}) collective-permute-start(bf16[4,48,4096]{2,1,0:T(8,128)(2,1)S(1)} %bitcast.200), channel_id=1, source_target_pairs={{0,8},{1,9},{2,10},{3,11},{4,12},{5,13},{6,14},{7,15},{8,0},{9,1},... | collective-permute-start | bytes 4718600 | tf_op jit(solution)/shard_map/ppermute | solution.py:952
  85.3 22.9 %collective-permute-start.17 = (bf16[4,48,4096]{2,1,0:T(8,128)(2,1)S(1)}, bf16[4,48,4096]{2,1,0:T(8,128)(2,1)}, u32[]{:S(2)}, u32[]{:S(2)}) collective-permute-start(bf16[4,48,4096]{2,1,0:T(8,128)(2,1)S(1)} %bitcast.201), channel_id=1, source_target_pairs={{0,2},{1,3},{2,0},{3,1},{4,6},{5,7},{6,4},{7,5},{8,24},{9,25},{10,... | collective-permute-start | bytes 4718600 | tf_op jit(solution)/shard_map/ppermute | solution.py:952
  108.1 10.9 %collective-permute-start.21 = (bf16[4,48,4096]{2,1,0:T(8,128)(2,1)}, bf16[4,48,4096]{2,1,0:T(8,128)(2,1)S(1)}, u32[]{:S(2)}, u32[]{:S(2)}) collective-permute-start(bf16[4,48,4096]{2,1,0:T(8,128)(2,1)} %collective-permute-done.17.refs_8_), channel_id=1, source_target_pairs={{0,8},{1,9},{2,10},{3,11},{4,12},{5,13},{6,14},{7,15},{8,0},{9,1},... | collective-permute-start | bytes 4718600 | tf_op jit(solution)/shard_map/ppermute | solution.py:952
  163.8 22.9 %collective-permute-start.23 = (bf16[384,6144]{1,0:T(8,128)(2,1)}, bf16[384,6144]{1,0:T(8,128)(2,1)}, u32[]{:S(2)}, u32[]{:S(2)}) collective-permute-start(bf16[384,6144]{1,0:T(8,128)(2,1)} %get-tuple-element.268), channel_id=1, source_target_pairs={{0,8},{1,9},{2,10},{3,11},{4,12},{5,13},{6,14},{7,15},{8,0},{9,1},... | collective-permute-start | bytes 14155784 | tf_op jit(solution)/shard_map/ppermute | solution.py:952
  195.2 29.4 %collective-permute-start.26 = (bf16[192,2048]{1,0:T(8,128)(2,1)}, bf16[192,2048]{1,0:T(8,128)(2,1)S(1)}, u32[]{:S(2)}, u32[]{:S(2)}) collective-permute-start(bf16[192,2048]{1,0:T(8,128)(2,1)} %get-tuple-element.303), channel_id=1, source_target_pairs={{0,16},{1,17},{2,18},{3,19},{4,20},{5,21},{6,22},{7,23},{8,24},{9,... | collective-permute-start | bytes 2359304 | tf_op jit(solution)/shard_map/ppermute | solution.py:952
  196.7 27.9 %collective-permute-start.25 = (bf16[192,5632]{1,0:T(8,128)(2,1)}, bf16[192,5632]{1,0:T(8,128)(2,1)S(1)}, u32[]{:S(2)}, u32[]{:S(2)}) collective-permute-start(bf16[192,5632]{1,0:T(8,128)(2,1)} %get-tuple-element.301), channel_id=1, source_target_pairs={{0,1},{1,0},{2,3},{3,2},{4,5},{5,4},{6,7},{7,6},{8,10},{9,11},{10,... | collective-permute-start | bytes 6488072 | tf_op jit(solution)/shard_map/ppermute | solution.py:952
  230.4 15.5 %collective-permute-start.27 = (bf16[96,5632]{1,0:T(8,128)(2,1)}, bf16[96,5632]{1,0:T(8,128)(2,1)S(1)}, u32[]{:S(2)}, u32[]{:S(2)}) collective-permute-start(bf16[96,5632]{1,0:T(8,128)(2,1)} %get-tuple-element.330), channel_id=1, source_target_pairs={{0,16},{1,17},{2,18},{3,19},{4,20},{5,21},{6,22},{7,23},{8,9},{9,8... | collective-permute-start | bytes 3244040 | tf_op jit(solution)/shard_map/ppermute | solution.py:952
  231.3 14.7 %collective-permute-start.28 = (bf16[96,2048]{1,0:T(8,128)(2,1)}, bf16[96,2048]{1,0:T(8,128)(2,1)S(1)}, u32[]{:S(2)}, u32[]{:S(2)}) collective-permute-start(bf16[96,2048]{1,0:T(8,128)(2,1)} %get-tuple-element.332), channel_id=1, source_target_pairs={{0,2},{1,3},{2,0},{3,1},{4,6},{5,7},{6,4},{7,5},{8,10},{9,11},{10,... | collective-permute-start | bytes 1179656 | tf_op jit(solution)/shard_map/ppermute | solution.py:952
  268.5 13.9 %collective-permute-start.33 = (bf16[192,1536]{1,0:T(8,128)(2,1)}, bf16[192,1536]{1,0:T(8,128)(2,1)S(1)}, u32[]{:S(2)}, u32[]{:S(2)}) collective-permute-start(bf16[192,1536]{1,0:T(8,128)(2,1)} %get-tuple-element.385), channel_id=1, source_target_pairs={{0,1},{1,0},{2,3},{3,2},{4,5},{5,4},{6,7},{7,6},{8,10},{9,11},{10,... | collective-permute-start | bytes 1769480 | tf_op jit(solution)/shard_map/ppermute | solution.py:952
  270.0 12.4 %collective-permute-start.34 = (bf16[192,1024]{1,0:T(8,128)(2,1)}, bf16[192,1024]{1,0:T(8,128)(2,1)S(1)}, u32[]{:S(2)}, u32[]{:S(2)}) collective-permute-start(bf16[192,1024]{1,0:T(8,128)(2,1)} %get-tuple-element.387), channel_id=1, source_target_pairs={{0,16},{1,17},{2,18},{3,19},{4,20},{5,21},{6,22},{7,23},{8,24},{9,... | collective-permute-start | bytes 1179656 | tf_op jit(solution)/shard_map/ppermute | solution.py:952
  270.5 16.9 %collective-permute-start.42 = (bf16[24,2048]{1,0:T(8,128)(2,1)S(1)}, bf16[24,2048]{1,0:T(8,128)(2,1)S(1)}, u32[]{:S(2)}, u32[]{:S(2)}) collective-permute-start(bf16[24,2048]{1,0:T(8,128)(2,1)S(1)} %copy-done.44), channel_id=1, source_target_pairs={{0,4},{1,5},{2,6},{3,7},{4,0},{5,1},{6,2},{7,3},{8,12},{9,13},{10,... | collective-permute-start | bytes 294920 | tf_op jit(solution)/shard_map/ppermute | solution.py:952
  274.3 27.9 %collective-permute-start.41 = (bf16[24,5632]{1,0:T(8,128)(2,1)S(1)}, bf16[24,5632]{1,0:T(8,128)(2,1)S(1)}, u32[]{:S(2)}, u32[]{:S(2)}) collective-permute-start(bf16[24,5632]{1,0:T(8,128)(2,1)S(1)} %copy-done.43), channel_id=1, source_target_pairs={{0,4},{1,5},{2,6},{3,7},{4,0},{5,1},{6,2},{7,3},{8,12},{9,13},{10,... | collective-permute-start | bytes 811016 | tf_op jit(solution)/shard_map/ppermute | solution.py:952
  286.9 10.8 %collective-permute-start.35 = (bf16[96,1536]{1,0:T(8,128)(2,1)}, bf16[96,1536]{1,0:T(8,128)(2,1)S(1)}, u32[]{:S(2)}, u32[]{:S(2)}) collective-permute-start(bf16[96,1536]{1,0:T(8,128)(2,1)} %get-tuple-element.394), channel_id=1, source_target_pairs={{0,16},{1,17},{2,18},{3,19},{4,20},{5,21},{6,22},{7,23},{8,9},{9,8... | collective-permute-start | bytes 884744 | tf_op jit(solution)/shard_map/ppermute | solution.py:952
  (66 other events, 403.0 us)

commit v2 on v1

--- a/solution.py
+++ b/solution.py
@@ -214,16 +214,16 @@
     b_run[...] = offset
 
 
-def ttt_backward_kernel(steps, q_ref, k_ref, dout_ref, rate_ref, w_ref, xh_ref, h_ref, grs_ref, xb_ref, stat_ref, score_ref,
+def ttt_backward_kernel(steps, carried, q_ref, k_ref, dout_ref, rate_ref, w_ref, xh_ref, h_ref, grs_ref, xb_ref, stat_ref, score_ref,
                         gain_ref, low_ref, full_ref, *refs):
-    states, refs = refs[:6], refs[6:]
+    states, refs = (refs[:6], refs[6:]) if carried else (None, refs)
     grad_ref, rdr_ref, dw_ref, db_ref, dgain_ref, dshift_ref, dgain_query_ref, dshift_query_ref, gain_query = refs[-9:]
     width = 768
 
     @pl.when(pl.program_id(0) == 0)
     def _():
-        for state, ref in zip(states, (dw_ref, db_ref, dgain_ref, dshift_ref, dgain_query_ref, dshift_query_ref)):
-            ref[...] = state[...]
+        for place, ref in enumerate((dw_ref, db_ref, dgain_ref, dshift_ref, dgain_query_ref, dshift_query_ref)):
+            ref[...] = states[place][...] if carried else jnp.zeros_like(ref)
         gain_query[...] = exchange(gain_ref[...])
 
     sides, same, crossed, tri, scale, scale_turned = read_constants(low_ref, full_ref)
@@ -413,15 +413,15 @@
     saved = lambda *tail: pl.BlockSpec((steps,) + tail, lambda at: (first + blocks - 1 - at, 0, 0))
     made = lambda *tail: pl.BlockSpec((steps,) + tail, lambda at: (blocks - 1 - at, 0, 0))
     extra = [] if before is None else [before]
-    inputs = [queries, keys, dout, rates, *saved_arrays, gains, *constants, *state]
+    inputs = [queries, keys, dout, rates, *saved_arrays, gains, *constants, *(state or [])]
     states = [whole(64, 1536)] + [whole(64, 384)] * 5
-    grad, rate_back, *state = pl.pallas_call(
-        lambda *refs: ttt_backward_kernel(steps, *refs),
+    grad, rate_back, *sums = pl.pallas_call(
+        lambda *refs: ttt_backward_kernel(steps, state is not None, *refs),
         grid=(blocks,),
         in_specs=[part(768), part(768, 1), part(768), saved(1, 384),
                   saved(64, 1536), saved(64, 384), saved(64, 384), saved(64, 384), saved(64, 384), saved(8, 384), saved(16, 384),
                   whole(64, 384), whole(288, 128), whole(272, 128)]
-        + states + [pl.BlockSpec(memory_space=pl.ANY)] * len(extra),
+        + (states if state else []) + [pl.BlockSpec(memory_space=pl.ANY)] * len(extra),
         out_specs=[part(2304), made(1, 384)] + states,
         out_shape=[jax.ShapeDtypeStruct((2, count * MINI, 2304), low), jax.ShapeDtypeStruct((end - begin, 1, 384), full)]
         + [jax.ShapeDtypeStruct((64, 1536), full)] + [jax.ShapeDtypeStruct((64, 384), full)] * 5,
@@ -431,7 +431,7 @@
         cost_estimate=pl.CostEstimate(flops=(end - begin) * 2_000_000_000, bytes_accessed=(end - begin) * 1_500_000, transcendentals=0),
         name="ttt_backward",
     )(*inputs, *extra)
-    return grad, rate_back, state
+    return grad, rate_back, sums
 
 
 def silu_parts(gate):
@@ -719,46 +719,99 @@
     )
 
 
-def fold_kernel(counts, paired, *refs):
-    pairs, outs = refs[: 2 * sum(counts)], refs[2 * sum(counts) :]
-    for group, count in enumerate(counts):
-        sent_ref, kept_ref = outs[2 * group : 2 * group + 2]
-        half = kept_ref.shape[0]
-        begin = 0
-        for _ in range(count):
-            (kept, got), pairs = pairs[:2], pairs[2:]
-            plain = kept.shape[1] - (2 * paired if group + 1 == len(counts) else 0)
-            columns = slice(begin, begin + plain)
-            sent_ref[:, columns] = (kept[half:, :plain].astype(full) + got[half:, :plain].astype(full)).astype(low)
-            kept_ref[:, columns] = (kept[:half, :plain].astype(full) + got[:half, :plain].astype(full)).astype(kept_ref.dtype)
-            if plain < kept.shape[1]:
-                total = kept[:, plain:].astype(full) + got[:, plain:].astype(full)
-                total = total[:, :paired] + total[:, paired:]
-                high = total[half:].astype(low)
-                sent_ref[:, plain : plain + paired] = high
-                sent_ref[:, plain + paired :] = (total[half:] - high.astype(full)).astype(low)
-                kept_ref[:, plain : plain + paired] = total[:half]
-                kept_ref[:, plain + paired :] = jnp.zeros_like(total[:half])
-            begin += kept.shape[1]
-
-
-def fold(groups, steps, paired=0, kind=full):
-    specs, arrays, outs, shapes = [], [], [], []
-    for group in groups:
-        rows = group[0][0].shape[0]
+def fold_kernel(layout, last, paired, *refs):
+    outs = refs[sum(sum(members) + extra for members, extra in layout) :]
+    for group, (members, extra) in enumerate(layout):
+        mine, refs = refs[: sum(members) + extra], refs[sum(members) + extra :]
+        totals = []
+        for count in members:
+            totals.append(sum(ref[...].astype(full) for ref in mine[:count]))
+            mine = mine[count:]
+        total = jnp.concatenate(totals, axis=1) if len(totals) > 1 else totals[0]
+        for ref in mine:
+            total = total + ref[...].astype(full)
+        if paired and group + 1 == len(layout):
+            plain = total.shape[1] - 2 * paired
+            tail = total[:, plain : plain + paired] + total[:, plain + paired :]
+            high = tail.astype(low).astype(full)
+            total = jnp.concatenate([total[:, :plain], high, tail - high], axis=1)
+        if last:
+            half = total.shape[0] // 2
+            outs[2 * group][...] = total[half:].astype(low)
+            outs[2 * group + 1][...] = total[:half]
+        else:
+            outs[group][...] = total.astype(low)
+
+
+def fold(groups, rows, steps, paired=0):
+    last = rows // 2 % MINI != 0
+    size, place = (rows, 0) if last else (rows // 2, 1)
+    specs, arrays, outs, shapes, layout = [], [], [], [], []
+    for members, extra in groups:
         width = 0
-        for kept, got, first, columns in group:
+        for addends, first, columns in members:
             part = columns // steps
-            specs += [pl.BlockSpec((rows, part), lambda at, begin=first // part: (0, begin + at))] * 2
-            arrays += [kept, got]
+            specs += [pl.BlockSpec((size, part), lambda at, begin=first // part: (place, begin + at))] * len(addends)
+            arrays += addends
             width += part
-        outs += [pl.BlockSpec((rows // 2, width), lambda at: (0, at))] * 2
-        shapes += [jax.ShapeDtypeStruct((rows // 2, width * steps), out) for out in (low, kind)]
+        specs += [pl.BlockSpec((size, width), lambda at: (place, at))] * len(extra)
+        arrays += extra
+        layout.append(([len(addends) for addends, _, _ in members], len(extra)))
+        outs += [pl.BlockSpec((rows // 2, width), lambda at: (0, at))] * (2 if last else 1)
+        shapes += [jax.ShapeDtypeStruct((rows // 2, width * steps), kind) for kind in ((low, full) if last else (low,))]
     results = call(
-        lambda *refs: fold_kernel([len(group) for group in groups], paired, *refs), "fold", (steps,), 0, specs, outs, shapes, [],
-        100_000_000, arrays,
-    )
-    return [(results[place], results[place + 1]) for place in range(0, len(results), 2)]
+        lambda *refs: fold_kernel(layout, last, paired, *refs), "fold", (steps,), 0, specs, outs, shapes, [], 100_000_000, arrays
+    )
+    return [(results[2 * group], results[2 * group + 1]) for group in range(len(groups))] if last else list(results)
+
+
+class Scatter:
+    def __init__(self, links, groups, rows, steps, paired=0):
+        self.links, self.steps, self.paired = links, steps, paired
+        self.groups = [(members, []) for members in groups]
+        self.rows, self.phase, self.kept, self.sent = rows, 0, None, None
+
+    def fold(self):
+        if self.kept is None:
+            made = fold(self.groups, self.rows, self.steps, self.paired)
+            if self.rows // 2 % MINI:
+                self.sent, self.kept = [sent for sent, _ in made], [kept for _, kept in made]
+            else:
+                self.sent = made
+        else:
+            half = self.rows // 2
+            totals = [kept + got.astype(full) for kept, got in zip(self.kept, self.got)]
+            self.sent, self.kept = [total[half:].astype(low) for total in totals], [total[:half] for total in totals]
+        self.rows //= 2
+
+    def send(self):
+        links, phase = self.links, self.phase
+        self.got = []
+        for sent, kind in zip(self.sent, ("split", "shared")):
+            bits = [order[phase] for order in links.orders[kind]] if phase < links.near else [links.far] * 2
+            self.got.append(links.swap(sent, bits))
+        self.phase += 1
+        if self.kept is None:
+            self.groups = [(members, extra + [got]) for (members, extra), got in zip(self.groups, self.got)]
+
+    def tied(self, *others):
+        state = (self.sent, self.kept, self.got, self.groups) if self.phase else (self.sent,)
+        arrays, tree = jax.tree.flatten(state)
+        numbers = [place for place, array in enumerate(arrays) if not isinstance(array, int)]
+        out = tie(*others, [arrays[place] for place in numbers])
+        for place, array in zip(numbers, out[-1]):
+            arrays[place] = array
+        state = jax.tree.unflatten(tree, arrays)
+        self.sent = state[0]
+        if len(state) > 1:
+            self.kept, self.got, self.groups = state[1:]
+        return out[:-1] if len(others) > 1 else out[0]
+
+    def result(self):
+        while self.phase <= self.links.near:
+            self.fold()
+            self.send()
+        return [kept + got.astype(full) for kept, got in zip(self.kept, self.got)]
 
 
 def post_back_kernel(dsecond_ref, first_ref, up_ref, inner_ref, gate_ref, w_out_ref, vec_ref,
@@ -1049,17 +1102,6 @@
     def exchange_cores(self, pair):
         return pair[1], self.swap(pair[0], [self.core] * 2)
 
-    def step(self, groups, phase):
-        done = []
-        for (sent, kept), kind in zip(groups, ("split", "shared")):
-            bits = [order[phase] for order in self.orders[kind]] if phase < self.near else [self.far] * 2
-            done.append((kept, self.swap(sent, bits)))
-        return done
-
-
-def refold(groups, steps, paired=0):
-    return fold([[(kept, got, 0, kept.shape[1])] for kept, got in groups], steps, paired)
-
 
 def tie(*groups):
     flat, tree = jax.tree.flatten(groups)
@@ -1119,14 +1161,11 @@
     held = next(mixer_phases)
     for _ in range(links.phases - 2):
         held = mixer_phases.send(held)
-    state = [jnp.zeros((HEAD, 1536), full), jnp.zeros((HEAD, 384), full)]
-    held, rest, upstream, state = tie(held, rest, upstream, state)
-    zero_state = [state[0]] + [state[1]] * 5
+    held, rest, upstream = tie(held, rest, upstream)
     rest_phases = links.gather_blocks(rest, kinds, [True, False], [False, False]) if aligned else links.gather(rest, kinds)
     held, rest = mixer_phases.send(held), next(rest_phases)
     held, rest = tie(held, rest)
     held, rest = mixer_phases.send(held), rest_phases.send(rest)
-    held, rest = tie(held, rest)
     held = mixer_phases.send(held)
     as_blocks = lambda arrays: [([array[None]], jnp.zeros((1,), jnp.int32)) for array in arrays]
     early, late = held if aligned else as_blocks(held)
@@ -1160,48 +1199,53 @@
     middle = middle_grads(table, mixed, dfirst_low, normed, dgate, devices)
     middle = links.exchange_cores(in_order(table, tuple(middle), device_rows))
     dinner, large, middle = tie(dinner, large, middle)
-    groups = fold([[(*large, 0, 2 * hidden), (*middle, 0, 2 * width)], [(*large, 2 * hidden, hidden)]], dp, 0, low)
-    dinner, groups = tie(dinner, groups)
-    groups = links.step(groups, 0)
+    large, middle = list(large), list(middle)
+    whole_rows = width // 2
+    first_sum = Scatter(
+        links, [[(large, 0, 2 * hidden), (middle, 0, 2 * width)], [(large, 2 * hidden, hidden)]], whole_rows, 2
+    )
+    first_sum.fold()
+    dinner = first_sum.tied(dinner)
+    first_sum.send()
     dinner = dinner.reshape(micro, slots, width)
-    dqkv, rate_late, state = ttt_backward(projected, dinner, rate_lanes, saved, zero_state, gain_lanes, 4, slots // MINI, None)
-    dqkv, state, groups = tie(dqkv, state, groups)
-    groups = refold(groups, 2)
-    dqkv, state, groups = tie(dqkv, state, groups)
-    groups = links.step(groups, 1)
+    dqkv, rate_late, state = ttt_backward(projected, dinner, rate_lanes, saved, None, gain_lanes, 4, slots // MINI, None)
+    dqkv, state = first_sum.tied(dqkv, state)
+    first_sum.fold()
+    dqkv, state = first_sum.tied(dqkv, state)
+    first_sum.send()
     dqkv, rate_early, state = ttt_backward(projected, dinner, rate_lanes, saved, state, gain_lanes, 0, 4, dqkv)
     dqkv = dqkv.reshape(rows, 3 * width)
     rate_back = jnp.concatenate([rate_early, rate_late], axis=0)
     early = weight_grads(table, normed, dqkv, devices)
-    dqkv, early, groups = tie(dqkv, list(early), groups)
-    groups = refold(groups, 2)
-    dqkv, early, groups = tie(dqkv, early, groups)
-    for phase in range(2, links.near):
-        groups = refold(groups, 2) if phase > 2 else groups
-        groups = links.step(groups, phase)
+    dqkv, early = first_sum.tied(dqkv, list(early))
+    first_sum.fold()
+    dqkv, early = first_sum.tied(dqkv, early)
+    first_sum.send()
     early = links.exchange_cores(in_order(table, tuple(early), device_rows))
     *late, dlog = last_grads(shared, normed, dqkv, sums, state, rate_back, rest_lanes, devices)
-    late, dlog, early, groups = tie(list(late), dlog, early, groups)
+    late, dlog, early = first_sum.tied(list(late), dlog, early)
     late = links.exchange_cores(in_order(shared, tuple(late), device_rows))
-    groups = refold(groups, 2)
-    late, groups = tie(late, groups)
-    groups = links.step(groups, links.near)
-    last = fold([[(*early, 0, 2 * width)], [(*late, 0, width + 2 * PAIR)]], 1, PAIR)
-    dlog, last = tie(dlog, last)
-    last = links.step(last, 0)
+    first_sum.fold()
+    late = first_sum.tied(late)
+    first_sum.send()
+    second_sum = Scatter(
+        links, [[(list(early), 0, 2 * width)], [(list(late), 0, width + 2 * PAIR)]], whole_rows, 1, PAIR
+    )
+    second_sum.fold()
+    dlog = second_sum.tied(dlog)
+    second_sum.send()
     grad_tokens = None
     for half in range(2):
         grad_tokens = finish(inputs, dfirst, dqkv, dgate, dlog, whole, vec_rows, half, grad_tokens)
-        grad_tokens, last = tie(grad_tokens, last)
-        last = links.step(refold(last, 1, PAIR), 1 + half)
-    for phase in range(3, links.near + 1):
-        last = links.step(refold(last, 1, PAIR), phase)
-    large, down = (kept + got.astype(full) for kept, got in groups)
-    early, late = (kept + got.astype(full) for kept, got in last)
+        grad_tokens = second_sum.tied(grad_tokens)
+        second_sum.fold()
+        second_sum.send()
+    early, late = second_sum.result()
+    large, down = first_sum.result()
     part = hidden // dp
-    large = large.reshape(device_rows, dp, -1)
-    both = large[:, :, : 2 * part].reshape(device_rows, dp, 2, part).transpose(0, 2, 1, 3).reshape(device_rows, 2 * hidden)
-    middle = large[:, :, 2 * part :].reshape(device_rows, 2 * width)
+    large = large.reshape(device_rows, 2, -1)
+    both = large[:, :, :hidden].reshape(device_rows, dp, 2, part).transpose(0, 2, 1, 3).reshape(device_rows, 2 * hidden)
+    middle = large[:, :, hidden:].reshape(device_rows, 2 * width)
     out_small = late[:, width : width + PAIR] + late[:, width + PAIR :]
     out_out, out_gate_in = middle[:, :width], middle[:, width:]
     out_mixer = jnp.concatenate([early, late[:, :width], out_gate_in], axis=1)

time: 326 us -> 318 us (0.975)
  Pallas kernels: 197 us -> 190 us
  waiting for transfers between devices: 45.3 us -> 48.9 us
    pallas_call x15, Pallas kernels: 128 us -> 122 us  [call(): pl.pallas_call(kernel, grid_spec=pltpu.PrefetchScalarGridSpec(num_scalar_...]
    ppermute x43, waiting for transfers between devices: 45.3 us -> 48.9 us  [swap(): return lax.ppermute(values, self.axes, pairs)]
    unnamed x97 -> x103, local copies, waits for them, and re-layouts: 13.4 us -> 12.6 us
  transfers between devices with their start and end apart: 43 -> 43, of which waited for: 14 -> 15; matrix products, arithmetic and copies ran while one was open for 5% -> 4% of each run, Pallas kernels for 41% -> 42%
where the time goes in v2:
time: 318 us; the launch traced here: 314 us
  Pallas kernels  190 us (60%)
  waiting for transfers between devices  48.9 us (15%)
  starting transfers between devices  40.5 us (13%)
  local copies, waits for them, and re-layouts  21.5 us (7%)
  other arithmetic  8.8 us (3%)
  between operations  3.29 us (1%)
    pallas_call x15, Pallas kernels, call(): pl.pallas_call(kernel, grid_spec=pltpu.PrefetchScalarGridSpec(num_scalar_...  122 us
    ppermute x43, waiting for transfers between devices, swap(): return lax.ppermute(values, self.axes, pairs)  48.9 us
    ppermute x43, starting transfers between devices, swap(): return lax.ppermute(values, self.axes, pairs)  40.5 us
    pallas_call x2, Pallas kernels, ttt_backward(): pl.pallas_call(lambda *refs: ttt_backward_kernel(steps, state is not None...  30.7 us
    pallas_call x1, Pallas kernels, ttt_forward(): pl.pallas_call(lambda *refs: ttt_forward_kernel(steps, *refs), grid=((end...  21.2 us
    pallas_call x2, Pallas kernels, finish(): pl.pallas_call(lambda *refs: finish_kernel(*refs[:9], refs[-1]), grid=(1,...  16 us
    unnamed x103, local copies, waits for them, and re-layouts  12.6 us
  transfers between devices with their start and end apart: 43, of which 15 were waited for; matrix products, arithmetic and copies ran while one was open for 4% of the time, Pallas kernels for 42%

profile of v2, /device:TPU:0, one launch (start us, length us, event | category | flops | bytes accessed | tf_op | source)
XLA Modules:
  0.0 313.8 jit_solution(515636663954486075)
XLA Ops:
  4.8 4.0 %collective-permute-start.2 = (bf16[24,1280]{1,0:T(8,128)(2,1)S(1)}, bf16[24,1280]{1,0:T(8,128)(2,1)S(1)}, u32[]{:S(2)}, u32[]{:S(2)}) collective-permute-start(bf16[24,1280]{1,0:T(8,128)(2,1)S(1)} %pad_maximum_fusion.13), channel_id=1, source_target_pairs={{0,4},{1,5},{2,6},{3,7},{4,0},{5,1},{6,2},{7,3},{8,12},{9,13},{10,... | collective-permute-start | bytes 184328 | tf_op jit(solution)/shard_map/ppermute | solution.py:1005
  14.4 4.1 %collective-permute-done = bf16[24,2688]{1,0:T(8,128)(2,1)S(1)} collective-permute-done((bf16[24,2688]{1,0:T(8,128)(2,1)S(1)}, bf16[24,2688]{1,0:T(8,128)(2,1)S(1)}, u32[]{:S(2)}, u32[]{:S(2)}) %collective-permute-start) | collective-permute-done | bytes 129056 | tf_op jit(solution)/shard_map/ppermute | solution.py:1005
  20.2 4.7 %collective-permute-done.1 = bf16[2,24,2688]{2,1,0:T(8,128)(2,1)S(1)} collective-permute-done((bf16[2,24,2688]{2,1,0:T(8,128)(2,1)S(1)}, bf16[2,24,2688]{2,1,0:T(8,128)(2,1)S(1)}, u32[]{:S(2)}, u32[]{:S(2)}) %collective-permute-start.1) | collective-permute-done | bytes 258080 | tf_op jit(solution)/shard_map/ppermute | solution.py:1005
  25.2 3.0 collective-permute-start.6
  30.2 6.7 %collective-permute-done.7 = bf16[64,768]{1,0:T(8,128)(2,1)S(1)} collective-permute-done((bf16[64,768]{1,0:T(8,128)(2,1)S(1)}, bf16[64,768]{1,0:T(8,128)(2,1)S(1)}, u32[]{:S(2)}, u32[]{:S(2)}) %collective-permute-start.7) | collective-permute-done | bytes 98336 | tf_op jit(solution)/shard_map/ppermute | solution.py:1005
  45.8 7.6 %collective-permute-done.11 = bf16[2,2,2,24,1280]{4,3,2,1,0:T(8,128)(2,1)S(1)} collective-permute-done((bf16[2,2,2,24,1280]{4,3,2,1,0:T(8,128)(2,1)S(1)}, bf16[2,2,2,24,1280]{4,3,2,1,0:T(8,128)(2,1)S(1)}, u32[]{:S(2)}, u32[]{:S(2)}) %collective-permute-start.11) | collective-permute-done | bytes 491552 | tf_op jit(solution)/shard_map/ppermute | solution.py:1005
  53.7 9.8 %collective-permute-done.8.refs_8_ = bf16[4,48,2688]{2,1,0:T(8,128)(2,1)S(1)} collective-permute-done((bf16[4,48,2688]{2,1,0:T(8,128)(2,1)S(1)}, bf16[4,48,2688]{2,1,0:T(8,128)(2,1)S(1)}, u32[]{:S(2)}, u32[]{:S(2)}) %collective-permute-start.8) | collective-permute-done | bytes 1032224 | tf_op jit(solution)/shard_map/ppermute | solution.py:1005
  67.2 14.5 %project.1 = (bf16[768,3968]{1,0:T(8,128)(2,1)}, f32[1024,2304]{1,0:T(8,128)}, bf16[1024,768]{1,0:T(8,128)(2,1)}, f32[32,1,384]{2,1,0:T(1,128)}, f32[32,384]{1,0...) custom-call(s32[2]{0:T(128)} %bitcast.218, ...), custom_call_target="tpu_custom_call" | custom-call | flops 5000000000 | bytes 10000000 | tf_op jit(solution)/shard_map/project/pallas_call | solution.py:475
  85.1 21.2 %ttt_forward.1 = (f32[2,512,768]{2,1,0:T(8,128)}, bf16[32,64,1536]{2,1,0:T(8,128)(2,1)}, f32[32,64,384]{2,1,0:T(8,128)}, f32[32,64,384]{2,1,0:T(8,128)}, f32[32,...) custom-call(f32[2,512,2304]{2,1,0:T(8,128)} %bitcast.182, ...), custom_call_target="tpu_custom_call" | custom-call | flops 44800000000 | bytes 48000000 | tf_op jit(solution)/shard_map/ttt_forward/pallas_call | solution.py:389
  108.9 8.5 %post.1 = (f32[1024,768]{1,0:T(8,128)}, bf16[1024,768]{1,0:T(8,128)(2,1)}, f32[1024,768]{1,0:T(8,128)}, bf16[1024,768]{1,0:T(8,128)(2,1)}) custom-call(f32[1024,768]{1,0:T(8,128)} %bitcast.193, bf16[1024,768]{1,0:T(8,128)(2,1)} %get-tuple-element.258.normed_ref.refs_3_.refs_1_, bf16[1024,768]{1,0:T(8,128)(2,1)} %bitcast.190, ...), custom_call_target="tpu_custom_call" | custom-call | flops 4000000000 | bytes 8000000 | tf_op jit(solution)/shard_map/post/pallas_call | solution.py:475
  118.7 43.3 %ffn.1 = (bf16[1024,768]{1,0:T(8,128)(2,1)}, f32[1024,768]{1,0:T(8,128)}, bf16[384,6144]{1,0:T(8,128)(2,1)}, bf16[384,6144]{1,0:T(8,128)(2,1)}) custom-call(s32[32]{0:T(128)} %pad_add_fusion.refs_0_, s32[32]{0:T(128)} %pad_add_fusion.1.refs_1_.refs_0_, s32[16]{0:T(128)} %pad_add_fusion.2.refs_1_.refs_2_, s32[32]{0:T(128)} %concatenate.33.refs_3_, ...), custom_call_target="tpu_custom_call" | custom-call | flops 28999999488 | bytes 58000000 | tf_op jit(solution)/shard_map/ffn/pallas_call | solution.py:475
  162.2 11.9 %post_back.1 = (f32[1024,768]{1,0:T(8,128)}, bf16[1024,768]{1,0:T(8,128)(2,1)}, f32[1024,768]{1,0:T(8,128)}, bf16[1024,768]{1,0:T(8,128)(2,1)}, f32[8,768]{1,0:T(8,128)}) custom-call(f32[1024,768]{1,0:T(8,128)} %get-tuple-element.271.dsecond_ref, f32[1024,768]{1,0:T(8,128)} %get-tuple-element.262.refs_5_.first_ref, bf16[1024,768]{1,0:T(8,128)(2,1)} %bitcast.197, ...), custom_call_target="tpu_custom_call" | custom-call | flops 4000000000 | bytes 8000000 | tf_op jit(solution)/shard_map/post_back/pallas_call | solution.py:475
  174.2 7.7 %middle_grads.1 = (bf16[384,1536]{1,0:T(8,128)(2,1)}, bf16[384,1536]{1,0:T(8,128)(2,1)}) custom-call(s32[32]{0:T(128)} %pad_add_fusion.refs_0_, bf16[1024,768]{1,0:T(8,128)(2,1)} %get-tuple-element.277.refs_1_, bf16[1024,768]{1,0:T(8,128)(2,1)} %get-tuple-element.278.refs_2_, bf16[1024,768]{1,0:T(8,128)(2,1)} %get-tuple-element.258.normed_ref.refs_3_.refs_1_, ...), custom_call_target="tpu_custom_call" | custom-call | flops 3000000000 | bytes 6000000 | tf_op jit(solution)/shard_map/middle_grads/pallas_call | solution.py:475
  186.0 4.3 %fold.8 = (bf16[192,5632]{1,0:T(8,128)(2,1)}, bf16[192,2048]{1,0:T(8,128)(2,1)}) custom-call(bf16[384,6144]{1,0:T(8,128)(2,1)} %get-tuple-element.398.refs_0_.refs_4_.refs_5_.refs_6_.refs_7_, bf16[384,6144]{1,0:T(8,128)(2,1)} %collective-permute-done.23.refs_1_.refs_5_.refs_6_.refs_7_.refs_8_, bf16[384,1536]{1,0:T(8,128)(2,1)} %get-tuple-element.393.refs_2_, ...), custom_call_target="tpu_custom_call" | custom-call | flops 100000000 | bytes 200000 | tf_op jit(solution)/shard_map/fold/pallas_call | solution.py:475
  193.0 24.3 %ttt_backward.2 = (bf16[2,512,2304]{2,1,0:T(8,128)(2,1)}, f32[28,1,384]{2,1,0:T(1,128)}, f32[64,1536]{1,0:T(8,128)}, f32[64,384]{1,0:T(8,128)}, f32[64,384]{1,0:...) custom-call(f32[2,512,2304]{2,1,0:T(8,128)} %bitcast.185, f32[2,512,2304]{2,1,0:T(8,128)} %bitcast.186, ...), custom_call_target="tpu_custom_call" | custom-call | flops 56000000000 | bytes 42000000 | tf_op jit(solution)/shard_map/ttt_backward/pallas_call | solution.py:418
  219.8 3.4 %fold.9 = (bf16[96,5632]{1,0:T(8,128)(2,1)}, bf16[96,2048]{1,0:T(8,128)(2,1)}) custom-call(bf16[384,6144]{1,0:T(8,128)(2,1)} %get-tuple-element.398.refs_0_.refs_4_.refs_5_.refs_6_.refs_7_, bf16[384,6144]{1,0:T(8,128)(2,1)} %collective-permute-done.23.refs_1_.refs_5_.refs_6_.refs_7_.refs_8_, bf16[384,1536]{1,0:T(8,128)(2,1)} %get-tuple-element.393.refs_2_, ...), custom_call_target="tpu_custom_call" | custom-call | flops 100000000 | bytes 200000 | tf_op jit(solution)/shard_map/fold/pallas_call | solution.py:475
  225.2 6.4 %ttt_backward.3 = (bf16[2,512,2304]{2,1,0:T(8,128)(2,1)}, f32[4,1,384]{2,1,0:T(1,128)}, f32[64,1536]{1,0:T(8,128)}, f32[64,384]{1,0:T(8,128)}, f32[64,384]{1,0:T...) custom-call(f32[2,512,2304]{2,1,0:T(8,128)} %bitcast.187, ...), custom_call_target="tpu_custom_call", output_to_operand_aliasing={{0}: (20, {})} | custom-call | flops 8000000000 | bytes 6000000 | tf_op jit(solution)/shard_map/ttt_backward/pallas_call | solution.py:418
  231.6 7.1 %weight_grads.1 = (bf16[384,1536]{1,0:T(8,128)(2,1)}, bf16[384,1536]{1,0:T(8,128)(2,1)}) custom-call(s32[32]{0:T(128)} %pad_add_fusion.refs_0_, bf16[1024,768]{1,0:T(8,128)(2,1)} %get-tuple-element.258.normed_ref.refs_3_.refs_1_, bf16[1024,2304]{1,0:T(8,128)(2,1)} %bitcast.178), custom_call_target="tpu_custom_call" | custom-call | flops 3000000000 | bytes 6000000 | tf_op jit(solution)/shard_map/weight_grads/pallas_call | solution.py:475
  245.7 6.3 %last_grads.1 = (bf16[384,1024]{1,0:T(8,128)(2,1)}, bf16[384,1024]{1,0:T(8,128)(2,1)}, bf16[1024,128]{1,0:T(8,128)(2,1)}) custom-call(s32[32]{0:T(128)} %pad_add_fusion.1.refs_1_.refs_0_, bf16[1024,768]{1,0:T(8,128)(2,1)} %get-tuple-element.258.normed_ref.refs_3_.refs_1_, bf16[1024,2304]{1,0:T(8,128)(2,1)} %bitcast.179, ...), custom_call_target="tpu_custom_call" | custom-call | flops 3000000000 | bytes 6000000 | tf_op jit(solution)/shard_map/last_grads/pallas_call | solution.py:475
  253.2 3.2 %fold.11 = (bf16[24,5632]{1,0:T(8,128)(2,1)}, f32[24,5632]{1,0:T(8,128)}, bf16[24,2048]{1,0:T(8,128)(2,1)}, f32[24,2048]{1,0:T(8,128)}) custom-call(bf16[384,6144]{1,0:T(8,128)(2,1)} %get-tuple-element.398.refs_0_.refs_4_.refs_5_.refs_6_.refs_7_, bf16[384,6144]{1,0:T(8,128)(2,1)} %collective-permute-done.23.refs_1_.refs_5_.refs_6_.refs_7_.refs_8_, ...), custom_call_target="tpu_custom_call" | custom-call | flops 100000000 | bytes 200000 | tf_op jit(solution)/shard_map/fold/pallas_call | solution.py:475
  262.2 3.7 %collective-permute-start.42 = (bf16[24,2048]{1,0:T(8,128)(2,1)S(1)}, bf16[24,2048]{1,0:T(8,128)(2,1)S(1)}, u32[]{:S(2)}, u32[]{:S(2)}) collective-permute-start(bf16[24,2048]{1,0:T(8,128)(2,1)S(1)} %copy-done.47), channel_id=1, source_target_pairs={{0,4},{1,5},{2,6},{3,7},{4,0},{5,1},{6,2},{7,3},{8,12},{9,13},{10,... | collective-permute-start | bytes 294920 | tf_op jit(solution)/shard_map/ppermute | solution.py:1005
  266.0 8.0 %finish.2.refs_9_ = bf16[1024,768]{1,0:T(8,128)(2,1)} custom-call(bf16[1024,768]{1,0:T(8,128)(2,1)} %bitcast.191, f32[1024,768]{1,0:T(8,128)} %get-tuple-element.273.refs_1_, bf16[1024,2304]{1,0:T(8,128)(2,1)} %bitcast.180, bf16[1024,768]{1,0:T(8,128)(2,1)} %get-tuple-element.279.refs_4_.refs_3_, bf16[1024,128]{1,0:T(8,128)(2,1)} %get-tuple-element.411.refs_4_, ...), custom_call_target="tpu_custom_call" | custom-call | flops 3000000000 | bytes 10000000 | tf_op jit(solution)/shard_map/finish/pallas_call | solution.py:972
  280.6 8.0 %finish.3 = bf16[1024,768]{1,0:T(8,128)(2,1)} custom-call(bf16[1024,768]{1,0:T(8,128)(2,1)} %bitcast.192, f32[1024,768]{1,0:T(8,128)} %get-tuple-element.273.refs_1_, bf16[1024,2304]{1,0:T(8,128)(2,1)} %bitcast.181, bf16[1024,768]{1,0:T(8,128)(2,1)} %get-tuple-element.279.refs_4_.refs_3_, ...), custom_call_target="tpu_custom_call", output_to_operand_aliasing={{}: (9, {})} | custom-call | flops 3000000000 | bytes 10000000 | tf_op jit(solution)/shard_map/finish/pallas_call | solution.py:972
  300.7 2.9 collective-permute-start.40
  (255 shorter events, 85.9 us)
Async XLA Ops:
  25.1 11.9 %collective-permute-start.7 = (bf16[64,768]{1,0:T(8,128)(2,1)S(1)}, bf16[64,768]{1,0:T(8,128)(2,1)S(1)}, u32[]{:S(2)}, u32[]{:S(2)}) collective-permute-start(bf16[64,768]{1,0:T(8,128)(2,1)S(1)} %copy-done.27), channel_id=1, source_target_pairs={{0,4},{1,5},{2,6},{3,7},{4,0},{5,1},{6,2},{7,3},{8,12},{9,13},{10,... | collective-permute-start | bytes 294920 | tf_op jit(solution)/shard_map/ppermute | solution.py:1005
  25.2 14.1 %collective-permute-start.6 = (bf16[24,4096]{1,0:T(8,128)(2,1)S(1)}, bf16[24,4096]{1,0:T(8,128)(2,1)S(1)}, u32[]{:S(2)}, u32[]{:S(2)}) collective-permute-start(bf16[24,4096]{1,0:T(8,128)(2,1)S(1)} %copy-done.22), channel_id=1, source_target_pairs={{0,4},{1,5},{2,6},{3,7},{4,0},{5,1},{6,2},{7,3},{8,12},{9,13},{10,... | collective-permute-start | bytes 589832 | tf_op jit(solution)/shard_map/ppermute | solution.py:1005
  28.2 11.2 %collective-permute-start.5 = (bf16[2,2,24,1280]{3,2,1,0:T(8,128)(2,1)S(1)}, bf16[2,2,24,1280]{3,2,1,0:T(8,128)(2,1)S(1)}, u32[]{:S(2)}, u32[]{:S(2)}) collective-permute-start(bf16[2,2,24,1280]{3,2,1,0:T(8,128)(2,1)S(1)} %pad_maximum_fusion.10), channel_id=1, source_target_pairs={{0,2},{1,3},{2,0},{3,1},{4,6},{5,7},{6,4},{7,5},{8,10},{9,11},{10,... | collective-permute-start | bytes 737288 | tf_op jit(solution)/shard_map/ppermute | solution.py:1005
  42.2 11.2 %collective-permute-start.11 = (bf16[2,2,2,24,1280]{4,3,2,1,0:T(8,128)(2,1)S(1)}, bf16[2,2,2,24,1280]{4,3,2,1,0:T(8,128)(2,1)S(1)}, u32[]{:S(2)}, u32[]{:S(2)}) collective-permute-start(bf16[2,2,2,24,1280]{4,3,2,1,0:T(8,128)(2,1)S(1)} %pad_maximum_fusion.5), channel_id=1, source_target_pairs={{0,1},{1,0},{2,3},{3,2},{4,5},{5,4},{6,7},{7,6},{8,9},{9,8},{10,11... | collective-permute-start | bytes 1474568 | tf_op jit(solution)/shard_map/ppermute | solution.py:1005
  44.9 19.6 %collective-permute-start.9 = (bf16[4,48,2688]{2,1,0:T(8,128)(2,1)S(1)}, bf16[4,48,2688]{2,1,0:T(8,128)(2,1)S(1)}, u32[]{:S(2)}, u32[]{:S(2)}) collective-permute-start(bf16[4,48,2688]{2,1,0:T(8,128)(2,1)S(1)} %bitcast.204), channel_id=1, source_target_pairs={{0,8},{1,9},{2,10},{3,11},{4,12},{5,13},{6,14},{7,15},{8,0},{9,1},... | collective-permute-start | bytes 3096584 | tf_op jit(solution)/shard_map/ppermute | solution.py:1005
  44.9 18.6 %collective-permute-start.8 = (bf16[4,48,2688]{2,1,0:T(8,128)(2,1)S(1)}, bf16[4,48,2688]{2,1,0:T(8,128)(2,1)S(1)}, u32[]{:S(2)}, u32[]{:S(2)}) collective-permute-start(bf16[4,48,2688]{2,1,0:T(8,128)(2,1)S(1)} %bitcast.205), channel_id=1, source_target_pairs={{0,2},{1,3},{2,0},{3,1},{4,6},{5,7},{6,4},{7,5},{8,24},{9,25},{10,... | collective-permute-start | bytes 3096584 | tf_op jit(solution)/shard_map/ppermute | solution.py:1005
  45.2 18.4 %collective-permute-start.13 = (bf16[2,24,4096]{2,1,0:T(8,128)(2,1)S(1)}, bf16[2,24,4096]{2,1,0:T(8,128)(2,1)S(1)}, u32[]{:S(2)}, u32[]{:S(2)}) collective-permute-start(bf16[2,24,4096]{2,1,0:T(8,128)(2,1)S(1)} %pad_maximum_fusion.6), channel_id=1, source_target_pairs={{0,1},{1,0},{2,3},{3,2},{4,5},{5,4},{6,7},{7,6},{8,10},{9,11},{10,... | collective-permute-start | bytes 1179656 | tf_op jit(solution)/shard_map/ppermute | solution.py:1005
  53.7 10.9 %collective-permute-start.12 = (bf16[8,48,1280]{2,1,0:T(8,128)(2,1)S(1)}, bf16[8,48,1280]{2,1,0:T(8,128)(2,1)S(1)}, u32[]{:S(2)}, u32[]{:S(2)}) collective-permute-start(bf16[8,48,1280]{2,1,0:T(8,128)(2,1)S(1)} %bitcast.207), channel_id=1, source_target_pairs={{0,8},{1,9},{2,10},{3,11},{4,12},{5,13},{6,14},{7,15},{8,0},{9,1},... | collective-permute-start | bytes 2949128 | tf_op jit(solution)/shard_map/ppermute | solution.py:1005
  66.2 15.5 %collective-permute-start.16 = (bf16[2,2,64,768]{3,2,1,0:T(8,128)(2,1)S(1)}, bf16[2,2,64,768]{3,2,1,0:T(8,128)(2,1)S(1)}, u32[]{:S(2)}, u32[]{:S(2)}) collective-permute-start(bf16[2,2,64,768]{3,2,1,0:T(8,128)(2,1)S(1)} %pad_maximum_fusion.7), channel_id=1, source_target_pairs={{0,2},{1,3},{2,0},{3,1},{4,6},{5,7},{6,4},{7,5},{8,10},{9,11},{10,... | collective-permute-start | bytes 1179656 | tf_op jit(solution)/shard_map/ppermute | solution.py:1005
  66.5 15.4 %collective-permute-start.15 = (bf16[2,2,24,4096]{3,2,1,0:T(8,128)(2,1)S(1)}, bf16[2,2,24,4096]{3,2,1,0:T(8,128)(2,1)S(1)}, u32[]{:S(2)}, u32[]{:S(2)}) collective-permute-start(bf16[2,2,24,4096]{3,2,1,0:T(8,128)(2,1)S(1)} %pad_maximum_fusion.2), channel_id=1, source_target_pairs={{0,16},{1,17},{2,18},{3,19},{4,20},{5,21},{6,22},{7,23},{8,9},{9,8... | collective-permute-start | bytes 2359304 | tf_op jit(solution)/shard_map/ppermute | solution.py:1005
  82.4 24.0 %collective-permute-start.20 = (bf16[8,64,768]{2,1,0:T(8,128)(2,1)S(1)}, bf16[8,64,768]{2,1,0:T(8,128)(2,1)}, u32[]{:S(2)}, u32[]{:S(2)}) collective-permute-start(bf16[8,64,768]{2,1,0:T(8,128)(2,1)S(1)} %bitcast.209), channel_id=1, source_target_pairs={{0,8},{1,9},{2,10},{3,11},{4,12},{5,13},{6,14},{7,15},{8,0},{9,1},... | collective-permute-start | bytes 2359304 | tf_op jit(solution)/shard_map/ppermute | solution.py:1005
  82.8 23.6 %collective-permute-start.19 = (bf16[8,64,768]{2,1,0:T(8,128)(2,1)S(1)}, bf16[8,64,768]{2,1,0:T(8,128)(2,1)}, u32[]{:S(2)}, u32[]{:S(2)}) collective-permute-start(bf16[8,64,768]{2,1,0:T(8,128)(2,1)S(1)} %bitcast.210), channel_id=1, source_target_pairs={{0,1},{1,0},{2,3},{3,2},{4,5},{5,4},{6,7},{7,6},{8,9},{9,8},{10,11... | collective-permute-start | bytes 2359304 | tf_op jit(solution)/shard_map/ppermute | solution.py:1005
  83.5 23.0 %collective-permute-start.18 = (bf16[4,48,4096]{2,1,0:T(8,128)(2,1)S(1)}, bf16[4,48,4096]{2,1,0:T(8,128)(2,1)S(1)}, u32[]{:S(2)}, u32[]{:S(2)}) collective-permute-start(bf16[4,48,4096]{2,1,0:T(8,128)(2,1)S(1)} %bitcast.200), channel_id=1, source_target_pairs={{0,8},{1,9},{2,10},{3,11},{4,12},{5,13},{6,14},{7,15},{8,0},{9,1},... | collective-permute-start | bytes 4718600 | tf_op jit(solution)/shard_map/ppermute | solution.py:1005
  83.5 23.0 %collective-permute-start.17 = (bf16[4,48,4096]{2,1,0:T(8,128)(2,1)S(1)}, bf16[4,48,4096]{2,1,0:T(8,128)(2,1)}, u32[]{:S(2)}, u32[]{:S(2)}) collective-permute-start(bf16[4,48,4096]{2,1,0:T(8,128)(2,1)S(1)} %bitcast.201), channel_id=1, source_target_pairs={{0,2},{1,3},{2,0},{3,1},{4,6},{5,7},{6,4},{7,5},{8,24},{9,25},{10,... | collective-permute-start | bytes 4718600 | tf_op jit(solution)/shard_map/ppermute | solution.py:1005
  106.4 11.0 %collective-permute-start.21 = (bf16[4,48,4096]{2,1,0:T(8,128)(2,1)}, bf16[4,48,4096]{2,1,0:T(8,128)(2,1)S(1)}, u32[]{:S(2)}, u32[]{:S(2)}) collective-permute-start(bf16[4,48,4096]{2,1,0:T(8,128)(2,1)} %collective-permute-done.17.refs_8_), channel_id=1, source_target_pairs={{0,8},{1,9},{2,10},{3,11},{4,12},{5,13},{6,14},{7,15},{8,0},{9,1},... | collective-permute-start | bytes 4718600 | tf_op jit(solution)/shard_map/ppermute | solution.py:1005
  162.0 23.0 %collective-permute-start.23 = (bf16[384,6144]{1,0:T(8,128)(2,1)}, bf16[384,6144]{1,0:T(8,128)(2,1)}, u32[]{:S(2)}, u32[]{:S(2)}) collective-permute-start(bf16[384,6144]{1,0:T(8,128)(2,1)} %get-tuple-element.276), channel_id=1, source_target_pairs={{0,8},{1,9},{2,10},{3,11},{4,12},{5,13},{6,14},{7,15},{8,0},{9,1},... | collective-permute-start | bytes 14155784 | tf_op jit(solution)/shard_map/ppermute | solution.py:1005
  190.2 27.1 %collective-permute-start.26 = (bf16[192,2048]{1,0:T(8,128)(2,1)}, bf16[192,2048]{1,0:T(8,128)(2,1)S(1)}, u32[]{:S(2)}, u32[]{:S(2)}) collective-permute-start(bf16[192,2048]{1,0:T(8,128)(2,1)} %get-tuple-element.305), channel_id=1, source_target_pairs={{0,16},{1,17},{2,18},{3,19},{4,20},{5,21},{6,22},{7,23},{8,24},{9,... | collective-permute-start | bytes 2359304 | tf_op jit(solution)/shard_map/ppermute | solution.py:1005
  191.5 26.9 %collective-permute-start.25 = (bf16[192,5632]{1,0:T(8,128)(2,1)}, bf16[192,5632]{1,0:T(8,128)(2,1)S(1)}, u32[]{:S(2)}, u32[]{:S(2)}) collective-permute-start(bf16[192,5632]{1,0:T(8,128)(2,1)} %get-tuple-element.304), channel_id=1, source_target_pairs={{0,1},{1,0},{2,3},{3,2},{4,5},{5,4},{6,7},{7,6},{8,10},{9,11},{10,... | collective-permute-start | bytes 6488072 | tf_op jit(solution)/shard_map/ppermute | solution.py:1005
  223.2 15.5 %collective-permute-start.27 = (bf16[96,5632]{1,0:T(8,128)(2,1)}, bf16[96,5632]{1,0:T(8,128)(2,1)S(1)}, u32[]{:S(2)}, u32[]{:S(2)}) collective-permute-start(bf16[96,5632]{1,0:T(8,128)(2,1)} %get-tuple-element.333), channel_id=1, source_target_pairs={{0,16},{1,17},{2,18},{3,19},{4,20},{5,21},{6,22},{7,23},{8,9},{9,8... | collective-permute-start | bytes 3244040 | tf_op jit(solution)/shard_map/ppermute | solution.py:1005
  224.0 14.7 %collective-permute-start.28 = (bf16[96,2048]{1,0:T(8,128)(2,1)}, bf16[96,2048]{1,0:T(8,128)(2,1)S(1)}, u32[]{:S(2)}, u32[]{:S(2)}) collective-permute-start(bf16[96,2048]{1,0:T(8,128)(2,1)} %get-tuple-element.334), channel_id=1, source_target_pairs={{0,2},{1,3},{2,0},{3,1},{4,6},{5,7},{6,4},{7,5},{8,10},{9,11},{10,... | collective-permute-start | bytes 1179656 | tf_op jit(solution)/shard_map/ppermute | solution.py:1005
  259.9 14.1 %collective-permute-start.33 = (bf16[192,1536]{1,0:T(8,128)(2,1)}, bf16[192,1536]{1,0:T(8,128)(2,1)S(1)}, u32[]{:S(2)}, u32[]{:S(2)}) collective-permute-start(bf16[192,1536]{1,0:T(8,128)(2,1)} %get-tuple-element.412), channel_id=1, source_target_pairs={{0,1},{1,0},{2,3},{3,2},{4,5},{5,4},{6,7},{7,6},{8,10},{9,11},{10,... | collective-permute-start | bytes 1769480 | tf_op jit(solution)/shard_map/ppermute | solution.py:1005
  261.5 12.5 %collective-permute-start.34 = (bf16[192,1024]{1,0:T(8,128)(2,1)}, bf16[192,1024]{1,0:T(8,128)(2,1)S(1)}, u32[]{:S(2)}, u32[]{:S(2)}) collective-permute-start(bf16[192,1024]{1,0:T(8,128)(2,1)} %get-tuple-element.413), channel_id=1, source_target_pairs={{0,16},{1,17},{2,18},{3,19},{4,20},{5,21},{6,22},{7,23},{8,24},{9,... | collective-permute-start | bytes 1179656 | tf_op jit(solution)/shard_map/ppermute | solution.py:1005
  262.2 16.4 %collective-permute-start.42 = (bf16[24,2048]{1,0:T(8,128)(2,1)S(1)}, bf16[24,2048]{1,0:T(8,128)(2,1)S(1)}, u32[]{:S(2)}, u32[]{:S(2)}) collective-permute-start(bf16[24,2048]{1,0:T(8,128)(2,1)S(1)} %copy-done.47), channel_id=1, source_target_pairs={{0,4},{1,5},{2,6},{3,7},{4,0},{5,1},{6,2},{7,3},{8,12},{9,13},{10,... | collective-permute-start | bytes 294920 | tf_op jit(solution)/shard_map/ppermute | solution.py:1005
  265.9 27.6 %collective-permute-start.41 = (bf16[24,5632]{1,0:T(8,128)(2,1)S(1)}, bf16[24,5632]{1,0:T(8,128)(2,1)S(1)}, u32[]{:S(2)}, u32[]{:S(2)}) collective-permute-start(bf16[24,5632]{1,0:T(8,128)(2,1)S(1)} %copy-done.46), channel_id=1, source_target_pairs={{0,4},{1,5},{2,6},{3,7},{4,0},{5,1},{6,2},{7,3},{8,12},{9,13},{10,... | collective-permute-start | bytes 811016 | tf_op jit(solution)/shard_map/ppermute | solution.py:1005
  (69 other events, 410.4 us)

commit v3 on v2

--- a/solution.py
+++ b/solution.py
@@ -1164,7 +1164,6 @@
     held, rest, upstream = tie(held, rest, upstream)
     rest_phases = links.gather_blocks(rest, kinds, [True, False], [False, False]) if aligned else links.gather(rest, kinds)
     held, rest = mixer_phases.send(held), next(rest_phases)
-    held, rest = tie(held, rest)
     held, rest = mixer_phases.send(held), rest_phases.send(rest)
     held = mixer_phases.send(held)
     as_blocks = lambda arrays: [([array[None]], jnp.zeros((1,), jnp.int32)) for array in arrays]

time: 318 us -> 314 us (0.987)
  waiting for transfers between devices: 48.9 us -> 44.6 us
    ppermute x43, waiting for transfers between devices: 48.9 us -> 44.6 us  [swap(): return lax.ppermute(values, self.axes, pairs)]
where the time goes in v3:
time: 314 us; the launch traced here: 310 us
  Pallas kernels  190 us (61%)
  waiting for transfers between devices  44.6 us (14%)
  starting transfers between devices  40 us (13%)
  local copies, waits for them, and re-layouts  21.7 us (7%)
  other arithmetic  8.7 us (3%)
  between operations  3.9 us (1%)
    pallas_call x15, Pallas kernels, call(): pl.pallas_call(kernel, grid_spec=pltpu.PrefetchScalarGridSpec(num_scalar_...  122 us
    ppermute x43, waiting for transfers between devices, swap(): return lax.ppermute(values, self.axes, pairs)  44.6 us
    ppermute x43, starting transfers between devices, swap(): return lax.ppermute(values, self.axes, pairs)  40 us
    pallas_call x2, Pallas kernels, ttt_backward(): pl.pallas_call(lambda *refs: ttt_backward_kernel(steps, state is not None...  30.7 us
    pallas_call x1, Pallas kernels, ttt_forward(): pl.pallas_call(lambda *refs: ttt_forward_kernel(steps, *refs), grid=((end...  21.2 us
    pallas_call x2, Pallas kernels, finish(): pl.pallas_call(lambda *refs: finish_kernel(*refs[:9], refs[-1]), grid=(1,...  16 us
    unnamed x103, local copies, waits for them, and re-layouts  12.9 us
  transfers between devices with their start and end apart: 43, of which 15 were waited for; matrix products, arithmetic and copies ran while one was open for 4% of the time, Pallas kernels for 42%

profile of v3, /device:TPU:0, one launch (start us, length us, event | category | flops | bytes accessed | tf_op | source)
XLA Modules:
  0.0 309.6 jit_solution(10611430527506619921)
XLA Ops:
  4.8 4.0 %collective-permute-start.2 = (bf16[24,1280]{1,0:T(8,128)(2,1)S(1)}, bf16[24,1280]{1,0:T(8,128)(2,1)S(1)}, u32[]{:S(2)}, u32[]{:S(2)}) collective-permute-start(bf16[24,1280]{1,0:T(8,128)(2,1)S(1)} %pad_maximum_fusion.13), channel_id=1, source_target_pairs={{0,4},{1,5},{2,6},{3,7},{4,0},{5,1},{6,2},{7,3},{8,12},{9,13},{10,... | collective-permute-start | bytes 184328 | tf_op jit(solution)/shard_map/ppermute | solution.py:1005
  20.2 4.7 %collective-permute-done.1 = bf16[2,24,2688]{2,1,0:T(8,128)(2,1)S(1)} collective-permute-done((bf16[2,24,2688]{2,1,0:T(8,128)(2,1)S(1)}, bf16[2,24,2688]{2,1,0:T(8,128)(2,1)S(1)}, u32[]{:S(2)}, u32[]{:S(2)}) %collective-permute-start.1) | collective-permute-done | bytes 258080 | tf_op jit(solution)/shard_map/ppermute | solution.py:1005
  25.7 2.9 collective-permute-start.11
  30.6 5.8 %collective-permute-done.13 = bf16[64,768]{1,0:T(8,128)(2,1)S(1)} collective-permute-done((bf16[64,768]{1,0:T(8,128)(2,1)S(1)}, bf16[64,768]{1,0:T(8,128)(2,1)S(1)}, u32[]{:S(2)}, u32[]{:S(2)}) %collective-permute-start.13) | collective-permute-done | bytes 98336 | tf_op jit(solution)/shard_map/ppermute | solution.py:1005
  42.8 14.3 %collective-permute-done.9 = bf16[2,2,2,24,1280]{4,3,2,1,0:T(8,128)(2,1)S(1)} collective-permute-done((bf16[2,2,2,24,1280]{4,3,2,1,0:T(8,128)(2,1)S(1)}, bf16[2,2,2,24,1280]{4,3,2,1,0:T(8,128)(2,1)S(1)}, u32[]{:S(2)}, u32[]{:S(2)}) %collective-permute-start.9) | collective-permute-done | bytes 491552 | tf_op jit(solution)/shard_map/ppermute | solution.py:1005
  63.8 14.5 %project.1 = (bf16[768,3968]{1,0:T(8,128)(2,1)}, f32[1024,2304]{1,0:T(8,128)}, bf16[1024,768]{1,0:T(8,128)(2,1)}, f32[32,1,384]{2,1,0:T(1,128)}, f32[32,384]{1,0...) custom-call(s32[2]{0:T(128)} %bitcast.218, ...), custom_call_target="tpu_custom_call" | custom-call | flops 5000000000 | bytes 10000000 | tf_op jit(solution)/shard_map/project/pallas_call | solution.py:475
  82.0 21.2 %ttt_forward.1 = (f32[2,512,768]{2,1,0:T(8,128)}, bf16[32,64,1536]{2,1,0:T(8,128)(2,1)}, f32[32,64,384]{2,1,0:T(8,128)}, f32[32,64,384]{2,1,0:T(8,128)}, f32[32,...) custom-call(f32[2,512,2304]{2,1,0:T(8,128)} %bitcast.182, ...), custom_call_target="tpu_custom_call" | custom-call | flops 44800000000 | bytes 48000000 | tf_op jit(solution)/shard_map/ttt_forward/pallas_call | solution.py:389
  105.7 8.5 %post.1 = (f32[1024,768]{1,0:T(8,128)}, bf16[1024,768]{1,0:T(8,128)(2,1)}, f32[1024,768]{1,0:T(8,128)}, bf16[1024,768]{1,0:T(8,128)(2,1)}) custom-call(f32[1024,768]{1,0:T(8,128)} %bitcast.193, bf16[1024,768]{1,0:T(8,128)(2,1)} %get-tuple-element.250.normed_ref.refs_3_.refs_1_, bf16[1024,768]{1,0:T(8,128)(2,1)} %bitcast.190, ...), custom_call_target="tpu_custom_call" | custom-call | flops 4000000000 | bytes 8000000 | tf_op jit(solution)/shard_map/post/pallas_call | solution.py:475
  115.8 43.2 %ffn.1 = (bf16[1024,768]{1,0:T(8,128)(2,1)}, f32[1024,768]{1,0:T(8,128)}, bf16[384,6144]{1,0:T(8,128)(2,1)}, bf16[384,6144]{1,0:T(8,128)(2,1)}) custom-call(s32[32]{0:T(128)} %pad_add_fusion.refs_0_, s32[32]{0:T(128)} %pad_add_fusion.1.refs_1_.refs_0_, s32[16]{0:T(128)} %pad_add_fusion.2.refs_1_.refs_2_, s32[32]{0:T(128)} %concatenate.33.refs_3_, ...), custom_call_target="tpu_custom_call" | custom-call | flops 28999999488 | bytes 58000000 | tf_op jit(solution)/shard_map/ffn/pallas_call | solution.py:475
  159.1 11.9 %post_back.1 = (f32[1024,768]{1,0:T(8,128)}, bf16[1024,768]{1,0:T(8,128)(2,1)}, f32[1024,768]{1,0:T(8,128)}, bf16[1024,768]{1,0:T(8,128)(2,1)}, f32[8,768]{1,0:T(8,128)}) custom-call(f32[1024,768]{1,0:T(8,128)} %get-tuple-element.263.dsecond_ref, f32[1024,768]{1,0:T(8,128)} %get-tuple-element.254.refs_5_.first_ref, bf16[1024,768]{1,0:T(8,128)(2,1)} %bitcast.197, ...), custom_call_target="tpu_custom_call" | custom-call | flops 4000000000 | bytes 8000000 | tf_op jit(solution)/shard_map/post_back/pallas_call | solution.py:475
  171.0 7.7 %middle_grads.1 = (bf16[384,1536]{1,0:T(8,128)(2,1)}, bf16[384,1536]{1,0:T(8,128)(2,1)}) custom-call(s32[32]{0:T(128)} %pad_add_fusion.refs_0_, bf16[1024,768]{1,0:T(8,128)(2,1)} %get-tuple-element.269.refs_1_, bf16[1024,768]{1,0:T(8,128)(2,1)} %get-tuple-element.270.refs_2_, bf16[1024,768]{1,0:T(8,128)(2,1)} %get-tuple-element.250.normed_ref.refs_3_.refs_1_, ...), custom_call_target="tpu_custom_call" | custom-call | flops 3000000000 | bytes 6000000 | tf_op jit(solution)/shard_map/middle_grads/pallas_call | solution.py:475
  179.2 2.7 collective-permute-done.24.refs_3_
  182.9 4.3 %fold.8 = (bf16[192,5632]{1,0:T(8,128)(2,1)}, bf16[192,2048]{1,0:T(8,128)(2,1)}) custom-call(bf16[384,6144]{1,0:T(8,128)(2,1)} %get-tuple-element.390.refs_0_.refs_4_.refs_5_.refs_6_.refs_7_, bf16[384,6144]{1,0:T(8,128)(2,1)} %collective-permute-done.23.refs_1_.refs_5_.refs_6_.refs_7_.refs_8_, bf16[384,1536]{1,0:T(8,128)(2,1)} %get-tuple-element.385.refs_2_, ...), custom_call_target="tpu_custom_call" | custom-call | flops 100000000 | bytes 200000 | tf_op jit(solution)/shard_map/fold/pallas_call | solution.py:475
  188.8 24.3 %ttt_backward.2 = (bf16[2,512,2304]{2,1,0:T(8,128)(2,1)}, f32[28,1,384]{2,1,0:T(1,128)}, f32[64,1536]{1,0:T(8,128)}, f32[64,384]{1,0:T(8,128)}, f32[64,384]{1,0:...) custom-call(f32[2,512,2304]{2,1,0:T(8,128)} %bitcast.185, f32[2,512,2304]{2,1,0:T(8,128)} %bitcast.186, ...), custom_call_target="tpu_custom_call" | custom-call | flops 56000000000 | bytes 42000000 | tf_op jit(solution)/shard_map/ttt_backward/pallas_call | solution.py:418
  216.6 3.4 %fold.9 = (bf16[96,5632]{1,0:T(8,128)(2,1)}, bf16[96,2048]{1,0:T(8,128)(2,1)}) custom-call(bf16[384,6144]{1,0:T(8,128)(2,1)} %get-tuple-element.390.refs_0_.refs_4_.refs_5_.refs_6_.refs_7_, bf16[384,6144]{1,0:T(8,128)(2,1)} %collective-permute-done.23.refs_1_.refs_5_.refs_6_.refs_7_.refs_8_, bf16[384,1536]{1,0:T(8,128)(2,1)} %get-tuple-element.385.refs_2_, ...), custom_call_target="tpu_custom_call" | custom-call | flops 100000000 | bytes 200000 | tf_op jit(solution)/shard_map/fold/pallas_call | solution.py:475
  221.9 6.4 %ttt_backward.3 = (bf16[2,512,2304]{2,1,0:T(8,128)(2,1)}, f32[4,1,384]{2,1,0:T(1,128)}, f32[64,1536]{1,0:T(8,128)}, f32[64,384]{1,0:T(8,128)}, f32[64,384]{1,0:T...) custom-call(f32[2,512,2304]{2,1,0:T(8,128)} %bitcast.187, ...), custom_call_target="tpu_custom_call", output_to_operand_aliasing={{0}: (20, {})} | custom-call | flops 8000000000 | bytes 6000000 | tf_op jit(solution)/shard_map/ttt_backward/pallas_call | solution.py:418
  228.3 7.1 %weight_grads.1 = (bf16[384,1536]{1,0:T(8,128)(2,1)}, bf16[384,1536]{1,0:T(8,128)(2,1)}) custom-call(s32[32]{0:T(128)} %pad_add_fusion.refs_0_, bf16[1024,768]{1,0:T(8,128)(2,1)} %get-tuple-element.250.normed_ref.refs_3_.refs_1_, bf16[1024,2304]{1,0:T(8,128)(2,1)} %bitcast.178), custom_call_target="tpu_custom_call" | custom-call | flops 3000000000 | bytes 6000000 | tf_op jit(solution)/shard_map/weight_grads/pallas_call | solution.py:475
  236.6 2.7 fold.10
  241.8 6.3 %last_grads.1 = (bf16[384,1024]{1,0:T(8,128)(2,1)}, bf16[384,1024]{1,0:T(8,128)(2,1)}, bf16[1024,128]{1,0:T(8,128)(2,1)}) custom-call(s32[32]{0:T(128)} %pad_add_fusion.1.refs_1_.refs_0_, bf16[1024,768]{1,0:T(8,128)(2,1)} %get-tuple-element.250.normed_ref.refs_3_.refs_1_, bf16[1024,2304]{1,0:T(8,128)(2,1)} %bitcast.179, ...), custom_call_target="tpu_custom_call" | custom-call | flops 3000000000 | bytes 6000000 | tf_op jit(solution)/shard_map/last_grads/pallas_call | solution.py:475
  249.8 3.2 %fold.11 = (bf16[24,5632]{1,0:T(8,128)(2,1)}, f32[24,5632]{1,0:T(8,128)}, bf16[24,2048]{1,0:T(8,128)(2,1)}, f32[24,2048]{1,0:T(8,128)}) custom-call(bf16[384,6144]{1,0:T(8,128)(2,1)} %get-tuple-element.390.refs_0_.refs_4_.refs_5_.refs_6_.refs_7_, bf16[384,6144]{1,0:T(8,128)(2,1)} %collective-permute-done.23.refs_1_.refs_5_.refs_6_.refs_7_.refs_8_, ...), custom_call_target="tpu_custom_call" | custom-call | flops 100000000 | bytes 200000 | tf_op jit(solution)/shard_map/fold/pallas_call | solution.py:475
  258.2 2.7 collective-permute-start.42
  261.1 8.0 %finish.2.refs_9_ = bf16[1024,768]{1,0:T(8,128)(2,1)} custom-call(bf16[1024,768]{1,0:T(8,128)(2,1)} %bitcast.191, f32[1024,768]{1,0:T(8,128)} %get-tuple-element.265.refs_1_, bf16[1024,2304]{1,0:T(8,128)(2,1)} %bitcast.180, bf16[1024,768]{1,0:T(8,128)(2,1)} %get-tuple-element.271.refs_4_.refs_3_, bf16[1024,128]{1,0:T(8,128)(2,1)} %get-tuple-element.403.refs_4_, ...), custom_call_target="tpu_custom_call" | custom-call | flops 3000000000 | bytes 10000000 | tf_op jit(solution)/shard_map/finish/pallas_call | solution.py:972
  275.7 8.0 %finish.3 = bf16[1024,768]{1,0:T(8,128)(2,1)} custom-call(bf16[1024,768]{1,0:T(8,128)(2,1)} %bitcast.192, f32[1024,768]{1,0:T(8,128)} %get-tuple-element.265.refs_1_, bf16[1024,2304]{1,0:T(8,128)(2,1)} %bitcast.181, bf16[1024,768]{1,0:T(8,128)(2,1)} %get-tuple-element.271.refs_4_.refs_3_, ...), custom_call_target="tpu_custom_call", output_to_operand_aliasing={{}: (9, {})} | custom-call | flops 3000000000 | bytes 10000000 | tf_op jit(solution)/shard_map/finish/pallas_call | solution.py:972
  304.7 3.0 collective-permute-done.39
  (255 shorter events, 84.8 us)
Async XLA Ops:
  25.1 11.4 %collective-permute-start.13 = (bf16[64,768]{1,0:T(8,128)(2,1)S(1)}, bf16[64,768]{1,0:T(8,128)(2,1)S(1)}, u32[]{:S(2)}, u32[]{:S(2)}) collective-permute-start(bf16[64,768]{1,0:T(8,128)(2,1)S(1)} %copy-done.27), channel_id=1, source_target_pairs={{0,4},{1,5},{2,6},{3,7},{4,0},{5,1},{6,2},{7,3},{8,12},{9,13},{10,... | collective-permute-start | bytes 294920 | tf_op jit(solution)/shard_map/ppermute | solution.py:1005
  25.7 14.0 %collective-permute-start.11 = (bf16[24,4096]{1,0:T(8,128)(2,1)S(1)}, bf16[24,4096]{1,0:T(8,128)(2,1)S(1)}, u32[]{:S(2)}, u32[]{:S(2)}) collective-permute-start(bf16[24,4096]{1,0:T(8,128)(2,1)S(1)} %copy-done.22), channel_id=1, source_target_pairs={{0,4},{1,5},{2,6},{3,7},{4,0},{5,1},{6,2},{7,3},{8,12},{9,13},{10,... | collective-permute-start | bytes 589832 | tf_op jit(solution)/shard_map/ppermute | solution.py:1005
  28.6 12.7 %collective-permute-start.8 = (bf16[2,2,24,1280]{3,2,1,0:T(8,128)(2,1)S(1)}, bf16[2,2,24,1280]{3,2,1,0:T(8,128)(2,1)S(1)}, u32[]{:S(2)}, u32[]{:S(2)}) collective-permute-start(bf16[2,2,24,1280]{3,2,1,0:T(8,128)(2,1)S(1)} %pad_maximum_fusion.10), channel_id=1, source_target_pairs={{0,2},{1,3},{2,0},{3,1},{4,6},{5,7},{6,4},{7,5},{8,10},{9,11},{10,... | collective-permute-start | bytes 737288 | tf_op jit(solution)/shard_map/ppermute | solution.py:1005
  29.1 13.0 %collective-permute-start.4 = (bf16[2,2,24,2688]{3,2,1,0:T(8,128)(2,1)S(1)}, bf16[2,2,24,2688]{3,2,1,0:T(8,128)(2,1)S(1)}, u32[]{:S(2)}, u32[]{:S(2)}) collective-permute-start(bf16[2,2,24,2688]{3,2,1,0:T(8,128)(2,1)S(1)} %pad_maximum_fusion.4), channel_id=1, source_target_pairs={{0,16},{1,17},{2,18},{3,19},{4,20},{5,21},{6,22},{7,23},{8,9},{9,8... | collective-permute-start | bytes 1548296 | tf_op jit(solution)/shard_map/ppermute | solution.py:1005
  39.8 18.1 %collective-permute-start.12 = (bf16[2,24,4096]{2,1,0:T(8,128)(2,1)S(1)}, bf16[2,24,4096]{2,1,0:T(8,128)(2,1)S(1)}, u32[]{:S(2)}, u32[]{:S(2)}) collective-permute-start(bf16[2,24,4096]{2,1,0:T(8,128)(2,1)S(1)} %pad_maximum_fusion.6), channel_id=1, source_target_pairs={{0,1},{1,0},{2,3},{3,2},{4,5},{5,4},{6,7},{7,6},{8,10},{9,11},{10,... | collective-permute-start | bytes 1179656 | tf_op jit(solution)/shard_map/ppermute | solution.py:1005
  41.5 15.6 %collective-permute-start.9 = (bf16[2,2,2,24,1280]{4,3,2,1,0:T(8,128)(2,1)S(1)}, bf16[2,2,2,24,1280]{4,3,2,1,0:T(8,128)(2,1)S(1)}, u32[]{:S(2)}, u32[]{:S(2)}) collective-permute-start(bf16[2,2,2,24,1280]{4,3,2,1,0:T(8,128)(2,1)S(1)} %pad_maximum_fusion.5), channel_id=1, source_target_pairs={{0,1},{1,0},{2,3},{3,2},{4,5},{5,4},{6,7},{7,6},{8,9},{9,8},{10,11... | collective-permute-start | bytes 1474568 | tf_op jit(solution)/shard_map/ppermute | solution.py:1005
  42.5 14.9 %collective-permute-start.5 = (bf16[4,48,2688]{2,1,0:T(8,128)(2,1)S(1)}, bf16[4,48,2688]{2,1,0:T(8,128)(2,1)S(1)}, u32[]{:S(2)}, u32[]{:S(2)}) collective-permute-start(bf16[4,48,2688]{2,1,0:T(8,128)(2,1)S(1)} %bitcast.204), channel_id=1, source_target_pairs={{0,2},{1,3},{2,0},{3,1},{4,6},{5,7},{6,4},{7,5},{8,24},{9,25},{10,... | collective-permute-start | bytes 3096584 | tf_op jit(solution)/shard_map/ppermute | solution.py:1005
  42.7 15.9 %collective-permute-start.6 = (bf16[4,48,2688]{2,1,0:T(8,128)(2,1)S(1)}, bf16[4,48,2688]{2,1,0:T(8,128)(2,1)S(1)}, u32[]{:S(2)}, u32[]{:S(2)}) collective-permute-start(bf16[4,48,2688]{2,1,0:T(8,128)(2,1)S(1)} %bitcast.205), channel_id=1, source_target_pairs={{0,8},{1,9},{2,10},{3,11},{4,12},{5,13},{6,14},{7,15},{8,0},{9,1},... | collective-permute-start | bytes 3096584 | tf_op jit(solution)/shard_map/ppermute | solution.py:1005
  61.4 16.9 %collective-permute-start.16 = (bf16[2,2,64,768]{3,2,1,0:T(8,128)(2,1)S(1)}, bf16[2,2,64,768]{3,2,1,0:T(8,128)(2,1)S(1)}, u32[]{:S(2)}, u32[]{:S(2)}) collective-permute-start(bf16[2,2,64,768]{3,2,1,0:T(8,128)(2,1)S(1)} %pad_maximum_fusion.7), channel_id=1, source_target_pairs={{0,2},{1,3},{2,0},{3,1},{4,6},{5,7},{6,4},{7,5},{8,10},{9,11},{10,... | collective-permute-start | bytes 1179656 | tf_op jit(solution)/shard_map/ppermute | solution.py:1005
  62.4 16.1 %collective-permute-start.15 = (bf16[2,2,24,4096]{3,2,1,0:T(8,128)(2,1)S(1)}, bf16[2,2,24,4096]{3,2,1,0:T(8,128)(2,1)S(1)}, u32[]{:S(2)}, u32[]{:S(2)}) collective-permute-start(bf16[2,2,24,4096]{3,2,1,0:T(8,128)(2,1)S(1)} %pad_maximum_fusion.2), channel_id=1, source_target_pairs={{0,16},{1,17},{2,18},{3,19},{4,20},{5,21},{6,22},{7,23},{8,9},{9,8... | collective-permute-start | bytes 2359304 | tf_op jit(solution)/shard_map/ppermute | solution.py:1005
  79.0 24.2 %collective-permute-start.20 = (bf16[8,64,768]{2,1,0:T(8,128)(2,1)S(1)}, bf16[8,64,768]{2,1,0:T(8,128)(2,1)S(1)}, u32[]{:S(2)}, u32[]{:S(2)}) collective-permute-start(bf16[8,64,768]{2,1,0:T(8,128)(2,1)S(1)} %bitcast.209), channel_id=1, source_target_pairs={{0,8},{1,9},{2,10},{3,11},{4,12},{5,13},{6,14},{7,15},{8,0},{9,1},... | collective-permute-start | bytes 2359304 | tf_op jit(solution)/shard_map/ppermute | solution.py:1005
  79.4 23.9 %collective-permute-start.19 = (bf16[8,64,768]{2,1,0:T(8,128)(2,1)S(1)}, bf16[8,64,768]{2,1,0:T(8,128)(2,1)}, u32[]{:S(2)}, u32[]{:S(2)}) collective-permute-start(bf16[8,64,768]{2,1,0:T(8,128)(2,1)S(1)} %bitcast.210), channel_id=1, source_target_pairs={{0,1},{1,0},{2,3},{3,2},{4,5},{5,4},{6,7},{7,6},{8,9},{9,8},{10,11... | collective-permute-start | bytes 2359304 | tf_op jit(solution)/shard_map/ppermute | solution.py:1005
  80.9 22.4 %collective-permute-start.18 = (bf16[4,48,4096]{2,1,0:T(8,128)(2,1)S(1)}, bf16[4,48,4096]{2,1,0:T(8,128)(2,1)}, u32[]{:S(2)}, u32[]{:S(2)}) collective-permute-start(bf16[4,48,4096]{2,1,0:T(8,128)(2,1)S(1)} %bitcast.200), channel_id=1, source_target_pairs={{0,8},{1,9},{2,10},{3,11},{4,12},{5,13},{6,14},{7,15},{8,0},{9,1},... | collective-permute-start | bytes 4718600 | tf_op jit(solution)/shard_map/ppermute | solution.py:1005
  80.9 22.4 %collective-permute-start.17 = (bf16[4,48,4096]{2,1,0:T(8,128)(2,1)S(1)}, bf16[4,48,4096]{2,1,0:T(8,128)(2,1)}, u32[]{:S(2)}, u32[]{:S(2)}) collective-permute-start(bf16[4,48,4096]{2,1,0:T(8,128)(2,1)S(1)} %bitcast.201), channel_id=1, source_target_pairs={{0,2},{1,3},{2,0},{3,1},{4,6},{5,7},{6,4},{7,5},{8,24},{9,25},{10,... | collective-permute-start | bytes 4718600 | tf_op jit(solution)/shard_map/ppermute | solution.py:1005
  103.3 11.0 %collective-permute-start.21 = (bf16[4,48,4096]{2,1,0:T(8,128)(2,1)}, bf16[4,48,4096]{2,1,0:T(8,128)(2,1)S(1)}, u32[]{:S(2)}, u32[]{:S(2)}) collective-permute-start(bf16[4,48,4096]{2,1,0:T(8,128)(2,1)} %collective-permute-done.17.refs_8_), channel_id=1, source_target_pairs={{0,8},{1,9},{2,10},{3,11},{4,12},{5,13},{6,14},{7,15},{8,0},{9,1},... | collective-permute-start | bytes 4718600 | tf_op jit(solution)/shard_map/ppermute | solution.py:1005
  159.0 22.9 %collective-permute-start.23 = (bf16[384,6144]{1,0:T(8,128)(2,1)}, bf16[384,6144]{1,0:T(8,128)(2,1)}, u32[]{:S(2)}, u32[]{:S(2)}) collective-permute-start(bf16[384,6144]{1,0:T(8,128)(2,1)} %get-tuple-element.268), channel_id=1, source_target_pairs={{0,8},{1,9},{2,10},{3,11},{4,12},{5,13},{6,14},{7,15},{8,0},{9,1},... | collective-permute-start | bytes 14155784 | tf_op jit(solution)/shard_map/ppermute | solution.py:1005
  187.2 25.9 %collective-permute-start.26 = (bf16[192,2048]{1,0:T(8,128)(2,1)}, bf16[192,2048]{1,0:T(8,128)(2,1)S(1)}, u32[]{:S(2)}, u32[]{:S(2)}) collective-permute-start(bf16[192,2048]{1,0:T(8,128)(2,1)} %get-tuple-element.297), channel_id=1, source_target_pairs={{0,16},{1,17},{2,18},{3,19},{4,20},{5,21},{6,22},{7,23},{8,24},{9,... | collective-permute-start | bytes 2359304 | tf_op jit(solution)/shard_map/ppermute | solution.py:1005
  188.3 26.9 %collective-permute-start.25 = (bf16[192,5632]{1,0:T(8,128)(2,1)}, bf16[192,5632]{1,0:T(8,128)(2,1)S(1)}, u32[]{:S(2)}, u32[]{:S(2)}) collective-permute-start(bf16[192,5632]{1,0:T(8,128)(2,1)} %get-tuple-element.296), channel_id=1, source_target_pairs={{0,1},{1,0},{2,3},{3,2},{4,5},{5,4},{6,7},{7,6},{8,10},{9,11},{10,... | collective-permute-start | bytes 6488072 | tf_op jit(solution)/shard_map/ppermute | solution.py:1005
  219.9 15.4 %collective-permute-start.27 = (bf16[96,5632]{1,0:T(8,128)(2,1)}, bf16[96,5632]{1,0:T(8,128)(2,1)S(1)}, u32[]{:S(2)}, u32[]{:S(2)}) collective-permute-start(bf16[96,5632]{1,0:T(8,128)(2,1)} %get-tuple-element.325), channel_id=1, source_target_pairs={{0,16},{1,17},{2,18},{3,19},{4,20},{5,21},{6,22},{7,23},{8,9},{9,8... | collective-permute-start | bytes 3244040 | tf_op jit(solution)/shard_map/ppermute | solution.py:1005
  221.0 14.4 %collective-permute-start.28 = (bf16[96,2048]{1,0:T(8,128)(2,1)}, bf16[96,2048]{1,0:T(8,128)(2,1)S(1)}, u32[]{:S(2)}, u32[]{:S(2)}) collective-permute-start(bf16[96,2048]{1,0:T(8,128)(2,1)} %get-tuple-element.326), channel_id=1, source_target_pairs={{0,2},{1,3},{2,0},{3,1},{4,6},{5,7},{6,4},{7,5},{8,10},{9,11},{10,... | collective-permute-start | bytes 1179656 | tf_op jit(solution)/shard_map/ppermute | solution.py:1005
  256.6 12.6 %collective-permute-start.33 = (bf16[192,1536]{1,0:T(8,128)(2,1)}, bf16[192,1536]{1,0:T(8,128)(2,1)S(1)}, u32[]{:S(2)}, u32[]{:S(2)}) collective-permute-start(bf16[192,1536]{1,0:T(8,128)(2,1)} %get-tuple-element.404), channel_id=1, source_target_pairs={{0,1},{1,0},{2,3},{3,2},{4,5},{5,4},{6,7},{7,6},{8,10},{9,11},{10,... | collective-permute-start | bytes 1769480 | tf_op jit(solution)/shard_map/ppermute | solution.py:1005
  257.1 12.0 %collective-permute-start.34 = (bf16[192,1024]{1,0:T(8,128)(2,1)}, bf16[192,1024]{1,0:T(8,128)(2,1)S(1)}, u32[]{:S(2)}, u32[]{:S(2)}) collective-permute-start(bf16[192,1024]{1,0:T(8,128)(2,1)} %get-tuple-element.405), channel_id=1, source_target_pairs={{0,16},{1,17},{2,18},{3,19},{4,20},{5,21},{6,22},{7,23},{8,24},{9,... | collective-permute-start | bytes 1179656 | tf_op jit(solution)/shard_map/ppermute | solution.py:1005
  258.2 15.6 %collective-permute-start.42 = (bf16[24,2048]{1,0:T(8,128)(2,1)S(1)}, bf16[24,2048]{1,0:T(8,128)(2,1)S(1)}, u32[]{:S(2)}, u32[]{:S(2)}) collective-permute-start(bf16[24,2048]{1,0:T(8,128)(2,1)S(1)} %copy-done.47), channel_id=1, source_target_pairs={{0,4},{1,5},{2,6},{3,7},{4,0},{5,1},{6,2},{7,3},{8,12},{9,13},{10,... | collective-permute-start | bytes 294920 | tf_op jit(solution)/shard_map/ppermute | solution.py:1005
  260.9 28.6 %collective-permute-start.41 = (bf16[24,5632]{1,0:T(8,128)(2,1)S(1)}, bf16[24,5632]{1,0:T(8,128)(2,1)S(1)}, u32[]{:S(2)}, u32[]{:S(2)}) collective-permute-start(bf16[24,5632]{1,0:T(8,128)(2,1)S(1)} %copy-done.46), channel_id=1, source_target_pairs={{0,4},{1,5},{2,6},{3,7},{4,0},{5,1},{6,2},{7,3},{8,12},{9,13},{10,... | collective-permute-start | bytes 811016 | tf_op jit(solution)/shard_map/ppermute | solution.py:1005
  (69 other events, 402.5 us)

commit v4 on v3

--- a/solution.py
+++ b/solution.py
@@ -604,11 +604,11 @@
 
 def post(inner, normed, tokens, whole, vectors):
     rows, width = tokens.shape
-    tile = rows // 4
+    tile = rows // 2
     row = pl.BlockSpec((tile, width), lambda at: (at, 0))
     shape = jax.ShapeDtypeStruct
     return call(
-        post_kernel, "post", (4,), 0,
+        post_kernel, "post", (2,), 0,
         [row, row, row, constant_spec(width, width, at=3, buffers=1), constant_spec(width, width, at=4, buffers=1), constant_spec(8, width)],
         [row] * 4, [shape((rows, width), kind) for kind in (full, low, full, low)], [], 4_000_000_000,
         (inner, normed, tokens, whole, whole, vectors),
@@ -1146,7 +1146,7 @@
     vectors = jnp.stack([inner_b, ttt_gain, ttt_shift, norm_one, post_gain, post_shift, norm_two])
     vectors = dot_tn(vectors, jnp.eye(7, PAIR, VECTORS, dtype=low)).astype(low)
     small = jnp.concatenate([inner_w, w_eta, zeros(PAIR - ETA - heads)], axis=1) + vectors
-    cut = 21 * PAIR
+    cut = 22 * PAIR
     pieces = [mixer_in[:, :cut], jnp.concatenate([mixer_in[:, cut:], w_out, small], axis=1)]
     rest = [w_gate_up, w_down]
     kinds = ["split", "shared"]

time: 314 us -> 312 us (level)
    unnamed x103 -> x101, local copies, waits for them, and re-layouts: 12.9 us -> 13 us
  transfers between devices with their start and end apart: 43 -> 43, of which waited for: 15 -> 15; matrix products, arithmetic and copies ran while one was open for 4% -> 5% of each run, Pallas kernels for 42% -> 42%
where the time goes in v4:
time: 312 us; the launch traced here: 308 us
  Pallas kernels  189 us (61%)
  waiting for transfers between devices  44.2 us (14%)
  starting transfers between devices  39.6 us (13%)
  local copies, waits for them, and re-layouts  21.8 us (7%)
  other arithmetic  9.44 us (3%)
    pallas_call x15, Pallas kernels, call(): pl.pallas_call(kernel, grid_spec=pltpu.PrefetchScalarGridSpec(num_scalar_...  121 us
    ppermute x43, waiting for transfers between devices, swap(): return lax.ppermute(values, self.axes, pairs)  44.2 us
    ppermute x43, starting transfers between devices, swap(): return lax.ppermute(values, self.axes, pairs)  39.6 us
    pallas_call x2, Pallas kernels, ttt_backward(): pl.pallas_call(lambda *refs: ttt_backward_kernel(steps, state is not None...  30.7 us
    pallas_call x1, Pallas kernels, ttt_forward(): pl.pallas_call(lambda *refs: ttt_forward_kernel(steps, *refs), grid=((end...  21.3 us
    pallas_call x2, Pallas kernels, finish(): pl.pallas_call(lambda *refs: finish_kernel(*refs[:9], refs[-1]), grid=(1,...  16 us
    unnamed x101, local copies, waits for them, and re-layouts  13 us
  transfers between devices with their start and end apart: 43, of which 15 were waited for; matrix products, arithmetic and copies ran while one was open for 5% of the time, Pallas kernels for 42%

profile of v4, /device:TPU:0, one launch (start us, length us, event | category | flops | bytes accessed | tf_op | source)
XLA Modules:
  0.0 307.8 jit_solution(15340387405277716466)
XLA Ops:
  4.8 4.0 %collective-permute-start.2 = (bf16[24,1152]{1,0:T(8,128)(2,1)S(1)}, bf16[24,1152]{1,0:T(8,128)(2,1)S(1)}, u32[]{:S(2)}, u32[]{:S(2)}) collective-permute-start(bf16[24,1152]{1,0:T(8,128)(2,1)S(1)} %pad_maximum_fusion.13), channel_id=1, source_target_pairs={{0,4},{1,5},{2,6},{3,7},{4,0},{5,1},{6,2},{7,3},{8,12},{9,13},{10,... | collective-permute-start | bytes 165896 | tf_op jit(solution)/shard_map/ppermute | solution.py:1005
  20.4 4.9 %collective-permute-done.1 = bf16[2,24,2816]{2,1,0:T(8,128)(2,1)S(1)} collective-permute-done((bf16[2,24,2816]{2,1,0:T(8,128)(2,1)S(1)}, bf16[2,24,2816]{2,1,0:T(8,128)(2,1)S(1)}, u32[]{:S(2)}, u32[]{:S(2)}) %collective-permute-start.1) | collective-permute-done | bytes 270368 | tf_op jit(solution)/shard_map/ppermute | solution.py:1005
  26.1 2.9 collective-permute-start.11
  30.7 5.9 %collective-permute-done.13 = bf16[64,768]{1,0:T(8,128)(2,1)S(1)} collective-permute-done((bf16[64,768]{1,0:T(8,128)(2,1)S(1)}, bf16[64,768]{1,0:T(8,128)(2,1)S(1)}, u32[]{:S(2)}, u32[]{:S(2)}) %collective-permute-start.13) | collective-permute-done | bytes 98336 | tf_op jit(solution)/shard_map/ppermute | solution.py:1005
  43.1 12.9 %collective-permute-done.9 = bf16[2,2,2,24,1152]{4,3,2,1,0:T(8,128)(2,1)S(1)} collective-permute-done((bf16[2,2,2,24,1152]{4,3,2,1,0:T(8,128)(2,1)S(1)}, bf16[2,2,2,24,1152]{4,3,2,1,0:T(8,128)(2,1)S(1)}, u32[]{:S(2)}, u32[]{:S(2)}) %collective-permute-start.9) | collective-permute-done | bytes 442400 | tf_op jit(solution)/shard_map/ppermute | solution.py:1005
  62.8 14.2 %project.1 = (bf16[768,3968]{1,0:T(8,128)(2,1)}, f32[1024,2304]{1,0:T(8,128)}, bf16[1024,768]{1,0:T(8,128)(2,1)}, f32[32,1,384]{2,1,0:T(1,128)}, f32[32,384]{1,0...) custom-call(s32[2]{0:T(128)} %bitcast.219, ...), custom_call_target="tpu_custom_call" | custom-call | flops 5000000000 | bytes 10000000 | tf_op jit(solution)/shard_map/project/pallas_call | solution.py:475
  80.6 21.3 %ttt_forward.1 = (f32[2,512,768]{2,1,0:T(8,128)}, bf16[32,64,1536]{2,1,0:T(8,128)(2,1)}, f32[32,64,384]{2,1,0:T(8,128)}, f32[32,64,384]{2,1,0:T(8,128)}, f32[32,...) custom-call(f32[2,512,2304]{2,1,0:T(8,128)} %bitcast.182, ...), custom_call_target="tpu_custom_call" | custom-call | flops 44800000000 | bytes 48000000 | tf_op jit(solution)/shard_map/ttt_forward/pallas_call | solution.py:389
  104.4 8.0 %post.1 = (f32[1024,768]{1,0:T(8,128)}, bf16[1024,768]{1,0:T(8,128)(2,1)}, f32[1024,768]{1,0:T(8,128)}, bf16[1024,768]{1,0:T(8,128)(2,1)}) custom-call(f32[1024,768]{1,0:T(8,128)} %bitcast.193, bf16[1024,768]{1,0:T(8,128)(2,1)} %get-tuple-element.250.normed_ref.refs_3_.refs_1_, bf16[1024,768]{1,0:T(8,128)(2,1)} %bitcast.190, ...), custom_call_target="tpu_custom_call" | custom-call | flops 4000000000 | bytes 8000000 | tf_op jit(solution)/shard_map/post/pallas_call | solution.py:475
  113.6 43.4 %ffn.1 = (bf16[1024,768]{1,0:T(8,128)(2,1)}, f32[1024,768]{1,0:T(8,128)}, bf16[384,6144]{1,0:T(8,128)(2,1)}, bf16[384,6144]{1,0:T(8,128)(2,1)}) custom-call(s32[32]{0:T(128)} %pad_add_fusion.refs_0_, s32[32]{0:T(128)} %pad_add_fusion.1.refs_1_.refs_0_, s32[16]{0:T(128)} %pad_add_fusion.2.refs_1_.refs_2_, s32[32]{0:T(128)} %concatenate.33.refs_3_, ...), custom_call_target="tpu_custom_call" | custom-call | flops 28999999488 | bytes 58000000 | tf_op jit(solution)/shard_map/ffn/pallas_call | solution.py:475
  157.2 11.9 %post_back.1 = (f32[1024,768]{1,0:T(8,128)}, bf16[1024,768]{1,0:T(8,128)(2,1)}, f32[1024,768]{1,0:T(8,128)}, bf16[1024,768]{1,0:T(8,128)(2,1)}, f32[8,768]{1,0:T(8,128)}) custom-call(f32[1024,768]{1,0:T(8,128)} %get-tuple-element.263.dsecond_ref, f32[1024,768]{1,0:T(8,128)} %get-tuple-element.254.refs_5_.first_ref, bf16[1024,768]{1,0:T(8,128)(2,1)} %bitcast.197, ...), custom_call_target="tpu_custom_call" | custom-call | flops 4000000000 | bytes 8000000 | tf_op jit(solution)/shard_map/post_back/pallas_call | solution.py:475
  169.1 7.8 %middle_grads.1 = (bf16[384,1536]{1,0:T(8,128)(2,1)}, bf16[384,1536]{1,0:T(8,128)(2,1)}) custom-call(s32[32]{0:T(128)} %pad_add_fusion.refs_0_, bf16[1024,768]{1,0:T(8,128)(2,1)} %get-tuple-element.269.refs_1_, bf16[1024,768]{1,0:T(8,128)(2,1)} %get-tuple-element.270.refs_2_, bf16[1024,768]{1,0:T(8,128)(2,1)} %get-tuple-element.250.normed_ref.refs_3_.refs_1_, ...), custom_call_target="tpu_custom_call" | custom-call | flops 3000000000 | bytes 6000000 | tf_op jit(solution)/shard_map/middle_grads/pallas_call | solution.py:475
  181.0 4.5 %fold.8 = (bf16[192,5632]{1,0:T(8,128)(2,1)}, bf16[192,2048]{1,0:T(8,128)(2,1)}) custom-call(bf16[384,6144]{1,0:T(8,128)(2,1)} %get-tuple-element.390.refs_0_.refs_4_.refs_5_.refs_6_.refs_7_, bf16[384,6144]{1,0:T(8,128)(2,1)} %collective-permute-done.23.refs_1_.refs_5_.refs_6_.refs_7_.refs_8_, bf16[384,1536]{1,0:T(8,128)(2,1)} %get-tuple-element.385.refs_2_, ...), custom_call_target="tpu_custom_call" | custom-call | flops 100000000 | bytes 200000 | tf_op jit(solution)/shard_map/fold/pallas_call | solution.py:475
  187.1 24.3 %ttt_backward.2 = (bf16[2,512,2304]{2,1,0:T(8,128)(2,1)}, f32[28,1,384]{2,1,0:T(1,128)}, f32[64,1536]{1,0:T(8,128)}, f32[64,384]{1,0:T(8,128)}, f32[64,384]{1,0:...) custom-call(f32[2,512,2304]{2,1,0:T(8,128)} %bitcast.185, f32[2,512,2304]{2,1,0:T(8,128)} %bitcast.186, ...), custom_call_target="tpu_custom_call" | custom-call | flops 56000000000 | bytes 42000000 | tf_op jit(solution)/shard_map/ttt_backward/pallas_call | solution.py:418
  214.9 3.3 %fold.9 = (bf16[96,5632]{1,0:T(8,128)(2,1)}, bf16[96,2048]{1,0:T(8,128)(2,1)}) custom-call(bf16[384,6144]{1,0:T(8,128)(2,1)} %get-tuple-element.390.refs_0_.refs_4_.refs_5_.refs_6_.refs_7_, bf16[384,6144]{1,0:T(8,128)(2,1)} %collective-permute-done.23.refs_1_.refs_5_.refs_6_.refs_7_.refs_8_, bf16[384,1536]{1,0:T(8,128)(2,1)} %get-tuple-element.385.refs_2_, ...), custom_call_target="tpu_custom_call" | custom-call | flops 100000000 | bytes 200000 | tf_op jit(solution)/shard_map/fold/pallas_call | solution.py:475
  220.2 6.4 %ttt_backward.3 = (bf16[2,512,2304]{2,1,0:T(8,128)(2,1)}, f32[4,1,384]{2,1,0:T(1,128)}, f32[64,1536]{1,0:T(8,128)}, f32[64,384]{1,0:T(8,128)}, f32[64,384]{1,0:T...) custom-call(f32[2,512,2304]{2,1,0:T(8,128)} %bitcast.187, ...), custom_call_target="tpu_custom_call", output_to_operand_aliasing={{0}: (20, {})} | custom-call | flops 8000000000 | bytes 6000000 | tf_op jit(solution)/shard_map/ttt_backward/pallas_call | solution.py:418
  226.6 7.0 %weight_grads.1 = (bf16[384,1536]{1,0:T(8,128)(2,1)}, bf16[384,1536]{1,0:T(8,128)(2,1)}) custom-call(s32[32]{0:T(128)} %pad_add_fusion.refs_0_, bf16[1024,768]{1,0:T(8,128)(2,1)} %get-tuple-element.250.normed_ref.refs_3_.refs_1_, bf16[1024,2304]{1,0:T(8,128)(2,1)} %bitcast.178), custom_call_target="tpu_custom_call" | custom-call | flops 3000000000 | bytes 6000000 | tf_op jit(solution)/shard_map/weight_grads/pallas_call | solution.py:475
  234.8 2.8 fold.10
  240.1 6.3 %last_grads.1 = (bf16[384,1024]{1,0:T(8,128)(2,1)}, bf16[384,1024]{1,0:T(8,128)(2,1)}, bf16[1024,128]{1,0:T(8,128)(2,1)}) custom-call(s32[32]{0:T(128)} %pad_add_fusion.1.refs_1_.refs_0_, bf16[1024,768]{1,0:T(8,128)(2,1)} %get-tuple-element.250.normed_ref.refs_3_.refs_1_, bf16[1024,2304]{1,0:T(8,128)(2,1)} %bitcast.179, ...), custom_call_target="tpu_custom_call" | custom-call | flops 3000000000 | bytes 6000000 | tf_op jit(solution)/shard_map/last_grads/pallas_call | solution.py:475
  248.1 3.2 %fold.11 = (bf16[24,5632]{1,0:T(8,128)(2,1)}, f32[24,5632]{1,0:T(8,128)}, bf16[24,2048]{1,0:T(8,128)(2,1)}, f32[24,2048]{1,0:T(8,128)}) custom-call(bf16[384,6144]{1,0:T(8,128)(2,1)} %get-tuple-element.390.refs_0_.refs_4_.refs_5_.refs_6_.refs_7_, bf16[384,6144]{1,0:T(8,128)(2,1)} %collective-permute-done.23.refs_1_.refs_5_.refs_6_.refs_7_.refs_8_, ...), custom_call_target="tpu_custom_call" | custom-call | flops 100000000 | bytes 200000 | tf_op jit(solution)/shard_map/fold/pallas_call | solution.py:475
  256.5 2.8 collective-permute-start.42
  259.4 8.0 %finish.2.refs_9_ = bf16[1024,768]{1,0:T(8,128)(2,1)} custom-call(bf16[1024,768]{1,0:T(8,128)(2,1)} %bitcast.191, f32[1024,768]{1,0:T(8,128)} %get-tuple-element.265.refs_1_, bf16[1024,2304]{1,0:T(8,128)(2,1)} %bitcast.180, bf16[1024,768]{1,0:T(8,128)(2,1)} %get-tuple-element.271.refs_4_.refs_3_, bf16[1024,128]{1,0:T(8,128)(2,1)} %get-tuple-element.403.refs_4_, ...), custom_call_target="tpu_custom_call" | custom-call | flops 3000000000 | bytes 10000000 | tf_op jit(solution)/shard_map/finish/pallas_call | solution.py:972
  274.0 8.0 %finish.3 = bf16[1024,768]{1,0:T(8,128)(2,1)} custom-call(bf16[1024,768]{1,0:T(8,128)(2,1)} %bitcast.192, f32[1024,768]{1,0:T(8,128)} %get-tuple-element.265.refs_1_, bf16[1024,2304]{1,0:T(8,128)(2,1)} %bitcast.181, bf16[1024,768]{1,0:T(8,128)(2,1)} %get-tuple-element.271.refs_4_.refs_3_, ...), custom_call_target="tpu_custom_call", output_to_operand_aliasing={{}: (9, {})} | custom-call | flops 3000000000 | bytes 10000000 | tf_op jit(solution)/shard_map/finish/pallas_call | solution.py:972
  295.0 2.8 collective-permute-start.40
  302.6 3.6 %collective-permute-done.39 = bf16[24,1536]{1,0:T(8,128)(2,1)S(1)} collective-permute-done((bf16[24,1536]{1,0:T(8,128)(2,1)S(1)}, bf16[24,1536]{1,0:T(8,128)(2,1)S(1)}, u32[]{:S(2)}, u32[]{:S(2)}) %collective-permute-start.39) | collective-permute-done | bytes 73760 | tf_op jit(solution)/shard_map/ppermute | solution.py:1005
  (253 shorter events, 85.0 us)
Async XLA Ops:
  25.4 11.2 %collective-permute-start.13 = (bf16[64,768]{1,0:T(8,128)(2,1)S(1)}, bf16[64,768]{1,0:T(8,128)(2,1)S(1)}, u32[]{:S(2)}, u32[]{:S(2)}) collective-permute-start(bf16[64,768]{1,0:T(8,128)(2,1)S(1)} %copy-done.27), channel_id=1, source_target_pairs={{0,4},{1,5},{2,6},{3,7},{4,0},{5,1},{6,2},{7,3},{8,12},{9,13},{10,... | collective-permute-start | bytes 294920 | tf_op jit(solution)/shard_map/ppermute | solution.py:1005
  26.1 13.7 %collective-permute-start.11 = (bf16[24,4096]{1,0:T(8,128)(2,1)S(1)}, bf16[24,4096]{1,0:T(8,128)(2,1)S(1)}, u32[]{:S(2)}, u32[]{:S(2)}) collective-permute-start(bf16[24,4096]{1,0:T(8,128)(2,1)S(1)} %copy-done.22), channel_id=1, source_target_pairs={{0,4},{1,5},{2,6},{3,7},{4,0},{5,1},{6,2},{7,3},{8,12},{9,13},{10,... | collective-permute-start | bytes 589832 | tf_op jit(solution)/shard_map/ppermute | solution.py:1005
  29.0 12.4 %collective-permute-start.8 = (bf16[2,2,24,1152]{3,2,1,0:T(8,128)(2,1)S(1)}, bf16[2,2,24,1152]{3,2,1,0:T(8,128)(2,1)S(1)}, u32[]{:S(2)}, u32[]{:S(2)}) collective-permute-start(bf16[2,2,24,1152]{3,2,1,0:T(8,128)(2,1)S(1)} %pad_maximum_fusion.10), channel_id=1, source_target_pairs={{0,2},{1,3},{2,0},{3,1},{4,6},{5,7},{6,4},{7,5},{8,10},{9,11},{10,... | collective-permute-start | bytes 663560 | tf_op jit(solution)/shard_map/ppermute | solution.py:1005
  29.2 12.9 %collective-permute-start.4 = (bf16[2,2,24,2816]{3,2,1,0:T(8,128)(2,1)S(1)}, bf16[2,2,24,2816]{3,2,1,0:T(8,128)(2,1)S(1)}, u32[]{:S(2)}, u32[]{:S(2)}) collective-permute-start(bf16[2,2,24,2816]{3,2,1,0:T(8,128)(2,1)S(1)} %pad_maximum_fusion.4), channel_id=1, source_target_pairs={{0,16},{1,17},{2,18},{3,19},{4,20},{5,21},{6,22},{7,23},{8,9},{9,8... | collective-permute-start | bytes 1622024 | tf_op jit(solution)/shard_map/ppermute | solution.py:1005
  39.8 17.9 %collective-permute-start.12 = (bf16[2,24,4096]{2,1,0:T(8,128)(2,1)S(1)}, bf16[2,24,4096]{2,1,0:T(8,128)(2,1)S(1)}, u32[]{:S(2)}, u32[]{:S(2)}) collective-permute-start(bf16[2,24,4096]{2,1,0:T(8,128)(2,1)S(1)} %pad_maximum_fusion.6), channel_id=1, source_target_pairs={{0,1},{1,0},{2,3},{3,2},{4,5},{5,4},{6,7},{7,6},{8,10},{9,11},{10,... | collective-permute-start | bytes 1179656 | tf_op jit(solution)/shard_map/ppermute | solution.py:1005
  41.5 14.5 %collective-permute-start.9 = (bf16[2,2,2,24,1152]{4,3,2,1,0:T(8,128)(2,1)S(1)}, bf16[2,2,2,24,1152]{4,3,2,1,0:T(8,128)(2,1)S(1)}, u32[]{:S(2)}, u32[]{:S(2)}) collective-permute-start(bf16[2,2,2,24,1152]{4,3,2,1,0:T(8,128)(2,1)S(1)} %pad_maximum_fusion.5), channel_id=1, source_target_pairs={{0,1},{1,0},{2,3},{3,2},{4,5},{5,4},{6,7},{7,6},{8,9},{9,8},{10,11... | collective-permute-start | bytes 1327112 | tf_op jit(solution)/shard_map/ppermute | solution.py:1005
  42.5 15.2 %collective-permute-start.5 = (bf16[4,48,2816]{2,1,0:T(8,128)(2,1)S(1)}, bf16[4,48,2816]{2,1,0:T(8,128)(2,1)S(1)}, u32[]{:S(2)}, u32[]{:S(2)}) collective-permute-start(bf16[4,48,2816]{2,1,0:T(8,128)(2,1)S(1)} %bitcast.204), channel_id=1, source_target_pairs={{0,2},{1,3},{2,0},{3,1},{4,6},{5,7},{6,4},{7,5},{8,24},{9,25},{10,... | collective-permute-start | bytes 3244040 | tf_op jit(solution)/shard_map/ppermute | solution.py:1005
  43.0 15.8 %collective-permute-start.6 = (bf16[4,48,2816]{2,1,0:T(8,128)(2,1)S(1)}, bf16[4,48,2816]{2,1,0:T(8,128)(2,1)S(1)}, u32[]{:S(2)}, u32[]{:S(2)}) collective-permute-start(bf16[4,48,2816]{2,1,0:T(8,128)(2,1)S(1)} %bitcast.205), channel_id=1, source_target_pairs={{0,8},{1,9},{2,10},{3,11},{4,12},{5,13},{6,14},{7,15},{8,0},{9,1},... | collective-permute-start | bytes 3244040 | tf_op jit(solution)/shard_map/ppermute | solution.py:1005
  60.4 16.6 %collective-permute-start.16 = (bf16[2,2,64,768]{3,2,1,0:T(8,128)(2,1)S(1)}, bf16[2,2,64,768]{3,2,1,0:T(8,128)(2,1)S(1)}, u32[]{:S(2)}, u32[]{:S(2)}) collective-permute-start(bf16[2,2,64,768]{3,2,1,0:T(8,128)(2,1)S(1)} %pad_maximum_fusion.7), channel_id=1, source_target_pairs={{0,2},{1,3},{2,0},{3,1},{4,6},{5,7},{6,4},{7,5},{8,10},{9,11},{10,... | collective-permute-start | bytes 1179656 | tf_op jit(solution)/shard_map/ppermute | solution.py:1005
  61.4 15.8 %collective-permute-start.15 = (bf16[2,2,24,4096]{3,2,1,0:T(8,128)(2,1)S(1)}, bf16[2,2,24,4096]{3,2,1,0:T(8,128)(2,1)S(1)}, u32[]{:S(2)}, u32[]{:S(2)}) collective-permute-start(bf16[2,2,24,4096]{3,2,1,0:T(8,128)(2,1)S(1)} %pad_maximum_fusion.2), channel_id=1, source_target_pairs={{0,16},{1,17},{2,18},{3,19},{4,20},{5,21},{6,22},{7,23},{8,9},{9,8... | collective-permute-start | bytes 2359304 | tf_op jit(solution)/shard_map/ppermute | solution.py:1005
  77.7 24.2 %collective-permute-start.20 = (bf16[8,64,768]{2,1,0:T(8,128)(2,1)S(1)}, bf16[8,64,768]{2,1,0:T(8,128)(2,1)S(1)}, u32[]{:S(2)}, u32[]{:S(2)}) collective-permute-start(bf16[8,64,768]{2,1,0:T(8,128)(2,1)S(1)} %bitcast.209), channel_id=1, source_target_pairs={{0,8},{1,9},{2,10},{3,11},{4,12},{5,13},{6,14},{7,15},{8,0},{9,1},... | collective-permute-start | bytes 2359304 | tf_op jit(solution)/shard_map/ppermute | solution.py:1005
  78.0 23.9 %collective-permute-start.19 = (bf16[8,64,768]{2,1,0:T(8,128)(2,1)S(1)}, bf16[8,64,768]{2,1,0:T(8,128)(2,1)}, u32[]{:S(2)}, u32[]{:S(2)}) collective-permute-start(bf16[8,64,768]{2,1,0:T(8,128)(2,1)S(1)} %bitcast.210), channel_id=1, source_target_pairs={{0,1},{1,0},{2,3},{3,2},{4,5},{5,4},{6,7},{7,6},{8,9},{9,8},{10,11... | collective-permute-start | bytes 2359304 | tf_op jit(solution)/shard_map/ppermute | solution.py:1005
  79.6 22.4 %collective-permute-start.18 = (bf16[4,48,4096]{2,1,0:T(8,128)(2,1)S(1)}, bf16[4,48,4096]{2,1,0:T(8,128)(2,1)}, u32[]{:S(2)}, u32[]{:S(2)}) collective-permute-start(bf16[4,48,4096]{2,1,0:T(8,128)(2,1)S(1)} %bitcast.200), channel_id=1, source_target_pairs={{0,8},{1,9},{2,10},{3,11},{4,12},{5,13},{6,14},{7,15},{8,0},{9,1},... | collective-permute-start | bytes 4718600 | tf_op jit(solution)/shard_map/ppermute | solution.py:1005
  79.6 22.4 %collective-permute-start.17 = (bf16[4,48,4096]{2,1,0:T(8,128)(2,1)S(1)}, bf16[4,48,4096]{2,1,0:T(8,128)(2,1)}, u32[]{:S(2)}, u32[]{:S(2)}) collective-permute-start(bf16[4,48,4096]{2,1,0:T(8,128)(2,1)S(1)} %bitcast.201), channel_id=1, source_target_pairs={{0,2},{1,3},{2,0},{3,1},{4,6},{5,7},{6,4},{7,5},{8,24},{9,25},{10,... | collective-permute-start | bytes 4718600 | tf_op jit(solution)/shard_map/ppermute | solution.py:1005
  157.0 23.0 %collective-permute-start.23 = (bf16[384,6144]{1,0:T(8,128)(2,1)}, bf16[384,6144]{1,0:T(8,128)(2,1)}, u32[]{:S(2)}, u32[]{:S(2)}) collective-permute-start(bf16[384,6144]{1,0:T(8,128)(2,1)} %get-tuple-element.268), channel_id=1, source_target_pairs={{0,8},{1,9},{2,10},{3,11},{4,12},{5,13},{6,14},{7,15},{8,0},{9,1},... | collective-permute-start | bytes 14155784 | tf_op jit(solution)/shard_map/ppermute | solution.py:1005
  185.5 25.9 %collective-permute-start.26 = (bf16[192,2048]{1,0:T(8,128)(2,1)}, bf16[192,2048]{1,0:T(8,128)(2,1)S(1)}, u32[]{:S(2)}, u32[]{:S(2)}) collective-permute-start(bf16[192,2048]{1,0:T(8,128)(2,1)} %get-tuple-element.297), channel_id=1, source_target_pairs={{0,16},{1,17},{2,18},{3,19},{4,20},{5,21},{6,22},{7,23},{8,24},{9,... | collective-permute-start | bytes 2359304 | tf_op jit(solution)/shard_map/ppermute | solution.py:1005
  186.6 26.9 %collective-permute-start.25 = (bf16[192,5632]{1,0:T(8,128)(2,1)}, bf16[192,5632]{1,0:T(8,128)(2,1)S(1)}, u32[]{:S(2)}, u32[]{:S(2)}) collective-permute-start(bf16[192,5632]{1,0:T(8,128)(2,1)} %get-tuple-element.296), channel_id=1, source_target_pairs={{0,1},{1,0},{2,3},{3,2},{4,5},{5,4},{6,7},{7,6},{8,10},{9,11},{10,... | collective-permute-start | bytes 6488072 | tf_op jit(solution)/shard_map/ppermute | solution.py:1005
  218.2 15.4 %collective-permute-start.27 = (bf16[96,5632]{1,0:T(8,128)(2,1)}, bf16[96,5632]{1,0:T(8,128)(2,1)S(1)}, u32[]{:S(2)}, u32[]{:S(2)}) collective-permute-start(bf16[96,5632]{1,0:T(8,128)(2,1)} %get-tuple-element.325), channel_id=1, source_target_pairs={{0,16},{1,17},{2,18},{3,19},{4,20},{5,21},{6,22},{7,23},{8,9},{9,8... | collective-permute-start | bytes 3244040 | tf_op jit(solution)/shard_map/ppermute | solution.py:1005
  219.2 14.4 %collective-permute-start.28 = (bf16[96,2048]{1,0:T(8,128)(2,1)}, bf16[96,2048]{1,0:T(8,128)(2,1)S(1)}, u32[]{:S(2)}, u32[]{:S(2)}) collective-permute-start(bf16[96,2048]{1,0:T(8,128)(2,1)} %get-tuple-element.326), channel_id=1, source_target_pairs={{0,2},{1,3},{2,0},{3,1},{4,6},{5,7},{6,4},{7,5},{8,10},{9,11},{10,... | collective-permute-start | bytes 1179656 | tf_op jit(solution)/shard_map/ppermute | solution.py:1005
  254.8 12.6 %collective-permute-start.33 = (bf16[192,1536]{1,0:T(8,128)(2,1)}, bf16[192,1536]{1,0:T(8,128)(2,1)S(1)}, u32[]{:S(2)}, u32[]{:S(2)}) collective-permute-start(bf16[192,1536]{1,0:T(8,128)(2,1)} %get-tuple-element.404), channel_id=1, source_target_pairs={{0,1},{1,0},{2,3},{3,2},{4,5},{5,4},{6,7},{7,6},{8,10},{9,11},{10,... | collective-permute-start | bytes 1769480 | tf_op jit(solution)/shard_map/ppermute | solution.py:1005
  255.3 12.1 %collective-permute-start.34 = (bf16[192,1024]{1,0:T(8,128)(2,1)}, bf16[192,1024]{1,0:T(8,128)(2,1)S(1)}, u32[]{:S(2)}, u32[]{:S(2)}) collective-permute-start(bf16[192,1024]{1,0:T(8,128)(2,1)} %get-tuple-element.405), channel_id=1, source_target_pairs={{0,16},{1,17},{2,18},{3,19},{4,20},{5,21},{6,22},{7,23},{8,24},{9,... | collective-permute-start | bytes 1179656 | tf_op jit(solution)/shard_map/ppermute | solution.py:1005
  256.5 15.8 %collective-permute-start.42 = (bf16[24,2048]{1,0:T(8,128)(2,1)S(1)}, bf16[24,2048]{1,0:T(8,128)(2,1)S(1)}, u32[]{:S(2)}, u32[]{:S(2)}) collective-permute-start(bf16[24,2048]{1,0:T(8,128)(2,1)S(1)} %copy-done.46), channel_id=1, source_target_pairs={{0,4},{1,5},{2,6},{3,7},{4,0},{5,1},{6,2},{7,3},{8,12},{9,13},{10,... | collective-permute-start | bytes 294920 | tf_op jit(solution)/shard_map/ppermute | solution.py:1005
  259.3 28.5 %collective-permute-start.41 = (bf16[24,5632]{1,0:T(8,128)(2,1)S(1)}, bf16[24,5632]{1,0:T(8,128)(2,1)S(1)}, u32[]{:S(2)}, u32[]{:S(2)}) collective-permute-start(bf16[24,5632]{1,0:T(8,128)(2,1)S(1)} %copy-done.45), channel_id=1, source_target_pairs={{0,4},{1,5},{2,6},{3,7},{4,0},{5,1},{6,2},{7,3},{8,12},{9,13},{10,... | collective-permute-start | bytes 811016 | tf_op jit(solution)/shard_map/ppermute | solution.py:1005
  271.2 10.8 %collective-permute-start.35 = (bf16[96,1536]{1,0:T(8,128)(2,1)}, bf16[96,1536]{1,0:T(8,128)(2,1)S(1)}, u32[]{:S(2)}, u32[]{:S(2)}) collective-permute-start(bf16[96,1536]{1,0:T(8,128)(2,1)} %get-tuple-element.413), channel_id=1, source_target_pairs={{0,16},{1,17},{2,18},{3,19},{4,20},{5,21},{6,22},{7,23},{8,9},{9,8... | collective-permute-start | bytes 884744 | tf_op jit(solution)/shard_map/ppermute | solution.py:1005
  (68 other events, 381.0 us)
